TPU v7x, 512 devices: a whole 4x8x8 slice. The times are simulated.
512 devices in a mesh: dp: 16 (over z_lo, x), expert: 32 (over z_hi, y, core).
Axes of the slice: x: 4, y: 8, z: 8 (z_hi: 2, z_lo: 4; z = z_hi * 4 + z_lo), core: 2. Of those that a mesh axis runs over, the one named last changes fastest.
Arguments:
- tokens: bfloat16 [24576, 1280], P(('dp', 'expert')), may hold values from -6 to 6
- cotangent: bfloat16 [24576, 1280], P(('dp', 'expert')), may hold values from -6 to 6
- chosen_rows: int32 [512, 32, 3], P(('dp', 'expert')), may hold values from 0 to 47, as said below
- combine_weights: float32 [512, 32, 3], P(('dp', 'expert')), may hold values from 0.05 to 1
- up_weight: bfloat16 [32, 1280, 3584], P('expert', None, 'dp'), may hold values from -0.15625 to 0.15625
- down_weight: bfloat16 [32, 3584, 1280], P('expert', 'dp'), may hold values from -0.09375 to 0.09375
- first_up: bfloat16 [32, 1280, 3584], P('expert', None, 'dp'), may hold values from -6 to 6
- first_down: bfloat16 [32, 3584, 1280], P('expert', 'dp'), may hold values from -6 to 6
- second_up: bfloat16 [32, 1280, 3584], P('expert', None, 'dp'), may hold values from 0.0099487305 to 1
- second_down: bfloat16 [32, 3584, 1280], P('expert', 'dp'), may hold values from 0.0099487305 to 1
- layer_index: int32 [1], replicated, may hold values from 16 to 31
Outputs:
- combined: bfloat16 [24576, 1280], P(('dp', 'expert'))
- gate_grad: float32 [512, 32, 3], P(('dp', 'expert'))
- step_up: bfloat16 [32, 1280, 3584], P('expert', None, 'dp')
- step_down: bfloat16 [32, 3584, 1280], P('expert', 'dp')
Inputs may be any that keep to these rules, and one draw needn't show every extreme that they name: `chosen_rows`: for each block and each expert the 3 positions are distinct.
All inputs are finite; a program needn't handle non-finite values.
Results may differ from a plain program's by a relative error of at most 0.024.
Values may be sent and summed in bfloat16 or wider, within the bound.
No kernel may reach another device: no remote copies, remote signals or barrier semaphores. Data moves between devices by JAX's collectives and lax.ppermute only.
A program may use at most 64 MiB of HBM per device.

v0:
```python
import jax
import jax.numpy as jnp
from jax import lax
from jax.sharding import PartitionSpec as P

LAYERS = 32
STEP_COUNT = 10


BETA_ONE = 0.9
BETA_TWO = 0.999
EPSILON = 1e-08
DECAY_RATE = 0.9
WEIGHT_DECAY = 0.1


def activation(values):
    return jax.nn.gelu(values, approximate=False)


def adam_step(gradient, first_moment, second_moment, weight, factor):
    running_mean = BETA_ONE * first_moment.astype(jnp.float32) + (1.0 - BETA_ONE) * gradient
    running_square = (
        BETA_TWO * second_moment.astype(jnp.float32) + (1.0 - BETA_TWO) * gradient * gradient
    )
    mean_hat = running_mean / (1.0 - BETA_ONE**STEP_COUNT)
    square_hat = running_square / (1.0 - BETA_TWO**STEP_COUNT)
    update = mean_hat / (jnp.sqrt(square_hat) + EPSILON) + WEIGHT_DECAY * weight.astype(jnp.float32)
    return (factor * update).astype(jnp.bfloat16)


def per_device(
    tokens,
    cotangent,
    chosen_rows,
    combine_weights,
    up_weight,
    down_weight,
    first_up,
    first_down,
    second_up,
    second_down,
    layer_index,
):
    chosen = chosen_rows[0]
    gate_local = combine_weights[0]
    experts, slot_count = chosen.shape
    width = tokens.shape[1]
    token_rows = tokens[chosen]
    back_rows = cotangent[chosen]
    scaled_send = (gate_local[..., None] * back_rows.astype(jnp.float32)).astype(jnp.bfloat16)
    moved_x = lax.all_to_all(token_rows, "expert", split_axis=0, concat_axis=0, tiled=True)
    gathered_x = lax.all_gather(moved_x, "dp", axis=0, tiled=True)
    rows_in = gathered_x.reshape(-1, width)
    up_block = up_weight[0]
    down_block = down_weight[0]
    pre_act = jnp.dot(rows_in, up_block, preferred_element_type=jnp.float32)
    hidden = activation(pre_act).astype(jnp.bfloat16)
    summed = lax.psum_scatter(
        jnp.dot(hidden, down_block, preferred_element_type=jnp.float32).astype(jnp.bfloat16),
        "dp",
        scatter_dimension=0,
        tiled=True,
    )
    expert_rows = summed.reshape(experts, slot_count, width)
    returned = lax.all_to_all(expert_rows, "expert", split_axis=0, concat_axis=0, tiled=True)
    flat_rows = returned.reshape(experts * slot_count, width).astype(jnp.float32)
    flat_pos = chosen.reshape(-1)
    local_ids = jnp.arange(tokens.shape[0], dtype=jnp.int32)
    one_hot = (flat_pos[None, :] == local_ids[:, None]).astype(jnp.float32) * gate_local.reshape(
        -1
    )[None, :]
    combined = jnp.dot(
        one_hot, flat_rows, precision=lax.Precision.HIGHEST, preferred_element_type=jnp.float32
    ).astype(jnp.bfloat16)
    gate_grad = jnp.sum(back_rows.astype(jnp.float32) * returned.astype(jnp.float32), axis=-1)[None]
    moved_g = lax.all_to_all(scaled_send, "expert", split_axis=0, concat_axis=0, tiled=True)
    gathered_g = lax.all_gather(moved_g, "dp", axis=0, tiled=True)
    grads_in = gathered_g.reshape(-1, width)
    back_hidden = lax.dot_general(
        grads_in, down_block, (((1,), (1,)), ((), ())), preferred_element_type=jnp.float32
    )
    _, pull_back = jax.vjp(activation, pre_act)
    back_pre = pull_back(back_hidden)[0].astype(jnp.bfloat16)
    grad_down = lax.dot_general(
        hidden, grads_in, (((0,), (0,)), ((), ())), preferred_element_type=jnp.float32
    )
    grad_up = lax.dot_general(
        rows_in, back_pre, (((0,), (0,)), ((), ())), preferred_element_type=jnp.float32
    )
    exponent = (LAYERS - 1 - layer_index[0]).astype(jnp.float32)
    factor = jnp.power(jnp.float32(DECAY_RATE), exponent)
    step_up = adam_step(grad_up, first_up[0], second_up[0], up_block, factor)[None]
    step_down = adam_step(grad_down, first_down[0], second_down[0], down_block, factor)[None]
    return (combined, gate_grad, step_up, step_down)


def solution(mesh):
    placed = (
        P(("dp", "expert"), None),
        P(("dp", "expert"), None),
        P(("dp", "expert"), None, None),
        P(("dp", "expert"), None, None),
        P("expert", None, "dp"),
        P("expert", "dp", None),
        P("expert", None, "dp"),
        P("expert", "dp", None),
        P("expert", None, "dp"),
        P("expert", "dp", None),
        P(),
    )
    return jax.shard_map(
        per_device,
        mesh=mesh,
        in_specs=placed,
        out_specs=(
            P(("dp", "expert"), None),
            P(("dp", "expert"), None, None),
            P("expert", None, "dp"),
            P("expert", "dp", None),
        ),
        check_vma=False,
    )
```

profile of v0, /device:TPU:42, one launch (start us, length us, event | category | flops | bytes accessed | tf_op | source)
XLA Modules:
  0.0 425.5 jit_solution(6139903270951267457)
XLA Ops:
  7.2 0.0 copy-start
  7.2 0.0 all-gather.3.cloned.1.call-start
  7.2 0.7 compare_select_fusion
  7.9 0.1 copy.27
  8.0 0.1 reshape.74
  8.1 0.0 copy-done
  8.1 0.8 gather_fusion
  8.9 0.1 reshape.73
  9.1 29.7 %all_to_all.15 = bf16[32,3,1280]{2,1,0:T(4,128)(2,1)S(1)} all-to-all(bf16[32,3,1280]{2,1,0:T(4,128)(2,1)S(1)} %reshape.73), channel_id=1, replica_groups=mesh['dp'=16,'expert'=32] {'expert'}, dimensions={0} | all-to-all | bytes 491520 | tf_op jit(solution)/shard_map/all_to_all | solution.py:52
  38.7 0.7 copy.28
  39.5 0.0 all-gather.3.cloned.1.call-update
  39.5 0.0 reduce-scatter.2.cloned.1.call-start
  39.5 88.5 %all-gather.3.cloned.1.call-done = bf16[512,3,1280]{2,0,1:T(8,128)(2,1)} async-done(((bf16[32,3,1280]{2,0,1:T(8,128)(2,1)}), bf16[512,3,1280]{2,0,1:T(8,128)(2,1)}) %all-gather.3.cloned.1.call-update) | async-done | bytes 3932176 | tf_op jit(solution)/shard_map/all_gather | solution.py:53
  128.0 7.8 %copy.29 = bf16[512,3,1280]{2,1,0:T(4,128)(2,1)} copy(bf16[512,3,1280]{2,0,1:T(8,128)(2,1)} %all-gather.3.cloned.1.call-done) | data formatting | bytes 7864320 | tf_op jit(solution)/shard_map/all_gather | solution.py:53
  135.8 0.0 copy-start.7
  135.8 10.5 %reshape.68 = bf16[1536,1280]{1,0:T(8,128)(2,1)} reshape(bf16[512,3,1280]{2,1,0:T(4,128)(2,1)} %copy.29) | data formatting | bytes 7864320 | tf_op jit(solution)/shard_map/reshape | solution.py:54
  146.3 0.0 copy-done.7
  146.3 0.0 copy-start.2
  146.3 7.1 %multiply_convert_fusion = (bf16[1536,224]{0,1:T(8,128)(2,1)S(1)}, f32[1536,224]{0,1:T(8,128)}) fusion(bf16[1536,1280]{1,0:T(8,128)(2,1)} %reshape.68, bf16[1,1280,224]{1,2,0:T(8,128)(2,1)S(1)} %copy-done.7), kind=kOutput, calls=%fused_computation.9 | convolution fusion | flops 903168000 | bytes 6569984 | tf_op jit(solution)/shard_map/dot_general | solution.py:57
  153.4 0.0 copy-done.2
  153.4 3.1 convolution_convert_fusion
  156.5 0.0 copy-start.4
  156.5 0.0 reduce-scatter.2.cloned.1.call-update
  156.5 0.0 copy-start.1
  156.5 90.3 %reduce-scatter.2.cloned.1.call-done = bf16[96,1280]{1,0:T(8,128)(2,1)} async-done(((bf16[1536,1280]{1,0:T(8,128)(2,1)}), bf16[96,1280]{1,0:T(8,128)(2,1)}) %reduce-scatter.2.cloned.1.call-update) | async-done | bytes 245776 | tf_op jit(solution)/shard_map/reduce_scatter | solution.py:59
  246.8 1.8 reshape.69
  248.6 12.0 %all-to-all-start.1 = ((bf16[32,3,1280]{2,1,0:T(4,128)(2,1)}), bf16[32,3,1280]{2,1,0:T(4,128)(2,1)S(1)}, u32[]{:S(2)}, u32[]{:S(2)}) async-start(bf16[32,3,1280]{2,1,0:T(4,128)(2,1)} %reshape.69), calls=%async_computation.2 | async-start | bytes 655360 | tf_op jit(solution)/shard_map/all_to_all | solution.py:66
  260.7 0.0 all-gather.5.cloned.1.call-start
  260.7 0.0 copy-done.4
  260.7 0.1 copy.26
  260.8 0.0 copy-done.1
  260.8 0.8 gather_fusion.1
  261.6 0.2 reshape.90
  261.8 12.9 %all-to-all-done.1 = bf16[32,3,1280]{2,1,0:T(4,128)(2,1)S(1)} async-done(((bf16[32,3,1280]{2,1,0:T(4,128)(2,1)}), bf16[32,3,1280]{2,1,0:T(4,128)(2,1)S(1)}, u32[]{:S(2)}, u32[]{:S(2)}) %all-to-all-start.1) | async-done | bytes 245792 | tf_op jit(solution)/shard_map/all_to_all | solution.py:66
  274.7 0.0 copy-start.3
  274.7 0.4 multiply_convert_fusion.3
  275.1 21.6 %all_to_all.16 = bf16[32,3,1280]{2,1,0:T(4,128)(2,1)S(1)} all-to-all(bf16[32,3,1280]{2,1,0:T(4,128)(2,1)S(1)} %get-tuple-element.16), channel_id=1, replica_groups=mesh['dp'=16,'expert'=32] {'expert'}, dimensions={0} | all-to-all | bytes 491520 | tf_op jit(solution)/shard_map/all_to_all | solution.py:77
  296.7 0.7 copy.32
  297.4 0.0 all-gather.5.cloned.1.call-update
  297.4 0.1 mul.133
  297.6 0.0 copy-done.3
  297.6 0.1 copy.25
  297.7 0.1 eq.15
  298.5 0.6 copy.34
  299.1 0.2 reshape.70
  299.3 0.9 convolution_convert_fusion.1
  300.2 85.5 %all-gather.5.cloned.1.call-done = bf16[512,3,1280]{2,0,1:T(8,128)(2,1)} async-done(((bf16[32,3,1280]{2,0,1:T(8,128)(2,1)}), bf16[512,3,1280]{2,0,1:T(8,128)(2,1)}) %all-gather.5.cloned.1.call-update) | async-done | bytes 3932176 | tf_op jit(solution)/shard_map/all_gather | solution.py:78
  385.7 7.8 %copy.33 = bf16[512,3,1280]{2,1,0:T(4,128)(2,1)} copy(bf16[512,3,1280]{2,0,1:T(8,128)(2,1)} %all-gather.5.cloned.1.call-done) | data formatting | bytes 7864320 | tf_op jit(solution)/shard_map/all_gather | solution.py:78
  393.5 0.0 copy-start.5
  393.5 0.0 copy-start.6
  393.5 10.5 %reshape.71 = bf16[1536,1280]{1,0:T(8,128)(2,1)} reshape(bf16[512,3,1280]{2,1,0:T(4,128)(2,1)} %copy.33) | data formatting | bytes 7864320 | tf_op jit(solution)/shard_map/reshape | solution.py:79
  404.0 0.0 copy-done.5
  404.0 0.0 copy-done.6
  404.0 4.7 %fusion.34 = bf16[1,224,1280]{2,1,0:T(8,128)(2,1)} fusion(bf16[1,224,1280]{2,1,0:T(8,128)(2,1)S(1)} %copy-done.2, bf16[1,224,1280]{2,1,0:T(8,128)(2,1)S(1)} %copy-done.5, bf16[1,224,1280]{2,1,0:T(8,128)(2,1)S(1)} %copy-done.6, f32[]{:T(128)} %bitcast.4, bf16[1536,224]{0,1:T(8,128)(2,1)S(1)} %get-tuple-element.18, bf16[1536,1280]{1,0:T(8,128)(2,1)} %reshape.71), kind=kOutput, calls=%fused_computation.53 | convolution fusion | flops 885964800 | bytes 6914052 | tf_op jit(solution)/shard_map/dot_general | solution.py:85
  408.7 10.3 %fusion.21 = bf16[1,1280,224]{1,2,0:T(8,128)(2,1)} fusion(bf16[1,1280,224]{1,2,0:T(8,128)(2,1)} %param.19, bf16[1536,1280]{1,0:T(8,128)(2,1)} %reshape.68, f32[1536,224]{0,1:T(8,128)} %get-tuple-element.19, bf16[1,1280,224]{1,2,0:T(8,128)(2,1)} %param.17, bf16[1536,1280]{1,0:T(8,128)(2,1)} %reshape.71, bf16[1,224,1280]{2,1,0:T(8,128)(2,1)S(1)} %copy-done.2, ...), kind=kOutput, calls=%fused_computation.42 | convolution fusion | flops 1791541248 | bytes 12107780 | tf_op jit(solution)/shard_map/dot_general | solution.py:88
  (1 shorter events, 0.0 us)
Async XLA Ops:
  7.2 1.0 copy-start
  7.2 120.8 %all-gather.3.cloned.1.call-start = ((), (), s32[]{:S(2)}) async-start(), calls=%async_computation.4 | async-start | bytes 4177920 | tf_op jit(solution)/shard_map/all_gather | solution.py:53
  39.5 207.3 %reduce-scatter.2.cloned.1.call-start = ((), (), s32[]{:S(2)}) async-start(), calls=%async_computation.5 | async-start | bytes 4177920 | tf_op jit(solution)/shard_map/reduce_scatter | solution.py:59
  135.8 10.5 %copy-start.7 = (bf16[1,1280,224]{1,2,0:T(8,128)(2,1)S(1)}, bf16[1,1280,224]{1,2,0:T(8,128)(2,1)}, u32[]{:S(2)}) copy-start(bf16[1,1280,224]{1,2,0:T(8,128)(2,1)} %param.15) | copy-start | bytes 1720324
  146.3 7.1 %copy-start.2 = (bf16[1,224,1280]{2,1,0:T(8,128)(2,1)S(1)}, bf16[1,224,1280]{2,1,0:T(8,128)(2,1)}, u32[]{:S(2)}) copy-start(bf16[1,224,1280]{2,1,0:T(8,128)(2,1)} %param.16) | copy-start | bytes 1720324
  156.5 104.2 %copy-start.4 = (f32[1,32,3]{1,0,2:T(1,128)S(1)}, f32[1,32,3]{1,0,2:T(1,128)}, u32[]{:S(2)}) copy-start(f32[1,32,3]{1,0,2:T(1,128)} %param.14) | copy-start | bytes 1156
  156.5 104.3 %copy-start.1 = (bf16[48,1280]{1,0:T(8,128)(2,1)S(1)}, bf16[48,1280]{1,0:T(8,128)(2,1)}, u32[]{:S(2)}) copy-start(bf16[48,1280]{1,0:T(8,128)(2,1)} %param.12) | copy-start | bytes 368644
  248.6 26.1 %all-to-all-start.1 = ((bf16[32,3,1280]{2,1,0:T(4,128)(2,1)}), bf16[32,3,1280]{2,1,0:T(4,128)(2,1)S(1)}, u32[]{:S(2)}, u32[]{:S(2)}) async-start(bf16[32,3,1280]{2,1,0:T(4,128)(2,1)} %reshape.69), calls=%async_computation.2 | async-start | bytes 655360 | tf_op jit(solution)/shard_map/all_to_all | solution.py:66
  260.7 125.1 %all-gather.5.cloned.1.call-start = ((), (), s32[]{:S(2)}) async-start(), calls=%async_computation.6 | async-start | bytes 4177920 | tf_op jit(solution)/shard_map/all_gather | solution.py:78
  274.7 22.8 %copy-start.3 = (s32[1,32,3]{1,0,2:T(1,128)S(1)}, s32[1,32,3]{1,0,2:T(1,128)}, u32[]{:S(2)}) copy-start(s32[1,32,3]{1,0,2:T(1,128)} %param.13) | copy-start | bytes 1156
  393.5 10.5 %copy-start.5 = (bf16[1,224,1280]{2,1,0:T(8,128)(2,1)S(1)}, bf16[1,224,1280]{2,1,0:T(8,128)(2,1)}, u32[]{:S(2)}) copy-start(bf16[1,224,1280]{2,1,0:T(8,128)(2,1)} %param.20) | copy-start | bytes 1720324
  393.5 10.5 %copy-start.6 = (bf16[1,224,1280]{2,1,0:T(8,128)(2,1)S(1)}, bf16[1,224,1280]{2,1,0:T(8,128)(2,1)}, u32[]{:S(2)}) copy-start(bf16[1,224,1280]{2,1,0:T(8,128)(2,1)} %param.18) | copy-start | bytes 1720324
Sparse Core Ops, SparseCore 0:
  39.6 88.3 all-gather.2
  156.6 90.1 reduce-scatter.1
  297.6 88.1 all-gather.4
where the time goes:
time: 427 us; the launch traced here: 426 us
  waiting for transfers between devices  277 us (65%)
  blocking collectives  51.3 us (12%)
  local copies, waits for them, and re-layouts  43.2 us (10%)
  matrix products  26.1 us (6%)
  between operations  14.5 us (3%)
  starting transfers between devices  12.2 us (3%)
    reduce_scatter x1, waiting for transfers between devices, per_device(): lax.psum_scatter(jnp.dot(hidden, down_block, preferred_element_type=jnp.f...  90.3 us
    all_gather x1, waiting for transfers between devices, per_device(): gathered_x = lax.all_gather(moved_x, 'dp', axis=0, tiled=True)  88.5 us
    all_gather x1, waiting for transfers between devices, per_device(): gathered_g = lax.all_gather(moved_g, 'dp', axis=0, tiled=True)  85.5 us
    all_to_all x1, blocking collectives, per_device(): lax.all_to_all(token_rows, 'expert', split_axis=0, concat_axis=0, tiled=T...  29.7 us
    all_to_all x1, blocking collectives, per_device(): lax.all_to_all(scaled_send, 'expert', split_axis=0, concat_axis=0, tiled=...  21.6 us
    all_to_all x1, waiting for transfers between devices, per_device(): lax.all_to_all(expert_rows, 'expert', split_axis=0, concat_axis=0, tiled=...  12.9 us
    all_to_all x1, starting transfers between devices, per_device(): lax.all_to_all(expert_rows, 'expert', split_axis=0, concat_axis=0, tiled=...  12 us
    reshape x1, local copies, waits for them, and re-layouts, per_device(): grads_in = gathered_g.reshape(-1, width)  10.5 us
  transfers between devices with their start and end apart: 4, of which 4 were waited for; matrix products, arithmetic and copies ran while one was open for 1% of the time, Pallas kernels for 0%

commit v1 on v0

v1 whole, which is shorter than its diff:
```python
import jax
import jax.numpy as jnp
from jax import lax
from jax.sharding import PartitionSpec as P

LAYERS = 32
STEP_COUNT = 10

BETA_ONE = 0.9
BETA_TWO = 0.999
EPSILON = 1e-08
DECAY_RATE = 0.9
WEIGHT_DECAY = 0.1

LINE = 4
RING = 4


def activation(values):
    return jax.nn.gelu(values, approximate=False)


def adam_step(gradient, first_moment, second_moment, weight, factor):
    running_mean = BETA_ONE * first_moment.astype(jnp.float32) + (1.0 - BETA_ONE) * gradient
    running_square = (
        BETA_TWO * second_moment.astype(jnp.float32) + (1.0 - BETA_TWO) * gradient * gradient
    )
    mean_hat = running_mean / (1.0 - BETA_ONE**STEP_COUNT)
    square_hat = running_square / (1.0 - BETA_TWO**STEP_COUNT)
    update = mean_hat / (jnp.sqrt(square_hat) + EPSILON) + WEIGHT_DECAY * weight.astype(jnp.float32)
    return (factor * update).astype(jnp.bfloat16)


def shift(values, along_z, along_x):
    pairs = []
    for z in range(LINE):
        for x in range(RING):
            target = (z + along_z) % LINE * RING + (x + along_x) % RING
            pairs.append((z * RING + x, target))
    return lax.ppermute(values, "dp", pairs)


def exchange(rows):
    return lax.all_to_all(rows, "expert", split_axis=0, concat_axis=0, tiled=True)


def contract(left, right, dims):
    return lax.dot_general(left, right, (dims, ((), ())), preferred_element_type=jnp.float32)


def per_device(
    tokens,
    cotangent,
    chosen_rows,
    combine_weights,
    up_weight,
    down_weight,
    first_up,
    first_down,
    second_up,
    second_down,
    layer_index,
):
    chosen = chosen_rows[0]
    gate_local = combine_weights[0]
    experts, picks = chosen.shape
    width = tokens.shape[1]
    slots = experts * picks
    up_own = up_weight[0].T
    down_own = down_weight[0]
    group = down_own.shape[0]

    own = jnp.concatenate([up_own, down_own])
    left = shift(own, 0, 1)
    right = shift(own, 0, -1)
    up_far = shift(left[:group], 0, 1)
    down_far = shift(right[group:], 0, -1)
    up_all = jnp.concatenate([up_own, left[:group], right[:group], up_far])
    down_all = jnp.concatenate([down_own, left[group:], right[group:], down_far])

    token_rows = tokens[chosen]
    back_rows = cotangent[chosen]
    scaled = (gate_local[..., None] * back_rows.astype(jnp.float32)).astype(jnp.bfloat16)
    rows_own = exchange(token_rows).reshape(slots, width)
    rows_in = jnp.concatenate([rows_own] + [shift(rows_own, -k, 0) for k in range(1, LINE)])
    rows_own, scaled = lax.optimization_barrier((rows_own, scaled))
    grads_own = exchange(scaled).reshape(slots, width)
    rows_in, grads_own = lax.optimization_barrier((rows_in, grads_own))
    grads_in = jnp.concatenate([grads_own] + [shift(grads_own, -k, 0) for k in range(1, LINE)])

    pre_act = contract(rows_in, up_all, ((1,), (1,)))
    hidden = activation(pre_act).astype(jnp.bfloat16)
    partial = contract(hidden, down_all, ((1,), (0,))).astype(jnp.bfloat16)
    parts = partial.reshape(LINE, slots, width)
    total = parts[0].astype(jnp.float32)
    for k in range(1, LINE):
        total = total + shift(parts[k], k, 0).astype(jnp.float32)
    expert_rows = total.astype(jnp.bfloat16).reshape(experts, picks, width)

    back_hidden = contract(grads_in, down_all, ((1,), (1,)))
    _, pull_back = jax.vjp(activation, pre_act)
    back_pre = pull_back(back_hidden)[0].astype(jnp.bfloat16)
    grad_down = contract(hidden, grads_in, ((0,), (0,)))
    grad_up = contract(back_pre, rows_in, ((0,), (0,)))

    def pieces(gradient):
        return [gradient[i * group : (i + 1) * group] for i in range(RING)]

    up_parts, down_parts = pieces(grad_up), pieces(grad_down)
    up_two = shift(up_parts[3].astype(jnp.bfloat16), 0, 1).astype(jnp.float32)
    down_two = shift(down_parts[3].astype(jnp.bfloat16), 0, -1).astype(jnp.float32)
    to_right = jnp.concatenate([up_parts[2] + up_two, down_parts[2]]).astype(jnp.bfloat16)
    to_left = jnp.concatenate([up_parts[1], down_parts[1] + down_two]).astype(jnp.bfloat16)
    expert_rows, to_right, to_left = lax.optimization_barrier((expert_rows, to_right, to_left))
    from_left = shift(to_right, 0, 1).astype(jnp.float32)
    from_right = shift(to_left, 0, -1).astype(jnp.float32)
    total_up = up_parts[0] + from_left[:group] + from_right[:group]
    total_down = down_parts[0] + from_left[group:] + from_right[group:]

    exponent = (LAYERS - 1 - layer_index[0]).astype(jnp.float32)
    factor = jnp.power(jnp.float32(DECAY_RATE), exponent)
    step_up = adam_step(total_up, first_up[0].T, second_up[0].T, up_own, factor).T[None]
    step_down = adam_step(total_down, first_down[0], second_down[0], down_own, factor)[None]

    returned = exchange(expert_rows)
    flat_rows = returned.reshape(slots, width).astype(jnp.float32)
    local_ids = jnp.arange(tokens.shape[0], dtype=jnp.int32)
    one_hot = (chosen.reshape(-1)[None, :] == local_ids[:, None]).astype(jnp.float32)
    combined = jnp.dot(
        one_hot * gate_local.reshape(-1)[None, :],
        flat_rows,
        precision=lax.Precision.HIGHEST,
        preferred_element_type=jnp.float32,
    ).astype(jnp.bfloat16)
    gate_grad = jnp.sum(back_rows.astype(jnp.float32) * returned.astype(jnp.float32), axis=-1)[None]
    return (combined, gate_grad, step_up, step_down)


def solution(mesh):
    placed = (
        P(("dp", "expert"), None),
        P(("dp", "expert"), None),
        P(("dp", "expert"), None, None),
        P(("dp", "expert"), None, None),
        P("expert", None, "dp"),
        P("expert", "dp", None),
        P("expert", None, "dp"),
        P("expert", "dp", None),
        P("expert", None, "dp"),
        P("expert", "dp", None),
        P(),
    )
    return jax.shard_map(
        per_device,
        mesh=mesh,
        in_specs=placed,
        out_specs=(
            P(("dp", "expert"), None),
            P(("dp", "expert"), None, None),
            P("expert", None, "dp"),
            P("expert", "dp", None),
        ),
        check_vma=False,
    )
```

time: 427 us -> 206 us (0.48)
  the two profiles are of different devices: /device:TPU:42 before, /device:TPU:1 now
where the time goes in v1:
time: 206 us; the launch traced here: 205 us
  starting transfers between devices  91.8 us (45%)
  waiting for transfers between devices  57.5 us (28%)
  matrix products  21.1 us (10%)
  other arithmetic  18.4 us (9%)
  local copies, waits for them, and re-layouts  14.3 us (7%)
    ppermute x17, starting transfers between devices, shift(): return lax.ppermute(values, 'dp', pairs)  58.8 us
    all_to_all x3, starting transfers between devices, exchange(): lax.all_to_all(rows, 'expert', split_axis=0, concat_axis=0, tiled=True)  33 us
    all_to_all x3, waiting for transfers between devices, exchange(): lax.all_to_all(rows, 'expert', split_axis=0, concat_axis=0, tiled=True)  29.9 us
    ppermute x17, waiting for transfers between devices, shift(): return lax.ppermute(values, 'dp', pairs)  27.6 us
    dot_general x4, matrix products, contract(): lax.dot_general(left, right, (dims, ((), ())), preferred_element_type=jnp...  20.2 us
    broadcast_in_dim x1, other arithmetic, per_device(): adam_step(total_down, first_down[0], second_down[0], down_own, factor)[None]  4.73 us
  transfers between devices with their start and end apart: 20, of which 9 were waited for; matrix products, arithmetic and copies ran while one was open for 19% of the time, Pallas kernels for 0%

profile of v1, /device:TPU:1, one launch (start us, length us, event | category | flops | bytes accessed | tf_op | source)
XLA Modules:
  0.0 204.9 jit_solution(2640126336215039948)
XLA Ops:
  0.6 0.7 compare_select_fusion
  1.5 0.1 reshape.83
  1.6 0.8 gather_fusion
  2.4 0.8 reshape.82
  3.3 17.3 %all-to-all-start = ((bf16[32,3,1280]{2,1,0:T(4,128)(2,1)}), bf16[32,3,1280]{2,1,0:T(4,128)(2,1)S(1)}, u32[]{:S(2)}, u32[]{:S(2)}) async-start(bf16[32,3,1280]{2,1,0:T(4,128)(2,1)} %reshape.82), calls=%async_computation | async-start | bytes 655360 | tf_op jit(solution)/shard_map/all_to_all | solution.py:44
  20.6 1.1 pad_maximum_fusion.1
  21.7 4.4 %collective-permute-start.4 = (bf16[448,1280]{1,0:T(8,128)(2,1)}, bf16[448,1280]{1,0:T(8,128)(2,1)}, u32[]{:S(2)}, u32[]{:S(2)}) collective-permute-start(bf16[448,1280]{1,0:T(8,128)(2,1)} %pad_maximum_fusion.1), channel_id=1, source_target_pairs={{0,96},{32,0},{64,32},{96,64},{128,224},{160,128},{192,160},{224,1... | collective-permute-start | bytes 3440648 | tf_op jit(solution)/shard_map/ppermute | solution.py:40
  26.2 0.8 gather_fusion.1
  27.0 0.2 reshape.99
  27.3 10.2 %all-to-all-done = bf16[32,3,1280]{2,1,0:T(4,128)(2,1)S(1)} async-done(((bf16[32,3,1280]{2,1,0:T(4,128)(2,1)}), bf16[32,3,1280]{2,1,0:T(4,128)(2,1)S(1)}, u32[]{:S(2)}, u32[]{:S(2)}) %all-to-all-start) | async-done | bytes 245792 | tf_op jit(solution)/shard_map/all_to_all | solution.py:44
  37.5 0.9 reshape.77
  38.4 3.1 %collective-permute-start.2 = (bf16[96,1280]{1,0:T(8,128)(2,1)}, bf16[96,1280]{1,0:T(8,128)(2,1)}, u32[]{:S(2)}, u32[]{:S(2)}) collective-permute-start(bf16[96,1280]{1,0:T(8,128)(2,1)} %reshape.77), channel_id=1, source_target_pairs={{0,128},{32,160},{64,192},{96,224},{128,256},{160,288},{192,320},{... | collective-permute-start | bytes 737288 | tf_op jit(solution)/shard_map/ppermute | solution.py:40
  41.5 4.0 %collective-permute-start.1 = (bf16[96,1280]{1,0:T(8,128)(2,1)}, bf16[96,1280]{1,0:T(8,128)(2,1)}, u32[]{:S(2)}, u32[]{:S(2)}) collective-permute-start(bf16[96,1280]{1,0:T(8,128)(2,1)} %reshape.77), channel_id=1, source_target_pairs={{0,256},{32,288},{64,320},{96,352},{128,384},{160,416},{192,448},{... | collective-permute-start | bytes 737288 | tf_op jit(solution)/shard_map/ppermute | solution.py:40
  45.5 3.1 %collective-permute-start = (bf16[96,1280]{1,0:T(8,128)(2,1)}, bf16[96,1280]{1,0:T(8,128)(2,1)}, u32[]{:S(2)}, u32[]{:S(2)}) collective-permute-start(bf16[96,1280]{1,0:T(8,128)(2,1)} %reshape.77), channel_id=1, source_target_pairs={{0,384},{32,416},{64,448},{96,480},{128,0},{160,32},{192,64},{224,... | collective-permute-start | bytes 737288 | tf_op jit(solution)/shard_map/ppermute | solution.py:40
  48.6 0.9 multiply_convert_fusion.3
  49.5 6.2 %all-to-all-start.1 = ((bf16[32,3,1280]{2,1,0:T(4,128)(2,1)}), bf16[32,3,1280]{2,1,0:T(4,128)(2,1)S(1)}, u32[]{:S(2)}, u32[]{:S(2)}) async-start(bf16[32,3,1280]{2,1,0:T(4,128)(2,1)} %multiply_convert_fusion.3), calls=%async_computation.1 | async-start | bytes 655360 | tf_op jit(solution)/shard_map/all_to_all | solution.py:44
  55.7 3.1 %collective-permute-start.3 = (bf16[448,1280]{1,0:T(8,128)(2,1)}, bf16[448,1280]{1,0:T(8,128)(2,1)S(1)}, u32[]{:S(2)}, u32[]{:S(2)}) collective-permute-start(bf16[448,1280]{1,0:T(8,128)(2,1)} %pad_maximum_fusion.1), channel_id=1, source_target_pairs={{0,32},{32,64},{64,96},{96,0},{128,160},{160,192},{192,224},{224,1... | collective-permute-start | bytes 3440648 | tf_op jit(solution)/shard_map/ppermute | solution.py:40
  58.8 7.8 %collective-permute-done.1 = bf16[96,1280]{1,0:T(8,128)(2,1)} collective-permute-done((bf16[96,1280]{1,0:T(8,128)(2,1)}, bf16[96,1280]{1,0:T(8,128)(2,1)}, u32[]{:S(2)}, u32[]{:S(2)}) %collective-permute-start.1) | collective-permute-done | bytes 245792 | tf_op jit(solution)/shard_map/ppermute | solution.py:40
  66.6 2.3 %pad_maximum_fusion.4 = bf16[384,1280]{1,0:T(8,128)(2,1)} fusion(bf16[96,1280]{1,0:T(8,128)(2,1)} %collective-permute-done.2, bf16[96,1280]{1,0:T(8,128)(2,1)} %collective-permute-done.1, bf16[96,1280]{1,0:T(8,128)(2,1)} %collective-permute-done, bf16[96,1280]{1,0:T(8,128)(2,1)} %reshape.77), kind=kLoop, calls=%fused_computation.61 | loop fusion | flops 3932160 | bytes 1966080 | tf_op jit(solution)/shard_map/concatenate | solution.py:85
  68.9 3.8 %all-to-all-done.1 = bf16[32,3,1280]{2,1,0:T(4,128)(2,1)S(1)} async-done(((bf16[32,3,1280]{2,1,0:T(4,128)(2,1)}), bf16[32,3,1280]{2,1,0:T(4,128)(2,1)S(1)}, u32[]{:S(2)}, u32[]{:S(2)}) %all-to-all-start.1) | async-done | bytes 245792 | tf_op jit(solution)/shard_map/all_to_all | solution.py:44
  72.7 0.9 reshape.78
  73.6 6.0 %collective-permute-start.12 = (bf16[96,1280]{1,0:T(8,128)(2,1)}, bf16[96,1280]{1,0:T(8,128)(2,1)S(1)}, u32[]{:S(2)}, u32[]{:S(2)}) collective-permute-start(bf16[96,1280]{1,0:T(8,128)(2,1)} %reshape.78), channel_id=1, source_target_pairs={{0,128},{32,160},{64,192},{96,224},{128,256},{160,288},{192,320},{... | collective-permute-start | bytes 737288 | tf_op jit(solution)/shard_map/ppermute | solution.py:40
  79.6 1.9 collective-permute-start.11
  81.5 4.0 %collective-permute-start.10 = (bf16[96,1280]{1,0:T(8,128)(2,1)}, bf16[96,1280]{1,0:T(8,128)(2,1)S(1)}, u32[]{:S(2)}, u32[]{:S(2)}) collective-permute-start(bf16[96,1280]{1,0:T(8,128)(2,1)} %reshape.78), channel_id=1, source_target_pairs={{0,384},{32,416},{64,448},{96,480},{128,0},{160,32},{192,64},{224,... | collective-permute-start | bytes 737288 | tf_op jit(solution)/shard_map/ppermute | solution.py:40
  85.5 1.0 constant_dynamic-update-slice_fusion.3
  86.5 1.3 fusion.53
  87.8 4.5 %collective-permute-start.6 = (bf16[224,1280]{1,0:T(8,128)(2,1)S(1)}, bf16[224,1280]{1,0:T(8,128)(2,1)S(1)}, u32[]{:S(2)}, u32[]{:S(2)}) collective-permute-start(bf16[224,1280]{1,0:T(8,128)(2,1)S(1)} %get-tuple-element.36), channel_id=1, source_target_pairs={{0,96},{32,0},{64,32},{96,64},{128,224},{160,128},{192,160},{224,1... | collective-permute-start | bytes 1720328 | tf_op jit(solution)/shard_map/ppermute | solution.py:40
  92.5 1.9 collective-permute-start.5
  94.4 0.9 collective-permute-done.10
  95.3 0.6 collective-permute-done.11
  96.0 12.7 %collective-permute-done.5 = bf16[224,1280]{1,0:T(8,128)(2,1)S(1)} collective-permute-done((bf16[224,1280]{1,0:T(8,128)(2,1)S(1)}, bf16[224,1280]{1,0:T(8,128)(2,1)S(1)}, u32[]{:S(2)}, u32[]{:S(2)}) %collective-permute-start.5) | collective-permute-done | bytes 573472 | tf_op jit(solution)/shard_map/ppermute | solution.py:40
  108.7 4.9 %multiply_convert_fusion = (bf16[384,896]{1,0:T(8,128)(2,1)S(1)}, f32[384,896]{1,0:T(8,128)}) fusion(bf16[384,1280]{1,0:T(8,128)(2,1)S(1)} %copy-done.10, bf16[224,1280]{1,0:T(8,128)(2,1)S(1)} %collective-permute-done.5, bf16[224,1280]{1,0:T(8,128)(2,1)S(1)} %get-tuple-element.37, bf16[224,1280]{1,0:T(8,128)(2,1)S(1)} %get-tuple-element.35, ...), kind=kOutput, calls=%fused_computation.18 | convolution fusion | flops 912343040 | bytes 5341184 | tf_op jit(solution)/shard_map/dot_general | solution.py:48
  113.6 1.2 convolution_convert_fusion
  114.8 0.9 fusion.54
  115.7 1.9 collective-permute-start.7
  117.7 5.2 %collective-permute-start.9 = (bf16[96,1280]{1,0:T(8,128)(2,1)}, bf16[96,1280]{1,0:T(8,128)(2,1)}, u32[]{:S(2)}, u32[]{:S(2)}) collective-permute-start(bf16[96,1280]{1,0:T(8,128)(2,1)} %get-tuple-element.39), channel_id=1, source_target_pairs={{0,384},{32,416},{64,448},{96,480},{128,0},{160,32},{192,64},{224,... | collective-permute-start | bytes 737288 | tf_op jit(solution)/shard_map/ppermute | solution.py:40
  122.8 2.1 %collective-permute-start.8 = (bf16[96,1280]{1,0:T(8,128)(2,1)}, bf16[96,1280]{1,0:T(8,128)(2,1)}, u32[]{:S(2)}, u32[]{:S(2)}) collective-permute-start(bf16[96,1280]{1,0:T(8,128)(2,1)} %get-tuple-element.40), channel_id=1, source_target_pairs={{0,256},{32,288},{64,320},{96,352},{128,384},{160,416},{192,448},{... | collective-permute-start | bytes 737288 | tf_op jit(solution)/shard_map/ppermute | solution.py:40
  124.9 3.5 %fusion.55 = (bf16[896,1280]{1,0:T(8,128)(2,1)S(1)}, f32[896,1280]{1,0:T(8,128)}) fusion(bf16[384,896]{1,0:T(8,128)(2,1)S(1)} %get-tuple-element.41, bf16[384,1280]{1,0:T(8,128)(2,1)S(1)} %constant_dynamic-update-slice_fusion), kind=kOutput, calls=%fused_computation.95 | convolution fusion | flops 881950720 | bytes 8552448 | tf_op jit(solution)/shard_map/dot_general | solution.py:48
  128.4 10.6 %fusion.56 = (bf16[896,1280]{1,0:T(8,128)(2,1)}, f32[896,1280]{1,0:T(8,128)}) fusion(bf16[384,1280]{1,0:T(8,128)(2,1)} %pad_maximum_fusion.4, f32[384,896]{1,0:T(8,128)} %get-tuple-element.42, bf16[384,1280]{1,0:T(8,128)(2,1)} %copy-done.8, bf16[224,1280]{1,0:T(8,128)(2,1)} %copy-done.19, bf16[224,1280]{1,0:T(8,128)(2,1)} %copy-done.15, ...), kind=kOutput, calls=%fused_computation.96 | convolution fusion | flops 1796702208 | bytes 12517376 | tf_op jit(solution)/shard_map/dot_general | solution.py:48
  139.1 2.4 %fusion.50 = (bf16[224,1280]{1,0:T(8,128)(2,1)}, bf16[224,1280]{1,0:T(8,128)(2,1)}) fusion(bf16[896,1280]{1,0:T(8,128)(2,1)} %get-tuple-element.45), kind=kLoop, calls=%fused_computation.90 | loop fusion | bytes 2293760 | tf_op jit(solution)/shard_map/slice | solution.py:107
  141.4 1.9 collective-permute-start.13
  143.4 1.1 fusion.51
  144.4 4.6 %collective-permute-start.14 = (bf16[224,1280]{1,0:T(8,128)(2,1)}, bf16[224,1280]{1,0:T(8,128)(2,1)S(1)}, u32[]{:S(2)}, u32[]{:S(2)}) collective-permute-start(bf16[224,1280]{1,0:T(8,128)(2,1)} %get-tuple-element.32), channel_id=1, source_target_pairs={{0,96},{32,0},{64,32},{96,64},{128,224},{160,128},{192,160},{224,1... | collective-permute-start | bytes 1720328 | tf_op jit(solution)/shard_map/ppermute | solution.py:40
  149.0 1.3 add_convert_fusion.2
  150.4 0.9 reshape.79
  151.2 5.3 %collective-permute-done.13 = bf16[224,1280]{1,0:T(8,128)(2,1)} collective-permute-done((bf16[224,1280]{1,0:T(8,128)(2,1)}, bf16[224,1280]{1,0:T(8,128)(2,1)}, u32[]{:S(2)}, u32[]{:S(2)}) %collective-permute-start.13) | collective-permute-done | bytes 573472 | tf_op jit(solution)/shard_map/ppermute | solution.py:40
  156.5 1.5 fusion.27
  158.1 0.4 collective-permute-done.14
  158.5 1.4 fusion.26
  159.9 1.1 pad_maximum_fusion.3
  161.0 1.9 collective-permute-start.15
  162.9 5.2 %collective-permute-start.16 = (bf16[448,1280]{1,0:T(8,128)(2,1)}, bf16[448,1280]{1,0:T(8,128)(2,1)}, u32[]{:S(2)}, u32[]{:S(2)}) collective-permute-start(bf16[448,1280]{1,0:T(8,128)(2,1)} %pad_maximum_fusion.3), channel_id=1, source_target_pairs={{0,96},{32,0},{64,32},{96,64},{128,224},{160,128},{192,160},{224,1... | collective-permute-start | bytes 3440648 | tf_op jit(solution)/shard_map/ppermute | solution.py:40
  168.1 9.5 %all-to-all-start.2 = ((bf16[32,3,1280]{2,1,0:T(4,128)(2,1)}), bf16[32,3,1280]{2,1,0:T(4,128)(2,1)S(1)}, u32[]{:S(2)}, u32[]{:S(2)}) async-start(bf16[32,3,1280]{2,1,0:T(4,128)(2,1)} %reshape.79), calls=%async_computation.2 | async-start | bytes 655360 | tf_op jit(solution)/shard_map/all_to_all | solution.py:44
  178.6 15.9 %all-to-all-done.2 = bf16[32,3,1280]{2,1,0:T(4,128)(2,1)S(1)} async-done(((bf16[32,3,1280]{2,1,0:T(4,128)(2,1)}), bf16[32,3,1280]{2,1,0:T(4,128)(2,1)S(1)}, u32[]{:S(2)}, u32[]{:S(2)}) %all-to-all-start.2) | async-done | bytes 245792 | tf_op jit(solution)/shard_map/all_to_all | solution.py:44
  194.5 0.2 multiply_reduce_fusion
  194.8 0.6 copy.30
  195.4 0.2 reshape.80
  195.6 0.9 convolution_convert_fusion.1
  196.5 1.4 convert_element_type.105
  198.0 1.6 convert_element_type.106
  199.7 0.2 copy-done.12
  199.9 0.2 copy-done.13
  200.0 0.2 copy-done.14
  200.2 4.7 %fusion.35 = (bf16[1,224,1280]{2,1,0:T(8,128)(2,1)}, bf16[1,1280,224]{1,2,0:T(8,128)(2,1)}) fusion(bf16[1,224,1280]{2,1,0:T(8,128)(2,1)S(1)} %copy-done.11, f32[448,1280]{1,0:T(8,128)S(1)} %convert_element_type.106, f32[448,1280]{1,0:T(8,128)S(1)} %convert_element_type.105, f32[896,1280]{1,0:T(8,128)} %get-tuple-element.44, ...), kind=kLoop, calls=%fused_computation.69 | loop fusion | flops 11468800 | bytes 11468804 | tf_op jit(solution)/shard_map/broadcast_in_dim | solution.py:123
  (59 shorter events, 0.9 us)
Async XLA Ops:
  0.6 0.9 copy-start
  1.6 19.0 %copy-start.2 = (bf16[1,224,1280]{2,1,0:T(8,128)(2,1)S(1)}, bf16[1,224,1280]{2,1,0:T(8,128)(2,1)}, u32[]{:S(2)}) copy-start(bf16[1,224,1280]{2,1,0:T(8,128)(2,1)} %param.16) | copy-start | bytes 1720324
  1.6 19.0 %copy-start.4 = (bf16[1,1280,224]{1,2,0:T(8,128)(2,1)S(1)}, bf16[1,1280,224]{1,2,0:T(8,128)(2,1)}, u32[]{:S(2)}) copy-start(bf16[1,1280,224]{1,2,0:T(8,128)(2,1)} %param.15) | copy-start | bytes 1720324
  3.3 22.9 %copy-start.18 = (f32[1,32,3]{1,0,2:T(1,128)S(1)}, f32[1,32,3]{1,0,2:T(1,128)}, u32[]{:S(2)}) copy-start(f32[1,32,3]{1,0,2:T(1,128)} %param.14) | copy-start | bytes 1156
  3.3 23.0 %copy-start.1 = (bf16[48,1280]{1,0:T(8,128)(2,1)S(1)}, bf16[48,1280]{1,0:T(8,128)(2,1)}, u32[]{:S(2)}) copy-start(bf16[48,1280]{1,0:T(8,128)(2,1)} %param.12) | copy-start | bytes 368644
  3.3 34.2 %all-to-all-start = ((bf16[32,3,1280]{2,1,0:T(4,128)(2,1)}), bf16[32,3,1280]{2,1,0:T(4,128)(2,1)S(1)}, u32[]{:S(2)}, u32[]{:S(2)}) async-start(bf16[32,3,1280]{2,1,0:T(4,128)(2,1)} %reshape.82), calls=%async_computation | async-start | bytes 655360 | tf_op jit(solution)/shard_map/all_to_all | solution.py:44
  21.7 64.8 %collective-permute-start.4 = (bf16[448,1280]{1,0:T(8,128)(2,1)}, bf16[448,1280]{1,0:T(8,128)(2,1)}, u32[]{:S(2)}, u32[]{:S(2)}) collective-permute-start(bf16[448,1280]{1,0:T(8,128)(2,1)} %pad_maximum_fusion.1), channel_id=1, source_target_pairs={{0,96},{32,0},{64,32},{96,64},{128,224},{160,128},{192,160},{224,1... | collective-permute-start | bytes 3440648 | tf_op jit(solution)/shard_map/ppermute | solution.py:40
  38.4 20.4 %collective-permute-start.2 = (bf16[96,1280]{1,0:T(8,128)(2,1)}, bf16[96,1280]{1,0:T(8,128)(2,1)}, u32[]{:S(2)}, u32[]{:S(2)}) collective-permute-start(bf16[96,1280]{1,0:T(8,128)(2,1)} %reshape.77), channel_id=1, source_target_pairs={{0,128},{32,160},{64,192},{96,224},{128,256},{160,288},{192,320},{... | collective-permute-start | bytes 737288 | tf_op jit(solution)/shard_map/ppermute | solution.py:40
  41.5 25.1 %collective-permute-start.1 = (bf16[96,1280]{1,0:T(8,128)(2,1)}, bf16[96,1280]{1,0:T(8,128)(2,1)}, u32[]{:S(2)}, u32[]{:S(2)}) collective-permute-start(bf16[96,1280]{1,0:T(8,128)(2,1)} %reshape.77), channel_id=1, source_target_pairs={{0,256},{32,288},{64,320},{96,352},{128,384},{160,416},{192,448},{... | collective-permute-start | bytes 737288 | tf_op jit(solution)/shard_map/ppermute | solution.py:40
  45.5 21.1 %collective-permute-start = (bf16[96,1280]{1,0:T(8,128)(2,1)}, bf16[96,1280]{1,0:T(8,128)(2,1)}, u32[]{:S(2)}, u32[]{:S(2)}) collective-permute-start(bf16[96,1280]{1,0:T(8,128)(2,1)} %reshape.77), channel_id=1, source_target_pairs={{0,384},{32,416},{64,448},{96,480},{128,0},{160,32},{192,64},{224,... | collective-permute-start | bytes 737288 | tf_op jit(solution)/shard_map/ppermute | solution.py:40
  49.5 23.2 %all-to-all-start.1 = ((bf16[32,3,1280]{2,1,0:T(4,128)(2,1)}), bf16[32,3,1280]{2,1,0:T(4,128)(2,1)S(1)}, u32[]{:S(2)}, u32[]{:S(2)}) async-start(bf16[32,3,1280]{2,1,0:T(4,128)(2,1)} %multiply_convert_fusion.3), calls=%async_computation.1 | async-start | bytes 655360 | tf_op jit(solution)/shard_map/all_to_all | solution.py:44
  55.7 36.7 %collective-permute-start.3 = (bf16[448,1280]{1,0:T(8,128)(2,1)}, bf16[448,1280]{1,0:T(8,128)(2,1)S(1)}, u32[]{:S(2)}, u32[]{:S(2)}) collective-permute-start(bf16[448,1280]{1,0:T(8,128)(2,1)} %pad_maximum_fusion.1), channel_id=1, source_target_pairs={{0,32},{32,64},{64,96},{96,0},{128,160},{160,192},{192,224},{224,1... | collective-permute-start | bytes 3440648 | tf_op jit(solution)/shard_map/ppermute | solution.py:40
  73.6 22.4 %collective-permute-start.12 = (bf16[96,1280]{1,0:T(8,128)(2,1)}, bf16[96,1280]{1,0:T(8,128)(2,1)S(1)}, u32[]{:S(2)}, u32[]{:S(2)}) collective-permute-start(bf16[96,1280]{1,0:T(8,128)(2,1)} %reshape.78), channel_id=1, source_target_pairs={{0,128},{32,160},{64,192},{96,224},{128,256},{160,288},{192,320},{... | collective-permute-start | bytes 737288 | tf_op jit(solution)/shard_map/ppermute | solution.py:40
  79.6 16.4 %collective-permute-start.11 = (bf16[96,1280]{1,0:T(8,128)(2,1)}, bf16[96,1280]{1,0:T(8,128)(2,1)S(1)}, u32[]{:S(2)}, u32[]{:S(2)}) collective-permute-start(bf16[96,1280]{1,0:T(8,128)(2,1)} %reshape.78), channel_id=1, source_target_pairs={{0,256},{32,288},{64,320},{96,352},{128,384},{160,416},{192,448},{... | collective-permute-start | bytes 737288 | tf_op jit(solution)/shard_map/ppermute | solution.py:40
  81.5 13.8 %collective-permute-start.10 = (bf16[96,1280]{1,0:T(8,128)(2,1)}, bf16[96,1280]{1,0:T(8,128)(2,1)S(1)}, u32[]{:S(2)}, u32[]{:S(2)}) collective-permute-start(bf16[96,1280]{1,0:T(8,128)(2,1)} %reshape.78), channel_id=1, source_target_pairs={{0,384},{32,416},{64,448},{96,480},{128,0},{160,32},{192,64},{224,... | collective-permute-start | bytes 737288 | tf_op jit(solution)/shard_map/ppermute | solution.py:40
  87.8 25.8 %copy-start.15 = (bf16[224,1280]{1,0:T(8,128)(2,1)}, bf16[224,1280]{1,0:T(8,128)(2,1)S(1)}, u32[]{:S(2)}) copy-start(bf16[224,1280]{1,0:T(8,128)(2,1)S(1)} %get-tuple-element.36) | copy-start | bytes 1720324
  87.8 20.9 %copy-start.10 = (bf16[384,1280]{1,0:T(8,128)(2,1)S(1)}, bf16[384,1280]{1,0:T(8,128)(2,1)}, u32[]{:S(2)}) copy-start(bf16[384,1280]{1,0:T(8,128)(2,1)} %pad_maximum_fusion.4) | copy-start | bytes 2949124
  87.8 25.7 %collective-permute-start.6 = (bf16[224,1280]{1,0:T(8,128)(2,1)S(1)}, bf16[224,1280]{1,0:T(8,128)(2,1)S(1)}, u32[]{:S(2)}, u32[]{:S(2)}) collective-permute-start(bf16[224,1280]{1,0:T(8,128)(2,1)S(1)} %get-tuple-element.36), channel_id=1, source_target_pairs={{0,96},{32,0},{64,32},{96,64},{128,224},{160,128},{192,160},{224,1... | collective-permute-start | bytes 1720328 | tf_op jit(solution)/shard_map/ppermute | solution.py:40
  92.5 21.1 %copy-start.16 = (bf16[224,1280]{1,0:T(8,128)(2,1)}, bf16[224,1280]{1,0:T(8,128)(2,1)S(1)}, u32[]{:S(2)}) copy-start(bf16[224,1280]{1,0:T(8,128)(2,1)S(1)} %get-tuple-element.34) | copy-start | bytes 1720324
  92.5 16.2 %collective-permute-start.5 = (bf16[224,1280]{1,0:T(8,128)(2,1)S(1)}, bf16[224,1280]{1,0:T(8,128)(2,1)S(1)}, u32[]{:S(2)}, u32[]{:S(2)}) collective-permute-start(bf16[224,1280]{1,0:T(8,128)(2,1)S(1)} %get-tuple-element.35), channel_id=1, source_target_pairs={{0,32},{32,64},{64,96},{96,0},{128,160},{160,192},{192,224},{224,1... | collective-permute-start | bytes 1720328 | tf_op jit(solution)/shard_map/ppermute | solution.py:40
  96.0 28.9 %copy-start.8 = (bf16[384,1280]{1,0:T(8,128)(2,1)}, bf16[384,1280]{1,0:T(8,128)(2,1)S(1)}, u32[]{:S(2)}) copy-start(bf16[384,1280]{1,0:T(8,128)(2,1)S(1)} %constant_dynamic-update-slice_fusion) | copy-start | bytes 2949124
  113.6 1.2 copy-start.19
  114.8 13.6 %copy-start.9 = (bf16[384,1280]{1,0:T(8,128)(2,1)}, bf16[384,1280]{1,0:T(8,128)(2,1)S(1)}, u32[]{:S(2)}) copy-start(bf16[384,1280]{1,0:T(8,128)(2,1)S(1)} %convolution_convert_fusion) | copy-start | bytes 2949124
  115.7 33.3 %collective-permute-start.7 = (bf16[96,1280]{1,0:T(8,128)(2,1)}, bf16[96,1280]{1,0:T(8,128)(2,1)S(1)}, u32[]{:S(2)}, u32[]{:S(2)}) collective-permute-start(bf16[96,1280]{1,0:T(8,128)(2,1)} %get-tuple-element.38), channel_id=1, source_target_pairs={{0,128},{32,160},{64,192},{96,224},{128,256},{160,288},{192,320},{... | collective-permute-start | bytes 737288 | tf_op jit(solution)/shard_map/ppermute | solution.py:40
  117.7 31.4 %collective-permute-start.9 = (bf16[96,1280]{1,0:T(8,128)(2,1)}, bf16[96,1280]{1,0:T(8,128)(2,1)}, u32[]{:S(2)}, u32[]{:S(2)}) collective-permute-start(bf16[96,1280]{1,0:T(8,128)(2,1)} %get-tuple-element.39), channel_id=1, source_target_pairs={{0,384},{32,416},{64,448},{96,480},{128,0},{160,32},{192,64},{224,... | collective-permute-start | bytes 737288 | tf_op jit(solution)/shard_map/ppermute | solution.py:40
  122.8 26.2 %collective-permute-start.8 = (bf16[96,1280]{1,0:T(8,128)(2,1)}, bf16[96,1280]{1,0:T(8,128)(2,1)}, u32[]{:S(2)}, u32[]{:S(2)}) collective-permute-start(bf16[96,1280]{1,0:T(8,128)(2,1)} %get-tuple-element.40), channel_id=1, source_target_pairs={{0,256},{32,288},{64,320},{96,352},{128,384},{160,416},{192,448},{... | collective-permute-start | bytes 737288 | tf_op jit(solution)/shard_map/ppermute | solution.py:40
  141.4 15.1 %collective-permute-start.13 = (bf16[224,1280]{1,0:T(8,128)(2,1)}, bf16[224,1280]{1,0:T(8,128)(2,1)}, u32[]{:S(2)}, u32[]{:S(2)}) collective-permute-start(bf16[224,1280]{1,0:T(8,128)(2,1)} %get-tuple-element.31), channel_id=1, source_target_pairs={{0,32},{32,64},{64,96},{96,0},{128,160},{160,192},{192,224},{224,1... | collective-permute-start | bytes 1720328 | tf_op jit(solution)/shard_map/ppermute | solution.py:40
  144.4 14.0 %collective-permute-start.14 = (bf16[224,1280]{1,0:T(8,128)(2,1)}, bf16[224,1280]{1,0:T(8,128)(2,1)S(1)}, u32[]{:S(2)}, u32[]{:S(2)}) collective-permute-start(bf16[224,1280]{1,0:T(8,128)(2,1)} %get-tuple-element.32), channel_id=1, source_target_pairs={{0,96},{32,0},{64,32},{96,64},{128,224},{160,128},{192,160},{224,1... | collective-permute-start | bytes 1720328 | tf_op jit(solution)/shard_map/ppermute | solution.py:40
  150.4 7.7 %copy-start.7 = (bf16[224,1280]{1,0:T(8,128)(2,1)S(1)}, bf16[224,1280]{1,0:T(8,128)(2,1)}, u32[]{:S(2)}) copy-start(bf16[224,1280]{1,0:T(8,128)(2,1)} %get-tuple-element.33) | copy-start | bytes 1720324
  158.1 1.7 copy-start.6
  159.9 17.9 %copy-start.17 = (s32[1,32,3]{1,0,2:T(1,128)S(1)}, s32[1,32,3]{1,0,2:T(1,128)}, u32[]{:S(2)}) copy-start(s32[1,32,3]{1,0,2:T(1,128)} %param.13) | copy-start | bytes 1156
  161.0 35.5 %collective-permute-start.15 = (bf16[448,1280]{1,0:T(8,128)(2,1)S(1)}, bf16[448,1280]{1,0:T(8,128)(2,1)}, u32[]{:S(2)}, u32[]{:S(2)}) collective-permute-start(bf16[448,1280]{1,0:T(8,128)(2,1)S(1)} %pad_maximum_fusion.2), channel_id=1, source_target_pairs={{0,32},{32,64},{64,96},{96,0},{128,160},{160,192},{192,224},{224,1... | collective-permute-start | bytes 3440648 | tf_op jit(solution)/shard_map/ppermute | solution.py:40
  162.9 35.1 %collective-permute-start.16 = (bf16[448,1280]{1,0:T(8,128)(2,1)}, bf16[448,1280]{1,0:T(8,128)(2,1)}, u32[]{:S(2)}, u32[]{:S(2)}) collective-permute-start(bf16[448,1280]{1,0:T(8,128)(2,1)} %pad_maximum_fusion.3), channel_id=1, source_target_pairs={{0,96},{32,0},{64,32},{96,64},{128,224},{160,128},{192,160},{224,1... | collective-permute-start | bytes 3440648 | tf_op jit(solution)/shard_map/ppermute | solution.py:40
  168.1 26.4 %all-to-all-start.2 = ((bf16[32,3,1280]{2,1,0:T(4,128)(2,1)}), bf16[32,3,1280]{2,1,0:T(4,128)(2,1)S(1)}, u32[]{:S(2)}, u32[]{:S(2)}) async-start(bf16[32,3,1280]{2,1,0:T(4,128)(2,1)} %reshape.79), calls=%async_computation.2 | async-start | bytes 655360 | tf_op jit(solution)/shard_map/all_to_all | solution.py:44
  197.9 1.6 copy-start.3
  197.9 1.6 copy-start.5
  198.0 1.7 copy-start.11
  198.0 1.9 copy-start.12
  198.0 2.1 %copy-start.13 = (bf16[1,1280,224]{1,2,0:T(8,128)(2,1)S(1)}, bf16[1,1280,224]{1,2,0:T(8,128)(2,1)}, u32[]{:S(2)}) copy-start(bf16[1,1280,224]{1,2,0:T(8,128)(2,1)} %param.19) | copy-start | bytes 1720324
  198.0 2.2 %copy-start.14 = (bf16[1,1280,224]{1,2,0:T(8,128)(2,1)S(1)}, bf16[1,1280,224]{1,2,0:T(8,128)(2,1)}, u32[]{:S(2)}) copy-start(bf16[1,1280,224]{1,2,0:T(8,128)(2,1)} %param.17) | copy-start | bytes 1720324

commit v2 on v0

v2 whole, which is shorter than its diff:
```python
import jax
import jax.numpy as jnp
from jax import lax
from jax.experimental import pallas as pl
from jax.experimental.pallas import tpu as pltpu
from jax.sharding import Mesh, PartitionSpec as P

LAYERS = 32
STEP_COUNT = 10

BETA_ONE = 0.9
BETA_TWO = 0.999
EPSILON = 1e-08
DECAY_RATE = 0.9
WEIGHT_DECAY = 0.1

RING = 4
COLUMN = 8
SOURCES = 16
PICKS = 3
EXPERTS = 32
FROM_ONE = 6
PADDED = 8
CHUNK = SOURCES * PICKS
WIDTH = 1280
GROUP = 224
ROWS = COLUMN * CHUNK
SMALL, LARGE = 12 * 1024 * 1024, 60 * 1024 * 1024


def adam_step(gradient, first_moment, second_moment, weight, factor):
    running_mean = BETA_ONE * first_moment.astype(jnp.float32) + (1.0 - BETA_ONE) * gradient
    running_square = (
        BETA_TWO * second_moment.astype(jnp.float32) + (1.0 - BETA_TWO) * gradient * gradient
    )
    mean_hat = running_mean * (1.0 / (1.0 - BETA_ONE**STEP_COUNT))
    square_hat = running_square * (1.0 / (1.0 - BETA_TWO**STEP_COUNT))
    update = mean_hat / (jnp.sqrt(square_hat) + EPSILON) + WEIGHT_DECAY * weight.astype(jnp.float32)
    return (factor * update).astype(jnp.bfloat16)


def contract(left, right, left_dim, right_dim, precision=None):
    return lax.dot_general(
        left,
        right,
        (((left_dim,), (right_dim,)), ((), ())),
        precision=precision,
        preferred_element_type=jnp.float32,
    )


def call(kernel, shapes, args, scratch=(), flops=0, limit=SMALL, outside=(), outputs_outside=False):
    spec = pl.BlockSpec(memory_space=pltpu.VMEM)
    moved = sum(a.size * a.dtype.itemsize for a in args)
    moved += sum(s.size * s.dtype.itemsize for s in shapes)
    far = pl.BlockSpec(memory_space=pl.ANY)
    scalar = pl.BlockSpec(memory_space=pltpu.SMEM)
    return pl.pallas_call(
        kernel,
        out_shape=shapes,
        in_specs=[
            scalar if a.ndim == 1 else far if i in outside else spec for i, a in enumerate(args)
        ],
        out_specs=[far if outputs_outside else spec] * len(shapes),
        scratch_shapes=scratch,
        compiler_params=pltpu.CompilerParams(vmem_limit_bytes=limit),
        cost_estimate=pl.CostEstimate(flops=flops, bytes_accessed=moved, transcendentals=0),
    )(*args)


def slot_masks():
    shape = (SOURCES * PADDED, EXPERTS)
    row = lax.broadcasted_iota(jnp.int32, shape, 0)
    lane = lax.broadcasted_iota(jnp.int32, shape, 1)
    slot = row & 7
    half = jnp.where(slot >= PICKS, 1, 0)
    same = (lane == half * SOURCES + (row >> 3)) & (slot < FROM_ONE)
    return [same & (slot - PICKS * half == k) for k in range(PICKS)]


def row_values(masks, values_ref):
    column = None
    for k in range(PICKS):
        term = jnp.where(masks[k], values_ref[k].astype(jnp.float32), 0.0)
        term = jnp.sum(term, axis=1, keepdims=True)
        column = term if column is None else column + term
    return column


def row_choice(masks, chosen_ref, tokens):
    chosen = row_values(masks, chosen_ref).astype(jnp.int32)
    local = lax.broadcasted_iota(jnp.int32, (SOURCES * PADDED, tokens), 1)
    return chosen == local


def pick_kernel(tokens, cotangent, chosen, gates, send, token_rows, back_rows, sems):
    copies = [
        pltpu.make_async_copy(tokens, token_rows, sems.at[0]),
        pltpu.make_async_copy(cotangent, back_rows, sems.at[1]),
    ]
    for copy in copies:
        copy.start()
    masks = slot_masks()
    choice = row_choice(masks, chosen, tokens.shape[0]).astype(jnp.bfloat16)
    gate = row_values(masks, gates)
    copies[0].wait()
    picked = contract(choice, token_rows[...], 1, 0)
    copies[1].wait()
    scaled = gate * contract(choice, back_rows[...], 1, 0)
    for i in range(SOURCES):
        here = slice(i * PADDED, i * PADDED + FROM_ONE)
        send[i, :FROM_ONE] = picked[here].astype(jnp.bfloat16)
        send[i, FROM_ONE:] = scaled[here].astype(jnp.bfloat16)


def spread_kernel(place, arrived, *rest):
    sends, (rows, halves) = rest[:4], rest[4:]
    rows[...] = jnp.zeros_like(rows)
    for i in range(SOURCES):
        rows[i * 16 : i * 16 + 2 * FROM_ONE, :] = arrived[i]
    shape = (2 * CHUNK, SOURCES * 16)
    after = lax.broadcasted_iota(jnp.int32, shape, 0)
    before = lax.broadcasted_iota(jnp.int32, shape, 1)
    second = jnp.where(after >= CHUNK, 1, 0)
    after = after - CHUNK * second
    slot = (before & 15) - FROM_ONE * second - (after >> 4)
    for half in range(2):
        order = ((before >> 4) == (after & 15)) & (slot == PICKS * half)
        ordered = contract(order.astype(jnp.bfloat16), rows[...], 1, 0)
        halves[half] = ordered.astype(jnp.bfloat16)
    for send, target in zip(sends, (place[0], place[1], place[2], place[3])):
        send[...] = halves[target >> 2]


def gather_kernel(arrived, send, total):
    for half in range(2):
        chunk = arrived[half].astype(jnp.float32)
        for z in range(1, 4):
            chunk = chunk + arrived[z * 2 + half].astype(jnp.float32)
        total[half * CHUNK : half * CHUNK + CHUNK, :] = chunk.astype(jnp.bfloat16)
    shape = (SOURCES * PADDED, 2 * CHUNK)
    after = lax.broadcasted_iota(jnp.int32, shape, 0)
    before = lax.broadcasted_iota(jnp.int32, shape, 1)
    half = jnp.where(before >= CHUNK, 1, 0)
    before = before - CHUNK * half
    order = ((before & 15) == (after >> 3)) & ((after & 7) == PICKS * half + (before >> 4))
    ordered = contract(order.astype(jnp.bfloat16), total[...], 1, 0)
    for i in range(SOURCES):
        send[i] = ordered[i * PADDED : i * PADDED + FROM_ONE].astype(jnp.bfloat16)


def expert_kernel(place, *args):
    blocks, (own, left, right, up_far, down_far) = args[:8], args[8:13]
    outs, args = args[13:22], args[22:]
    staged, (rows, grads, up, down, units, slopes, sems, out_sems) = args[:9], args[9:]
    halves = pl.ds(0, GROUP), pl.ds(GROUP, GROUP)
    pairs = [(b.at[pl.ds(0, CHUNK)], rows.at[pl.ds(j * CHUNK, CHUNK)]) for j, b in enumerate(blocks)]
    pairs += [(piece.at[halves[0]], up.at[i]) for i, piece in enumerate((own, left, right), 1)]
    pairs += [(up_far, up.at[0])]
    pairs += [(piece.at[halves[1]], down.at[i]) for i, piece in enumerate((own, left, right), 1)]
    pairs += [(down_far, down.at[0])]
    pairs += [
        (b.at[pl.ds(CHUNK, CHUNK)], grads.at[pl.ds(j * CHUNK, CHUNK)]) for j, b in enumerate(blocks)
    ]
    copies = [pltpu.make_async_copy(src, dst, sems.at[n]) for n, (src, dst) in enumerate(pairs)]
    for copy in copies:
        copy.start()
    for copy in copies[:12]:
        copy.wait()
    for i in range(RING):
        pre = contract(up[i], rows[...], 1, 1)
        share = 0.5 * (1.0 + lax.erf(pre * 0.7071067811865476))
        units[i] = (pre * share).astype(jnp.bfloat16)
        slopes[i] = share + pre * (0.3989422804014327 * jnp.exp(-0.5 * pre * pre))
    for copy in copies[12:]:
        copy.wait()
    cuts = [pl.ds(n, 256) for n in range(0, WIDTH, 256)]
    writes = [pltpu.make_async_copy(s, o, out_sems.at[n]) for n, (s, o) in enumerate(zip(staged, outs))]
    for n, i in enumerate((0, 2, 3, 1)):
        back = (slopes[i] * contract(down[i], grads[...], 1, 1)).astype(jnp.bfloat16)
        for cut in cuts:
            for out, a, b in zip(staged[2 * n : 2 * n + 2], (back, units[i]), (rows, grads)):
                out[:, cut] = contract(a, b[:, cut], 1, 0).astype(out.dtype)
        writes[2 * n].start()
        writes[2 * n + 1].start()
    for cut in cuts:
        total = contract(units[0], down[0, :, cut], 0, 0)
        for i in range(1, RING):
            total = total + contract(units[i], down[i, :, cut], 0, 0)
        for j in range(8):
            staged[8][place[j], :, cut] = total[j * CHUNK : j * CHUNK + CHUNK].astype(jnp.bfloat16)
    writes[8].start()
    for write in writes:
        write.wait()


def combine_kernel(returned, cotangent, chosen, gates, combined, gate_grad, rows):
    tokens = cotangent.shape[0]
    rows[...] = jnp.zeros_like(rows)
    for i in range(SOURCES):
        rows[i * PADDED : i * PADDED + FROM_ONE, :] = returned[i].astype(jnp.float32)
    masks = slot_masks()
    choice = row_choice(masks, chosen, tokens)
    gate = row_values(masks, gates)
    weighted = jnp.where(choice, gate, 0.0)
    combined[...] = contract(weighted, rows[...], 0, 0, lax.Precision.HIGHEST).astype(jnp.bfloat16)
    back = contract(choice.astype(jnp.bfloat16), cotangent[...], 1, 0)
    inner = jnp.sum(back * rows[...], axis=1, keepdims=True)
    for k in range(PICKS):
        gate_grad[k] = jnp.sum(jnp.where(masks[k], inner, 0.0), axis=0, keepdims=True)


def shape(*dims, dtype=jnp.bfloat16):
    return jax.ShapeDtypeStruct(dims, dtype)


def along_x(values, step):
    return lax.ppermute(values, "x", [(i, (i + step) % RING) for i in range(RING)])


def within_z(rows):
    return lax.all_to_all(rows, ("y", "core"), split_axis=0, concat_axis=0, tiled=True)


def along_z(rows):
    return lax.all_to_all(rows, ("zlo", "zhi"), split_axis=0, concat_axis=0, tiled=True)


def rank(z):
    return z % 4 * 2 + z // 4


def mate(z):
    return z + 1 - 2 * (z % 2)


def to_chip(rows, target):
    pairs = [(rank(z), rank(target(z) % COLUMN)) for z in range(COLUMN)]
    return lax.ppermute(rows, ("zlo", "zhi"), pairs)


HOPS = (
    lambda z: z + 2 - 4 * (z % 2),
    lambda z: z - 1 + 2 * (z % 2),
    lambda z: z - 3 + 6 * (z % 2),
)
ORIGINS = (lambda z: z - 2 + 4 * (z % 2), HOPS[1], HOPS[2])


def per_device(
    tokens,
    cotangent,
    chosen_rows,
    combine_weights,
    up_weight,
    down_weight,
    first_up,
    first_down,
    second_up,
    second_down,
    layer_index,
):
    chosen = chosen_rows.transpose(2, 0, 1)
    gates = combine_weights.transpose(2, 0, 1)
    up_own = up_weight[0].T
    down_own = down_weight[0]
    f32, bf16 = jnp.float32, jnp.bfloat16

    own = jnp.concatenate([up_own, down_own])
    left = along_x(own, 1)
    right = along_x(own, -1)
    up_far = along_x(left[:GROUP], 1)
    down_far = along_x(right[GROUP:], -1)

    z = (lax.axis_index("zhi") * 4 + lax.axis_index("zlo")).astype(jnp.int32)
    first = [z] + [hop(z) % COLUMN for hop in HOPS]
    sources = [z] + [origin(z) for origin in ORIGINS]
    sources += [mate(z)] + [origin(mate(z)) for origin in ORIGINS]
    slots = jnp.stack([rank(source % COLUMN) for source in sources])
    (send,) = call(
        pick_kernel,
        [shape(SOURCES, 2 * FROM_ONE, WIDTH)],
        [tokens, cotangent, chosen, gates],
        [pltpu.VMEM(tokens.shape, bf16)] * 2 + [pltpu.SemaphoreType.DMA((2,))],
        outside=(0, 1),
    )
    blocks = call(
        spread_kernel,
        [shape(2 * CHUNK, WIDTH)] * 4,
        [jnp.stack(first), within_z(send)],
        [pltpu.VMEM((SOURCES * 16, WIDTH), bf16), pltpu.VMEM((2, 2 * CHUNK, WIDTH), bf16)],
    )
    blocks = [blocks[0]] + [to_chip(block, hop) for block, hop in zip(blocks[1:], HOPS)]
    blocks += [to_chip(block, mate) for block in blocks]

    weight = shape(GROUP, WIDTH)
    wide = shape(GROUP, WIDTH, dtype=f32)
    gradients = [weight, weight, weight, wide, wide, weight, wide, wide]
    results = [*gradients, shape(COLUMN, CHUNK, WIDTH)]
    outputs = call(
        expert_kernel,
        results,
        [slots, *blocks, own, left, right, up_far, down_far],
        [pltpu.VMEM(r.shape, r.dtype) for r in results]
        + [pltpu.VMEM((ROWS, WIDTH), bf16)] * 2
        + [pltpu.VMEM((RING, GROUP, WIDTH), bf16)] * 2
        + [pltpu.VMEM((RING, GROUP, ROWS), dtype) for dtype in (bf16, f32)]
        + [pltpu.SemaphoreType.DMA((24,)), pltpu.SemaphoreType.DMA((9,))],
        flops=40 * ROWS * GROUP * WIDTH,
        limit=LARGE,
        outside=range(1, 14),
        outputs_outside=True,
    )
    far_up, far_down, left_up, left_down, right_up, right_down, own_up, own_down, partial = outputs
    arrived = along_z(partial)

    up_two = along_x(far_up, 1).astype(f32)
    down_two = along_x(far_down, -1).astype(f32)
    up_from_right = along_x(left_up, -1).astype(f32)
    down_from_left = along_x(right_down, 1).astype(f32)
    up_from_left = along_x((right_up + up_two).astype(jnp.bfloat16), 1).astype(f32)
    down_from_right = along_x((left_down + down_two).astype(jnp.bfloat16), -1).astype(f32)
    total_up = own_up + up_from_right + up_from_left
    total_down = own_down + down_from_left + down_from_right

    exponent = (LAYERS - 1 - layer_index[0]).astype(f32)
    factor = jnp.power(f32(DECAY_RATE), exponent)
    step_up = adam_step(total_up, first_up[0].T, second_up[0].T, up_own, factor).T[None]
    step_down = adam_step(total_down, first_down[0], second_down[0], down_own, factor)[None]

    scratch = [pltpu.VMEM((2 * CHUNK, WIDTH), bf16)]
    (summed,) = call(gather_kernel, [shape(SOURCES, FROM_ONE, WIDTH)], [arrived], scratch)
    combined, gate_grad = call(
        combine_kernel,
        [shape(tokens.shape[0], WIDTH), shape(PICKS, 1, EXPERTS, dtype=f32)],
        [within_z(summed), cotangent, chosen, gates],
        [pltpu.VMEM((SOURCES * PADDED, WIDTH), f32)],
    )
    return (combined, gate_grad.transpose(1, 2, 0), step_up, step_down)


def solution(mesh):
    fine = Mesh(mesh.devices.reshape(4, RING, 2, 8, 2), ("zlo", "x", "zhi", "y", "core"))
    dp, expert = ("zlo", "x"), ("zhi", "y", "core")
    both = dp + expert
    placed = (
        P(both, None),
        P(both, None),
        P(both, None, None),
        P(both, None, None),
        P(expert, None, dp),
        P(expert, dp, None),
        P(expert, None, dp),
        P(expert, dp, None),
        P(expert, None, dp),
        P(expert, dp, None),
        P(),
    )
    return jax.shard_map(
        per_device,
        mesh=fine,
        in_specs=placed,
        out_specs=(P(both, None), P(both, None, None), P(expert, None, dp), P(expert, dp, None)),
        check_vma=False,
    )
```

time: 427 us -> 169 us (0.40)
  the two profiles are of different devices: /device:TPU:42 before, /device:TPU:1 now
where the time goes in v2:
time: 169 us; the launch traced here: 168 us
  starting transfers between devices  82.8 us (49%)
  waiting for transfers between devices  53.2 us (31%)
  Pallas kernels  18 us (11%)
  other arithmetic  8.9 us (5%)
  local copies, waits for them, and re-layouts  3.29 us (2%)
  between operations  2.24 us (1%)
    ppermute x7, starting transfers between devices, to_chip(): return lax.ppermute(rows, ('zlo', 'zhi'), pairs)  32.3 us
    ppermute x10, starting transfers between devices, along_x(): lax.ppermute(values, 'x', [(i, (i + step) % RING) for i in range(RING)])  32.2 us
    all_to_all x2, waiting for transfers between devices, within_z(): lax.all_to_all(rows, ('y', 'core'), split_axis=0, concat_axis=0, tiled=True)  23.2 us
    ppermute x10, waiting for transfers between devices, along_x(): lax.ppermute(values, 'x', [(i, (i + step) % RING) for i in range(RING)])  18.4 us
    pallas_call x5, Pallas kernels, call(): pl.pallas_call(kernel, out_shape=shapes, in_specs=[scalar if a.ndim == 1...  18 us
    all_to_all x2, starting transfers between devices, within_z(): lax.all_to_all(rows, ('y', 'core'), split_axis=0, concat_axis=0, tiled=True)  13.9 us
    ppermute x7, waiting for transfers between devices, to_chip(): return lax.ppermute(rows, ('zlo', 'zhi'), pairs)  11.7 us
    all_to_all x1, starting transfers between devices, along_z(): lax.all_to_all(rows, ('zlo', 'zhi'), split_axis=0, concat_axis=0, tiled=T...  4.47 us
  transfers between devices with their start and end apart: 20, of which 10 were waited for; matrix products, arithmetic and copies ran while one was open for 6% of the time, Pallas kernels for 2%

profile of v2, /device:TPU:1, one launch (start us, length us, event | category | flops | bytes accessed | tf_op | source)
XLA Modules:
  0.0 168.5 jit_solution(13197680101651912433)
XLA Ops:
  0.6 0.0 copy-start
  0.6 0.0 copy-start.1
  0.7 1.4 pad_maximum_fusion.args_8_
  2.1 5.2 %collective-permute-start.8 = (bf16[448,1280]{1,0:T(8,128)(2,1)S(1)}, bf16[448,1280]{1,0:T(8,128)(2,1)S(1)}, u32[]{:S(2)}, u32[]{:S(2)}) collective-permute-start(bf16[448,1280]{1,0:T(8,128)(2,1)S(1)} %pad_maximum_fusion.args_8_), channel_id=1, source_target_pairs={{0,96},{32,0},{64,32},{96,64},{1,97},{33,1},{65,33},{97,65},{2,98}... | collective-permute-start | bytes 3440648 | tf_op jit(solution)/shard_map/ppermute | solution.py:218
  7.3 1.9 %collective-permute-start.7 = (bf16[448,1280]{1,0:T(8,128)(2,1)S(1)}, bf16[448,1280]{1,0:T(8,128)(2,1)}, u32[]{:S(2)}, u32[]{:S(2)}) collective-permute-start(bf16[448,1280]{1,0:T(8,128)(2,1)S(1)} %pad_maximum_fusion.args_8_), channel_id=1, source_target_pairs={{0,32},{32,64},{64,96},{96,0},{1,33},{33,65},{65,97},{97,1},{2,34}... | collective-permute-start | bytes 3440648 | tf_op jit(solution)/shard_map/ppermute | solution.py:218
  9.2 1.9 %shard_map.138 = bf16[16,12,1280]{2,1,0:T(8,128)(2,1)} custom-call(bf16[48,1280]{1,0:T(8,128)(2,1)S(1)} %copy-done.1, bf16[48,1280]{1,0:T(8,128)(2,1)S(1)} %copy-done, s32[3,1,32]{2,1,0:T(1,128)S(1)} %bitcast.64, f32[3,1,32]{2,1,0:T(1,128)S(1)} %bitcast.66), custom_call_target="tpu_custom_call" | custom-call | bytes 738048 | tf_op jit(solution)/shard_map/pallas_call | solution.py:58
  11.1 9.0 %all-to-all-start = ((bf16[16,12,1280]{2,1,0:T(8,128)(2,1)}), bf16[16,12,1280]{2,1,0:T(8,128)(2,1)S(1)}, u32[]{:S(2)}, u32[]{:S(2)}) async-start(bf16[16,12,1280]{2,1,0:T(8,128)(2,1)} %shard_map.138), calls=%async_computation | async-start | bytes 1310720 | tf_op jit(solution)/shard_map/all_to_all | solution.py:222
  20.1 0.1 pad_add_fusion.place
  20.2 19.9 %all-to-all-done.arrived = bf16[16,12,1280]{2,1,0:T(8,128)(2,1)S(1)} async-done(((bf16[16,12,1280]{2,1,0:T(8,128)(2,1)}), bf16[16,12,1280]{2,1,0:T(8,128)(2,1)S(1)}, u32[]{:S(2)}, u32[]{:S(2)}) %all-to-all-start) | async-done | bytes 491552 | tf_op jit(solution)/shard_map/all_to_all | solution.py:222
  40.1 1.0 shard_map.139
  41.1 4.9 %collective-permute-start = (bf16[96,1280]{1,0:T(8,128)(2,1)S(1)}, bf16[96,1280]{1,0:T(8,128)(2,1)S(1)}, u32[]{:S(2)}, u32[]{:S(2)}) collective-permute-start(bf16[96,1280]{1,0:T(8,128)(2,1)S(1)} %get-tuple-element.20), channel_id=1, source_target_pairs={{0,256},{128,400},{256,16},{384,128},{16,272},{144,384},{272,0},{4... | collective-permute-start | bytes 737288 | tf_op jit(solution)/shard_map/ppermute | solution.py:239
  46.0 0.0 collective-permute-done.8.args_10_
  46.1 0.0 copy-start.15
  46.1 4.9 %collective-permute-start.10 = (bf16[224,1280]{1,0:T(8,128)(2,1)S(1)}, bf16[224,1280]{1,0:T(8,128)(2,1)}, u32[]{:S(2)}, u32[]{:S(2)}) collective-permute-start(bf16[224,1280]{1,0:T(8,128)(2,1)S(1)} %slice.9), channel_id=1, source_target_pairs={{0,96},{32,0},{64,32},{96,64},{1,97},{33,1},{65,33},{97,65},{2,98}... | collective-permute-start | bytes 1720328 | tf_op jit(solution)/shard_map/ppermute | solution.py:218
  51.0 0.0 collective-permute-done.7.args_9_
  51.0 1.1 slice.8
  52.1 1.9 %collective-permute-start.9 = (bf16[224,1280]{1,0:T(8,128)(2,1)S(1)}, bf16[224,1280]{1,0:T(8,128)(2,1)S(1)}, u32[]{:S(2)}, u32[]{:S(2)}) collective-permute-start(bf16[224,1280]{1,0:T(8,128)(2,1)S(1)} %slice.8), channel_id=1, source_target_pairs={{0,32},{32,64},{64,96},{96,0},{1,33},{33,65},{65,97},{97,1},{2,34}... | collective-permute-start | bytes 1720328 | tf_op jit(solution)/shard_map/ppermute | solution.py:218
  54.0 7.0 %collective-permute-start.1 = (bf16[96,1280]{1,0:T(8,128)(2,1)S(1)}, bf16[96,1280]{1,0:T(8,128)(2,1)}, u32[]{:S(2)}, u32[]{:S(2)}) collective-permute-start(bf16[96,1280]{1,0:T(8,128)(2,1)S(1)} %get-tuple-element.21), channel_id=1, source_target_pairs={{0,400},{128,256},{256,128},{384,16},{16,384},{144,272},{272,144},... | collective-permute-start | bytes 737288 | tf_op jit(solution)/shard_map/ppermute | solution.py:239
  61.1 2.8 %collective-permute-start.2 = (bf16[96,1280]{1,0:T(8,128)(2,1)S(1)}, bf16[96,1280]{1,0:T(8,128)(2,1)S(1)}, u32[]{:S(2)}, u32[]{:S(2)}) collective-permute-start(bf16[96,1280]{1,0:T(8,128)(2,1)S(1)} %get-tuple-element.22), channel_id=1, source_target_pairs={{0,144},{128,16},{256,400},{384,272},{16,128},{144,0},{272,384},{4... | collective-permute-start | bytes 737288 | tf_op jit(solution)/shard_map/ppermute | solution.py:239
  63.9 0.0 collective-permute-done.args_1_
  63.9 3.1 %collective-permute-start.3 = (bf16[96,1280]{1,0:T(8,128)(2,1)S(1)}, bf16[96,1280]{1,0:T(8,128)(2,1)S(1)}, u32[]{:S(2)}, u32[]{:S(2)}) collective-permute-start(bf16[96,1280]{1,0:T(8,128)(2,1)S(1)} %get-tuple-element.19.args_0_), channel_id=1, source_target_pairs={{0,128},{128,0},{256,384},{384,256},{16,144},{144,16},{272,400},{4... | collective-permute-start | bytes 737288 | tf_op jit(solution)/shard_map/ppermute | solution.py:239
  67.0 0.0 collective-permute-done.1.args_2_
  67.0 6.3 %collective-permute-start.4 = (bf16[96,1280]{1,0:T(8,128)(2,1)S(1)}, bf16[96,1280]{1,0:T(8,128)(2,1)S(1)}, u32[]{:S(2)}, u32[]{:S(2)}) collective-permute-start(bf16[96,1280]{1,0:T(8,128)(2,1)S(1)} %collective-permute-done.args_1_), channel_id=1, source_target_pairs={{0,128},{128,0},{256,384},{384,256},{16,144},{144,16},{272,400},{4... | collective-permute-start | bytes 737288 | tf_op jit(solution)/shard_map/ppermute | solution.py:239
  73.3 0.6 collective-permute-done.2.args_3_
  73.9 5.4 %collective-permute-start.5 = (bf16[96,1280]{1,0:T(8,128)(2,1)}, bf16[96,1280]{1,0:T(8,128)(2,1)S(1)}, u32[]{:S(2)}, u32[]{:S(2)}) collective-permute-start(bf16[96,1280]{1,0:T(8,128)(2,1)} %collective-permute-done.1.args_2_), channel_id=1, source_target_pairs={{0,128},{128,0},{256,384},{384,256},{16,144},{144,16},{272,400},{4... | collective-permute-start | bytes 737288 | tf_op jit(solution)/shard_map/ppermute | solution.py:239
  79.3 0.0 collective-permute-done.3.args_4_
  79.4 2.8 %collective-permute-start.6 = (bf16[96,1280]{1,0:T(8,128)(2,1)S(1)}, bf16[96,1280]{1,0:T(8,128)(2,1)S(1)}, u32[]{:S(2)}, u32[]{:S(2)}) collective-permute-start(bf16[96,1280]{1,0:T(8,128)(2,1)S(1)} %collective-permute-done.2.args_3_), channel_id=1, source_target_pairs={{0,128},{128,0},{256,384},{384,256},{16,144},{144,16},{272,400},{4... | collective-permute-start | bytes 737288 | tf_op jit(solution)/shard_map/ppermute | solution.py:239
  82.6 0.6 stack.50.place
  83.2 1.1 collective-permute-done.4.args_5_
  84.3 5.3 %collective-permute-done.5.args_6_ = bf16[96,1280]{1,0:T(8,128)(2,1)S(1)} collective-permute-done((bf16[96,1280]{1,0:T(8,128)(2,1)}, bf16[96,1280]{1,0:T(8,128)(2,1)S(1)}, u32[]{:S(2)}, u32[]{:S(2)}) %collective-permute-start.5) | collective-permute-done | bytes 245792 | tf_op jit(solution)/shard_map/ppermute | solution.py:239
  89.6 4.7 %collective-permute-done.6.args_7_ = bf16[96,1280]{1,0:T(8,128)(2,1)S(1)} collective-permute-done((bf16[96,1280]{1,0:T(8,128)(2,1)S(1)}, bf16[96,1280]{1,0:T(8,128)(2,1)S(1)}, u32[]{:S(2)}, u32[]{:S(2)}) %collective-permute-start.6) | collective-permute-done | bytes 245792 | tf_op jit(solution)/shard_map/ppermute | solution.py:239
  94.3 0.0 collective-permute-done.10.args_12_
  94.3 0.0 collective-permute-done.9.args_11_
  94.3 0.0 copy-done.17
  94.3 0.0 copy-done.18
  94.3 0.0 copy-done.19
  94.3 0.0 copy-done.20
  94.3 0.0 copy-done.21
  94.3 0.6 copy-done.22
  95.0 0.8 copy-done.16
  95.8 12.7 %shard_map.140 = (bf16[224,1280]{1,0:T(8,128)(2,1)}, bf16[224,1280]{1,0:T(8,128)(2,1)}, bf16[224,1280]{1,0:T(8,128)(2,1)}, f32[224,1280]{1,0:T(8,128)}, f32[224,...) custom-call(s32[8]{0:T(128)} %stack.50.place, ...), custom_call_target="tpu_custom_call" | custom-call | flops 4404019200 | bytes 14417952 | tf_op jit(solution)/shard_map/pallas_call | solution.py:58
  108.5 5.3 %collective-permute-start.15 = (bf16[224,1280]{1,0:T(8,128)(2,1)}, bf16[224,1280]{1,0:T(8,128)(2,1)}, u32[]{:S(2)}, u32[]{:S(2)}) collective-permute-start(bf16[224,1280]{1,0:T(8,128)(2,1)} %get-tuple-element.33), channel_id=1, source_target_pairs={{0,96},{32,0},{64,32},{96,64},{1,97},{33,1},{65,33},{97,65},{2,98}... | collective-permute-start | bytes 1720328 | tf_op jit(solution)/shard_map/ppermute | solution.py:218
  113.8 1.9 %collective-permute-start.14 = (bf16[224,1280]{1,0:T(8,128)(2,1)}, bf16[224,1280]{1,0:T(8,128)(2,1)S(1)}, u32[]{:S(2)}, u32[]{:S(2)}) collective-permute-start(bf16[224,1280]{1,0:T(8,128)(2,1)} %get-tuple-element.31), channel_id=1, source_target_pairs={{0,32},{32,64},{64,96},{96,0},{1,33},{33,65},{65,97},{97,1},{2,34}... | collective-permute-start | bytes 1720328 | tf_op jit(solution)/shard_map/ppermute | solution.py:218
  115.7 1.9 %collective-permute-start.12 = (bf16[224,1280]{1,0:T(8,128)(2,1)}, bf16[224,1280]{1,0:T(8,128)(2,1)S(1)}, u32[]{:S(2)}, u32[]{:S(2)}) collective-permute-start(bf16[224,1280]{1,0:T(8,128)(2,1)} %get-tuple-element.29), channel_id=1, source_target_pairs={{0,32},{32,64},{64,96},{96,0},{1,33},{33,65},{65,97},{97,1},{2,34}... | collective-permute-start | bytes 1720328 | tf_op jit(solution)/shard_map/ppermute | solution.py:218
  117.7 4.5 %all-to-all-start.1 = ((bf16[8,48,1280]{2,1,0:T(8,128)(2,1)}), bf16[8,48,1280]{2,1,0:T(8,128)(2,1)S(1)}, u32[]{:S(2)}, u32[]{:S(2)}) async-start(bf16[8,48,1280]{2,1,0:T(8,128)(2,1)} %get-tuple-element.23), calls=%async_computation.1 | async-start | bytes 1966080 | tf_op jit(solution)/shard_map/all_to_all | solution.py:226
  122.1 3.9 %collective-permute-done.15 = bf16[224,1280]{1,0:T(8,128)(2,1)} collective-permute-done((bf16[224,1280]{1,0:T(8,128)(2,1)}, bf16[224,1280]{1,0:T(8,128)(2,1)}, u32[]{:S(2)}, u32[]{:S(2)}) %collective-permute-start.15) | collective-permute-done | bytes 573472 | tf_op jit(solution)/shard_map/ppermute | solution.py:218
  126.1 1.3 add_convert_fusion
  127.4 5.3 %collective-permute-start.16 = (bf16[224,1280]{1,0:T(8,128)(2,1)S(1)}, bf16[224,1280]{1,0:T(8,128)(2,1)S(1)}, u32[]{:S(2)}, u32[]{:S(2)}) collective-permute-start(bf16[224,1280]{1,0:T(8,128)(2,1)S(1)} %add_convert_fusion), channel_id=1, source_target_pairs={{0,96},{32,0},{64,32},{96,64},{1,97},{33,1},{65,33},{97,65},{2,98}... | collective-permute-start | bytes 1720328 | tf_op jit(solution)/shard_map/ppermute | solution.py:218
  133.4 1.9 %collective-permute-start.11 = (bf16[224,1280]{1,0:T(8,128)(2,1)}, bf16[224,1280]{1,0:T(8,128)(2,1)}, u32[]{:S(2)}, u32[]{:S(2)}) collective-permute-start(bf16[224,1280]{1,0:T(8,128)(2,1)} %get-tuple-element.27), channel_id=1, source_target_pairs={{0,96},{32,0},{64,32},{96,64},{1,97},{33,1},{65,33},{97,65},{2,98}... | collective-permute-start | bytes 1720328 | tf_op jit(solution)/shard_map/ppermute | solution.py:218
  135.3 8.0 %collective-permute-done.12 = bf16[224,1280]{1,0:T(8,128)(2,1)S(1)} collective-permute-done((bf16[224,1280]{1,0:T(8,128)(2,1)}, bf16[224,1280]{1,0:T(8,128)(2,1)S(1)}, u32[]{:S(2)}, u32[]{:S(2)}) %collective-permute-start.12) | collective-permute-done | bytes 573472 | tf_op jit(solution)/shard_map/ppermute | solution.py:218
  143.3 0.9 add_convert_fusion.1
  144.2 1.9 %collective-permute-start.13 = (bf16[224,1280]{1,0:T(8,128)(2,1)}, bf16[224,1280]{1,0:T(8,128)(2,1)}, u32[]{:S(2)}, u32[]{:S(2)}) collective-permute-start(bf16[224,1280]{1,0:T(8,128)(2,1)} %add_convert_fusion.1), channel_id=1, source_target_pairs={{0,32},{32,64},{64,96},{96,0},{1,33},{33,65},{65,97},{97,1},{2,34}... | collective-permute-start | bytes 1720328 | tf_op jit(solution)/shard_map/ppermute | solution.py:218
  146.1 0.0 collective-permute-done.14
  146.1 0.0 collective-permute-done.16
  146.2 0.0 copy-start.14
  146.2 1.9 %fusion.15 = bf16[1,224,1280]{2,1,0:T(8,128)(2,1)} fusion(bf16[1,224,1280]{2,1,0:T(8,128)(2,1)S(1)} %copy-done.12, bf16[224,1280]{1,0:T(8,128)(2,1)S(1)} %collective-permute-done.16, f32[224,1280]{1,0:T(8,128)S(1)} %copy-done.8, bf16[224,1280]{1,0:T(8,128)(2,1)S(1)} %collective-permute-done.14, bf16[1,224,1280]{2,1,0:T(8,128)(2,1)S(1)} %copy-done.13, ...), kind=kLoop, calls=%fused_computation.24 | loop fusion | flops 6307840 | bytes 4587524 | tf_op jit(solution)/shard_map/broadcast_in_dim | solution.py:329
  148.1 0.0 all-to-all-done.1.arrived
  148.1 1.1 shard_map.141
  149.2 4.9 %all-to-all-start.2 = ((bf16[16,6,1280]{2,1,0:T(8,128)(2,1)}), bf16[16,6,1280]{2,1,0:T(8,128)(2,1)S(1)}, u32[]{:S(2)}, u32[]{:S(2)}) async-start(bf16[16,6,1280]{2,1,0:T(8,128)(2,1)} %shard_map.141), calls=%async_computation.2 | async-start | bytes 655360 | tf_op jit(solution)/shard_map/all_to_all | solution.py:222
  154.0 2.1 %collective-permute-done.11 = bf16[224,1280]{1,0:T(8,128)(2,1)} collective-permute-done((bf16[224,1280]{1,0:T(8,128)(2,1)}, bf16[224,1280]{1,0:T(8,128)(2,1)}, u32[]{:S(2)}, u32[]{:S(2)}) %collective-permute-start.11) | collective-permute-done | bytes 573472 | tf_op jit(solution)/shard_map/ppermute | solution.py:218
  156.1 4.4 %collective-permute-done.13 = bf16[224,1280]{1,0:T(8,128)(2,1)} collective-permute-done((bf16[224,1280]{1,0:T(8,128)(2,1)}, bf16[224,1280]{1,0:T(8,128)(2,1)}, u32[]{:S(2)}, u32[]{:S(2)}) %collective-permute-start.13) | collective-permute-done | bytes 573472 | tf_op jit(solution)/shard_map/ppermute | solution.py:218
  160.5 3.3 %fusion.14 = bf16[1,1280,224]{1,2,0:T(8,128)(2,1)} fusion(bf16[1,1280,224]{1,2,0:T(8,128)(2,1)S(1)} %copy-done.14, bf16[224,1280]{1,0:T(8,128)(2,1)} %collective-permute-done.13, f32[224,1280]{1,0:T(8,128)S(1)} %copy-done.7, bf16[224,1280]{1,0:T(8,128)(2,1)} %collective-permute-done.11, bf16[1,1280,224]{1,2,0:T(8,128)(2,1)} %param.17, f32[]{:T(128)} %bitcast.18, ...), kind=kLoop, calls=%fused_computation.23 | loop fusion | flops 6307840 | bytes 4587524 | tf_op jit(solution)/shard_map/broadcast_in_dim | solution.py:328
  163.8 3.2 %all-to-all-done.2.returned = bf16[16,6,1280]{2,1,0:T(8,128)(2,1)S(1)} async-done(((bf16[16,6,1280]{2,1,0:T(8,128)(2,1)}), bf16[16,6,1280]{2,1,0:T(8,128)(2,1)S(1)}, u32[]{:S(2)}, u32[]{:S(2)}) %all-to-all-start.2) | async-done | bytes 245792 | tf_op jit(solution)/shard_map/all_to_all | solution.py:222
  167.1 1.4 shard_map.142
  (36 shorter events, 0.1 us)
Async XLA Ops:
  0.6 8.6 %copy-start = (bf16[48,1280]{1,0:T(8,128)(2,1)S(1)}, bf16[48,1280]{1,0:T(8,128)(2,1)}, u32[]{:S(2)}) copy-start(bf16[48,1280]{1,0:T(8,128)(2,1)} %cotangent.3) | copy-start | bytes 368644
  0.6 8.6 %copy-start.1 = (bf16[48,1280]{1,0:T(8,128)(2,1)S(1)}, bf16[48,1280]{1,0:T(8,128)(2,1)}, u32[]{:S(2)}) copy-start(bf16[48,1280]{1,0:T(8,128)(2,1)} %tokens.1) | copy-start | bytes 368644
  0.7 8.6 %copy-start.2 = (s32[1,32,3]{1,0,2:T(1,128)S(1)}, s32[1,32,3]{1,0,2:T(1,128)}, u32[]{:S(2)}) copy-start(s32[1,32,3]{1,0,2:T(1,128)} %param.13) | copy-start | bytes 1156
  0.7 8.6 %copy-start.3 = (f32[1,32,3]{1,0,2:T(1,128)S(1)}, f32[1,32,3]{1,0,2:T(1,128)}, u32[]{:S(2)}) copy-start(f32[1,32,3]{1,0,2:T(1,128)} %param.14) | copy-start | bytes 1156
  2.0 18.1 %copy-start.9 = (bf16[448,1280]{1,0:T(8,128)(2,1)}, bf16[448,1280]{1,0:T(8,128)(2,1)S(1)}, u32[]{:S(2)}) copy-start(bf16[448,1280]{1,0:T(8,128)(2,1)S(1)} %pad_maximum_fusion.args_8_) | copy-start | bytes 3440644
  2.1 44.0 %collective-permute-start.8 = (bf16[448,1280]{1,0:T(8,128)(2,1)S(1)}, bf16[448,1280]{1,0:T(8,128)(2,1)S(1)}, u32[]{:S(2)}, u32[]{:S(2)}) collective-permute-start(bf16[448,1280]{1,0:T(8,128)(2,1)S(1)} %pad_maximum_fusion.args_8_), channel_id=1, source_target_pairs={{0,96},{32,0},{64,32},{96,64},{1,97},{33,1},{65,33},{97,65},{2,98}... | collective-permute-start | bytes 3440648 | tf_op jit(solution)/shard_map/ppermute | solution.py:218
  7.3 43.7 %collective-permute-start.7 = (bf16[448,1280]{1,0:T(8,128)(2,1)S(1)}, bf16[448,1280]{1,0:T(8,128)(2,1)}, u32[]{:S(2)}, u32[]{:S(2)}) collective-permute-start(bf16[448,1280]{1,0:T(8,128)(2,1)S(1)} %pad_maximum_fusion.args_8_), channel_id=1, source_target_pairs={{0,32},{32,64},{64,96},{96,0},{1,33},{33,65},{65,97},{97,1},{2,34}... | collective-permute-start | bytes 3440648 | tf_op jit(solution)/shard_map/ppermute | solution.py:218
  11.1 29.0 %all-to-all-start = ((bf16[16,12,1280]{2,1,0:T(8,128)(2,1)}), bf16[16,12,1280]{2,1,0:T(8,128)(2,1)S(1)}, u32[]{:S(2)}, u32[]{:S(2)}) async-start(bf16[16,12,1280]{2,1,0:T(8,128)(2,1)} %shard_map.138), calls=%async_computation | async-start | bytes 1310720 | tf_op jit(solution)/shard_map/all_to_all | solution.py:222
  41.1 22.8 %copy-start.4 = (bf16[96,1280]{1,0:T(8,128)(2,1)}, bf16[96,1280]{1,0:T(8,128)(2,1)S(1)}, u32[]{:S(2)}) copy-start(bf16[96,1280]{1,0:T(8,128)(2,1)S(1)} %get-tuple-element.19.args_0_) | copy-start | bytes 737284
  41.1 22.8 %collective-permute-start = (bf16[96,1280]{1,0:T(8,128)(2,1)S(1)}, bf16[96,1280]{1,0:T(8,128)(2,1)S(1)}, u32[]{:S(2)}, u32[]{:S(2)}) collective-permute-start(bf16[96,1280]{1,0:T(8,128)(2,1)S(1)} %get-tuple-element.20), channel_id=1, source_target_pairs={{0,256},{128,400},{256,16},{384,128},{16,272},{144,384},{272,0},{4... | collective-permute-start | bytes 737288 | tf_op jit(solution)/shard_map/ppermute | solution.py:239
  46.1 8.0 %copy-start.15 = (bf16[448,1280]{1,0:T(8,128)(2,1)}, bf16[448,1280]{1,0:T(8,128)(2,1)S(1)}, u32[]{:S(2)}) copy-start(bf16[448,1280]{1,0:T(8,128)(2,1)S(1)} %collective-permute-done.8.args_10_) | copy-start | bytes 3440644
  46.1 48.2 %collective-permute-start.10 = (bf16[224,1280]{1,0:T(8,128)(2,1)S(1)}, bf16[224,1280]{1,0:T(8,128)(2,1)}, u32[]{:S(2)}, u32[]{:S(2)}) collective-permute-start(bf16[224,1280]{1,0:T(8,128)(2,1)S(1)} %slice.9), channel_id=1, source_target_pairs={{0,96},{32,0},{64,32},{96,64},{1,97},{33,1},{65,33},{97,65},{2,98}... | collective-permute-start | bytes 1720328 | tf_op jit(solution)/shard_map/ppermute | solution.py:218
  52.1 42.2 %collective-permute-start.9 = (bf16[224,1280]{1,0:T(8,128)(2,1)S(1)}, bf16[224,1280]{1,0:T(8,128)(2,1)S(1)}, u32[]{:S(2)}, u32[]{:S(2)}) collective-permute-start(bf16[224,1280]{1,0:T(8,128)(2,1)S(1)} %slice.8), channel_id=1, source_target_pairs={{0,32},{32,64},{64,96},{96,0},{1,33},{33,65},{65,97},{97,1},{2,34}... | collective-permute-start | bytes 1720328 | tf_op jit(solution)/shard_map/ppermute | solution.py:218
  54.0 13.0 %collective-permute-start.1 = (bf16[96,1280]{1,0:T(8,128)(2,1)S(1)}, bf16[96,1280]{1,0:T(8,128)(2,1)}, u32[]{:S(2)}, u32[]{:S(2)}) collective-permute-start(bf16[96,1280]{1,0:T(8,128)(2,1)S(1)} %get-tuple-element.21), channel_id=1, source_target_pairs={{0,400},{128,256},{256,128},{384,16},{16,384},{144,272},{272,144},... | collective-permute-start | bytes 737288 | tf_op jit(solution)/shard_map/ppermute | solution.py:239
  61.1 12.9 %collective-permute-start.2 = (bf16[96,1280]{1,0:T(8,128)(2,1)S(1)}, bf16[96,1280]{1,0:T(8,128)(2,1)S(1)}, u32[]{:S(2)}, u32[]{:S(2)}) collective-permute-start(bf16[96,1280]{1,0:T(8,128)(2,1)S(1)} %get-tuple-element.22), channel_id=1, source_target_pairs={{0,144},{128,16},{256,400},{384,272},{16,128},{144,0},{272,384},{4... | collective-permute-start | bytes 737288 | tf_op jit(solution)/shard_map/ppermute | solution.py:239
  63.9 30.4 %copy-start.17 = (bf16[96,1280]{1,0:T(8,128)(2,1)}, bf16[96,1280]{1,0:T(8,128)(2,1)S(1)}, u32[]{:S(2)}) copy-start(bf16[96,1280]{1,0:T(8,128)(2,1)S(1)} %collective-permute-done.args_1_) | copy-start | bytes 737284
  63.9 15.4 %collective-permute-start.3 = (bf16[96,1280]{1,0:T(8,128)(2,1)S(1)}, bf16[96,1280]{1,0:T(8,128)(2,1)S(1)}, u32[]{:S(2)}, u32[]{:S(2)}) collective-permute-start(bf16[96,1280]{1,0:T(8,128)(2,1)S(1)} %get-tuple-element.19.args_0_), channel_id=1, source_target_pairs={{0,128},{128,0},{256,384},{384,256},{16,144},{144,16},{272,400},{4... | collective-permute-start | bytes 737288 | tf_op jit(solution)/shard_map/ppermute | solution.py:239
  67.0 17.3 %collective-permute-start.4 = (bf16[96,1280]{1,0:T(8,128)(2,1)S(1)}, bf16[96,1280]{1,0:T(8,128)(2,1)S(1)}, u32[]{:S(2)}, u32[]{:S(2)}) collective-permute-start(bf16[96,1280]{1,0:T(8,128)(2,1)S(1)} %collective-permute-done.args_1_), channel_id=1, source_target_pairs={{0,128},{128,0},{256,384},{384,256},{16,144},{144,16},{272,400},{4... | collective-permute-start | bytes 737288 | tf_op jit(solution)/shard_map/ppermute | solution.py:239
  73.9 20.4 %copy-start.18 = (bf16[96,1280]{1,0:T(8,128)(2,1)}, bf16[96,1280]{1,0:T(8,128)(2,1)S(1)}, u32[]{:S(2)}) copy-start(bf16[96,1280]{1,0:T(8,128)(2,1)S(1)} %collective-permute-done.2.args_3_) | copy-start | bytes 737284
  73.9 15.7 %collective-permute-start.5 = (bf16[96,1280]{1,0:T(8,128)(2,1)}, bf16[96,1280]{1,0:T(8,128)(2,1)S(1)}, u32[]{:S(2)}, u32[]{:S(2)}) collective-permute-start(bf16[96,1280]{1,0:T(8,128)(2,1)} %collective-permute-done.1.args_2_), channel_id=1, source_target_pairs={{0,128},{128,0},{256,384},{384,256},{16,144},{144,16},{272,400},{4... | collective-permute-start | bytes 737288 | tf_op jit(solution)/shard_map/ppermute | solution.py:239
  79.3 15.0 %copy-start.19 = (bf16[96,1280]{1,0:T(8,128)(2,1)}, bf16[96,1280]{1,0:T(8,128)(2,1)S(1)}, u32[]{:S(2)}) copy-start(bf16[96,1280]{1,0:T(8,128)(2,1)S(1)} %collective-permute-done.3.args_4_) | copy-start | bytes 737284
  79.4 14.9 %collective-permute-start.6 = (bf16[96,1280]{1,0:T(8,128)(2,1)S(1)}, bf16[96,1280]{1,0:T(8,128)(2,1)S(1)}, u32[]{:S(2)}, u32[]{:S(2)}) collective-permute-start(bf16[96,1280]{1,0:T(8,128)(2,1)S(1)} %collective-permute-done.2.args_3_), channel_id=1, source_target_pairs={{0,128},{128,0},{256,384},{384,256},{16,144},{144,16},{272,400},{4... | collective-permute-start | bytes 737288 | tf_op jit(solution)/shard_map/ppermute | solution.py:239
  84.3 10.0 %copy-start.20 = (bf16[96,1280]{1,0:T(8,128)(2,1)}, bf16[96,1280]{1,0:T(8,128)(2,1)S(1)}, u32[]{:S(2)}) copy-start(bf16[96,1280]{1,0:T(8,128)(2,1)S(1)} %collective-permute-done.4.args_5_) | copy-start | bytes 737284
  89.6 4.7 %copy-start.21 = (bf16[96,1280]{1,0:T(8,128)(2,1)}, bf16[96,1280]{1,0:T(8,128)(2,1)S(1)}, u32[]{:S(2)}) copy-start(bf16[96,1280]{1,0:T(8,128)(2,1)S(1)} %collective-permute-done.5.args_6_) | copy-start | bytes 737284
  94.3 0.7 copy-start.22
  95.0 0.8 copy-start.16
  108.5 17.5 %copy-start.11 = (f32[224,1280]{1,0:T(8,128)S(1)}, f32[224,1280]{1,0:T(8,128)}, u32[]{:S(2)}) copy-start(f32[224,1280]{1,0:T(8,128)} %get-tuple-element.32) | copy-start | bytes 3440644
  108.5 17.5 %collective-permute-start.15 = (bf16[224,1280]{1,0:T(8,128)(2,1)}, bf16[224,1280]{1,0:T(8,128)(2,1)}, u32[]{:S(2)}, u32[]{:S(2)}) collective-permute-start(bf16[224,1280]{1,0:T(8,128)(2,1)} %get-tuple-element.33), channel_id=1, source_target_pairs={{0,96},{32,0},{64,32},{96,64},{1,97},{33,1},{65,33},{97,65},{2,98}... | collective-permute-start | bytes 1720328 | tf_op jit(solution)/shard_map/ppermute | solution.py:218
  113.8 32.3 %collective-permute-start.14 = (bf16[224,1280]{1,0:T(8,128)(2,1)}, bf16[224,1280]{1,0:T(8,128)(2,1)S(1)}, u32[]{:S(2)}, u32[]{:S(2)}) collective-permute-start(bf16[224,1280]{1,0:T(8,128)(2,1)} %get-tuple-element.31), channel_id=1, source_target_pairs={{0,32},{32,64},{64,96},{96,0},{1,33},{33,65},{65,97},{97,1},{2,34}... | collective-permute-start | bytes 1720328 | tf_op jit(solution)/shard_map/ppermute | solution.py:218
  115.7 27.5 %collective-permute-start.12 = (bf16[224,1280]{1,0:T(8,128)(2,1)}, bf16[224,1280]{1,0:T(8,128)(2,1)S(1)}, u32[]{:S(2)}, u32[]{:S(2)}) collective-permute-start(bf16[224,1280]{1,0:T(8,128)(2,1)} %get-tuple-element.29), channel_id=1, source_target_pairs={{0,32},{32,64},{64,96},{96,0},{1,33},{33,65},{65,97},{97,1},{2,34}... | collective-permute-start | bytes 1720328 | tf_op jit(solution)/shard_map/ppermute | solution.py:218
  117.7 30.5 %all-to-all-start.1 = ((bf16[8,48,1280]{2,1,0:T(8,128)(2,1)}), bf16[8,48,1280]{2,1,0:T(8,128)(2,1)S(1)}, u32[]{:S(2)}, u32[]{:S(2)}) async-start(bf16[8,48,1280]{2,1,0:T(8,128)(2,1)} %get-tuple-element.23), calls=%async_computation.1 | async-start | bytes 1966080 | tf_op jit(solution)/shard_map/all_to_all | solution.py:226
  126.1 17.2 %copy-start.10 = (f32[224,1280]{1,0:T(8,128)S(1)}, f32[224,1280]{1,0:T(8,128)}, u32[]{:S(2)}) copy-start(f32[224,1280]{1,0:T(8,128)} %get-tuple-element.28) | copy-start | bytes 3440644
  126.1 20.0 %copy-start.13 = (bf16[1,224,1280]{2,1,0:T(8,128)(2,1)S(1)}, bf16[1,224,1280]{2,1,0:T(8,128)(2,1)}, u32[]{:S(2)}) copy-start(bf16[1,224,1280]{2,1,0:T(8,128)(2,1)} %param.18) | copy-start | bytes 1720324
  127.4 18.8 %collective-permute-start.16 = (bf16[224,1280]{1,0:T(8,128)(2,1)S(1)}, bf16[224,1280]{1,0:T(8,128)(2,1)S(1)}, u32[]{:S(2)}, u32[]{:S(2)}) collective-permute-start(bf16[224,1280]{1,0:T(8,128)(2,1)S(1)} %add_convert_fusion), channel_id=1, source_target_pairs={{0,96},{32,0},{64,32},{96,64},{1,97},{33,1},{65,33},{97,65},{2,98}... | collective-permute-start | bytes 1720328 | tf_op jit(solution)/shard_map/ppermute | solution.py:218
  133.4 22.7 %collective-permute-start.11 = (bf16[224,1280]{1,0:T(8,128)(2,1)}, bf16[224,1280]{1,0:T(8,128)(2,1)}, u32[]{:S(2)}, u32[]{:S(2)}) collective-permute-start(bf16[224,1280]{1,0:T(8,128)(2,1)} %get-tuple-element.27), channel_id=1, source_target_pairs={{0,96},{32,0},{64,32},{96,64},{1,97},{33,1},{65,33},{97,65},{2,98}... | collective-permute-start | bytes 1720328 | tf_op jit(solution)/shard_map/ppermute | solution.py:218
  143.3 2.9 %copy-start.5 = (bf16[1,224,1280]{2,1,0:T(8,128)(2,1)S(1)}, bf16[1,224,1280]{2,1,0:T(8,128)(2,1)}, u32[]{:S(2)}) copy-start(bf16[1,224,1280]{2,1,0:T(8,128)(2,1)} %param.16) | copy-start | bytes 1720324
  143.3 2.9 %copy-start.8 = (f32[224,1280]{1,0:T(8,128)S(1)}, f32[224,1280]{1,0:T(8,128)}, u32[]{:S(2)}) copy-start(f32[224,1280]{1,0:T(8,128)} %get-tuple-element.30) | copy-start | bytes 3440644
  143.3 2.9 %copy-start.12 = (bf16[1,224,1280]{2,1,0:T(8,128)(2,1)S(1)}, bf16[1,224,1280]{2,1,0:T(8,128)(2,1)}, u32[]{:S(2)}) copy-start(bf16[1,224,1280]{2,1,0:T(8,128)(2,1)} %param.20) | copy-start | bytes 1720324
  144.2 16.3 %collective-permute-start.13 = (bf16[224,1280]{1,0:T(8,128)(2,1)}, bf16[224,1280]{1,0:T(8,128)(2,1)}, u32[]{:S(2)}, u32[]{:S(2)}) collective-permute-start(bf16[224,1280]{1,0:T(8,128)(2,1)} %add_convert_fusion.1), channel_id=1, source_target_pairs={{0,32},{32,64},{64,96},{96,0},{1,33},{33,65},{65,97},{97,1},{2,34}... | collective-permute-start | bytes 1720328 | tf_op jit(solution)/shard_map/ppermute | solution.py:218
  146.2 14.4 %copy-start.14 = (bf16[1,1280,224]{1,2,0:T(8,128)(2,1)S(1)}, bf16[1,1280,224]{1,2,0:T(8,128)(2,1)}, u32[]{:S(2)}) copy-start(bf16[1,1280,224]{1,2,0:T(8,128)(2,1)} %param.19) | copy-start | bytes 1720324
  148.1 12.4 %copy-start.6 = (bf16[1,1280,224]{1,2,0:T(8,128)(2,1)S(1)}, bf16[1,1280,224]{1,2,0:T(8,128)(2,1)}, u32[]{:S(2)}) copy-start(bf16[1,1280,224]{1,2,0:T(8,128)(2,1)} %param.15) | copy-start | bytes 1720324
  148.1 12.4 %copy-start.7 = (f32[224,1280]{1,0:T(8,128)S(1)}, f32[224,1280]{1,0:T(8,128)}, u32[]{:S(2)}) copy-start(f32[224,1280]{1,0:T(8,128)} %get-tuple-element.26) | copy-start | bytes 3440644
  149.2 17.9 %all-to-all-start.2 = ((bf16[16,6,1280]{2,1,0:T(8,128)(2,1)}), bf16[16,6,1280]{2,1,0:T(8,128)(2,1)S(1)}, u32[]{:S(2)}, u32[]{:S(2)}) async-start(bf16[16,6,1280]{2,1,0:T(8,128)(2,1)} %shard_map.141), calls=%async_computation.2 | async-start | bytes 655360 | tf_op jit(solution)/shard_map/all_to_all | solution.py:222

commit v3 on v2

--- a/solution.py
+++ b/solution.py
@@ -109,15 +109,20 @@
     scaled = gate * contract(choice, back_rows[...], 1, 0)
     for i in range(SOURCES):
         here = slice(i * PADDED, i * PADDED + FROM_ONE)
-        send[i, :FROM_ONE] = picked[here].astype(jnp.bfloat16)
-        send[i, FROM_ONE:] = scaled[here].astype(jnp.bfloat16)
-
-
-def spread_kernel(place, arrived, *rest):
-    sends, (rows, halves) = rest[:4], rest[4:]
+        for n in range(2):
+            cut = slice(n * WIDTH // 2, (n + 1) * WIDTH // 2)
+            first = 2 * n * FROM_ONE
+            send[i, first : first + FROM_ONE] = picked[here, cut].astype(jnp.bfloat16)
+            send[i, first + FROM_ONE : first + 2 * FROM_ONE] = scaled[here, cut].astype(jnp.bfloat16)
+
+
+def spread_kernel(arrived, send, rows):
     rows[...] = jnp.zeros_like(rows)
     for i in range(SOURCES):
-        rows[i * 16 : i * 16 + 2 * FROM_ONE, :] = arrived[i]
+        for n in range(2):
+            cut = slice(n * WIDTH // 2, (n + 1) * WIDTH // 2)
+            part = slice(2 * n * FROM_ONE, 2 * (n + 1) * FROM_ONE)
+            rows[i * 16 : i * 16 + 2 * FROM_ONE, cut] = arrived[i, part]
     shape = (2 * CHUNK, SOURCES * 16)
     after = lax.broadcasted_iota(jnp.int32, shape, 0)
     before = lax.broadcasted_iota(jnp.int32, shape, 1)
@@ -127,9 +132,9 @@
     for half in range(2):
         order = ((before >> 4) == (after & 15)) & (slot == PICKS * half)
         ordered = contract(order.astype(jnp.bfloat16), rows[...], 1, 0)
-        halves[half] = ordered.astype(jnp.bfloat16)
-    for send, target in zip(sends, (place[0], place[1], place[2], place[3])):
-        send[...] = halves[target >> 2]
+        ordered = ordered.astype(jnp.bfloat16)
+        for z in range(4):
+            send[z * 2 + half] = ordered
 
 
 def gather_kernel(arrived, send, total):
@@ -146,59 +151,89 @@
     order = ((before & 15) == (after >> 3)) & ((after & 7) == PICKS * half + (before >> 4))
     ordered = contract(order.astype(jnp.bfloat16), total[...], 1, 0)
     for i in range(SOURCES):
-        send[i] = ordered[i * PADDED : i * PADDED + FROM_ONE].astype(jnp.bfloat16)
-
-
-def expert_kernel(place, *args):
-    blocks, (own, left, right, up_far, down_far) = args[:8], args[8:13]
-    outs, args = args[13:22], args[22:]
-    staged, (rows, grads, up, down, units, slopes, sems, out_sems) = args[:9], args[9:]
-    halves = pl.ds(0, GROUP), pl.ds(GROUP, GROUP)
-    pairs = [(b.at[pl.ds(0, CHUNK)], rows.at[pl.ds(j * CHUNK, CHUNK)]) for j, b in enumerate(blocks)]
-    pairs += [(piece.at[halves[0]], up.at[i]) for i, piece in enumerate((own, left, right), 1)]
-    pairs += [(up_far, up.at[0])]
-    pairs += [(piece.at[halves[1]], down.at[i]) for i, piece in enumerate((own, left, right), 1)]
-    pairs += [(down_far, down.at[0])]
-    pairs += [
-        (b.at[pl.ds(CHUNK, CHUNK)], grads.at[pl.ds(j * CHUNK, CHUNK)]) for j, b in enumerate(blocks)
-    ]
-    copies = [pltpu.make_async_copy(src, dst, sems.at[n]) for n, (src, dst) in enumerate(pairs)]
+        chunk = ordered[i * PADDED : i * PADDED + FROM_ONE].astype(jnp.bfloat16)
+        for n in range(5):
+            send[i, n * FROM_ONE : (n + 1) * FROM_ONE] = chunk[:, n * 256 : (n + 1) * 256]
+
+
+def start_all(pairs, sems, first=0):
+    copies = []
+    for n, (source, target) in enumerate(pairs, first):
+        copies.append(pltpu.make_async_copy(source, target, sems.at[n]))
+        copies[-1].start()
+    return copies
+
+
+def wait_all(copies):
     for copy in copies:
-        copy.start()
-    for copy in copies[:12]:
         copy.wait()
+
+
+def row_copies(arrived, half, rows):
+    cut = pl.ds(half * CHUNK, CHUNK)
+    return [(arrived.at[j, cut], rows.at[pl.ds(j * CHUNK, CHUNK)]) for j in range(COLUMN)]
+
+
+CUTS = [pl.ds(n, 256) for n in range(0, WIDTH, 256)]
+
+
+def expert_kernel(arrived, *args):
+    ups, downs, outs, staged = args[:4], args[4:8], args[8:17], args[17:26]
+    rows, grads, up, down, units, slopes, sems, out_sems = args[26:]
+    partial = 8
+    pairs = row_copies(arrived, 0, rows)
+    pairs += [(ups[i], up.at[i]) for i in range(RING)] + row_copies(arrived, 1, grads)
+    pairs += [(downs[i], down.at[i]) for i in range(RING)]
+    copies = start_all(pairs, sems)
+    wait_all(copies[:COLUMN])
     for i in range(RING):
+        copies[COLUMN + i].wait()
         pre = contract(up[i], rows[...], 1, 1)
         share = 0.5 * (1.0 + lax.erf(pre * 0.7071067811865476))
         units[i] = (pre * share).astype(jnp.bfloat16)
         slopes[i] = share + pre * (0.3989422804014327 * jnp.exp(-0.5 * pre * pre))
-    for copy in copies[12:]:
-        copy.wait()
-    cuts = [pl.ds(n, 256) for n in range(0, WIDTH, 256)]
-    writes = [pltpu.make_async_copy(s, o, out_sems.at[n]) for n, (s, o) in enumerate(zip(staged, outs))]
-    for n, i in enumerate((0, 2, 3, 1)):
+    wait_all(copies[COLUMN + RING :])
+    writes = []
+    for i in range(RING):
         back = (slopes[i] * contract(down[i], grads[...], 1, 1)).astype(jnp.bfloat16)
-        for cut in cuts:
-            for out, a, b in zip(staged[2 * n : 2 * n + 2], (back, units[i]), (rows, grads)):
-                out[:, cut] = contract(a, b[:, cut], 1, 0).astype(out.dtype)
-        writes[2 * n].start()
-        writes[2 * n + 1].start()
-    for cut in cuts:
+        here = slice(2 * i, 2 * i + 2)
+        for cut in CUTS:
+            for out, a, b in zip(staged[here], (back, units[i]), (rows, grads)):
+                out[:, cut] = contract(a, b[:, cut], 1, 0).astype(jnp.bfloat16)
+        writes += start_all(list(zip(staged[here], outs[here])), out_sems, len(writes))
+    for cut in CUTS:
         total = contract(units[0], down[0, :, cut], 0, 0)
         for i in range(1, RING):
             total = total + contract(units[i], down[i, :, cut], 0, 0)
-        for j in range(8):
-            staged[8][place[j], :, cut] = total[j * CHUNK : j * CHUNK + CHUNK].astype(jnp.bfloat16)
-    writes[8].start()
-    for write in writes:
-        write.wait()
+        for j in range(COLUMN):
+            staged[partial][j, :, cut] = total[j * CHUNK : j * CHUNK + CHUNK].astype(jnp.bfloat16)
+    wait_all(writes + start_all([(staged[partial], outs[partial])], out_sems, len(writes)))
+
+
+def step_kernel(factor, *args):
+    sources, outs, (held, staged, sems, out_sems) = args[:12], args[12:14], args[14:]
+    parts = [sources[:6], sources[6:]]
+    pairs = [(source, held.at[n, m]) for n in range(2) for m, source in enumerate(parts[n])]
+    copies = start_all(pairs, sems)
+    writes = []
+    for n in range(2):
+        wait_all(copies[6 * n : 6 * n + 6])
+        for start in range(0, GROUP, 32):
+            here = pl.ds(start, 32)
+            first_moment, second_moment, weight, own, one, two = [held[n, m, here] for m in range(6)]
+            gradient = own.astype(jnp.float32) + one.astype(jnp.float32) + two.astype(jnp.float32)
+            staged[n, here] = adam_step(gradient, first_moment, second_moment, weight, factor[0])
+        writes += start_all([(staged.at[n], outs[n])], out_sems, len(writes))
+    wait_all(writes)
 
 
 def combine_kernel(returned, cotangent, chosen, gates, combined, gate_grad, rows):
     tokens = cotangent.shape[0]
     rows[...] = jnp.zeros_like(rows)
     for i in range(SOURCES):
-        rows[i * PADDED : i * PADDED + FROM_ONE, :] = returned[i].astype(jnp.float32)
+        for n in range(5):
+            part = returned[i, n * FROM_ONE : (n + 1) * FROM_ONE].astype(jnp.float32)
+            rows[i * PADDED : i * PADDED + FROM_ONE, n * 256 : (n + 1) * 256] = part
     masks = slot_masks()
     choice = row_choice(masks, chosen, tokens)
     gate = row_values(masks, gates)
@@ -224,27 +259,6 @@
 
 def along_z(rows):
     return lax.all_to_all(rows, ("zlo", "zhi"), split_axis=0, concat_axis=0, tiled=True)
-
-
-def rank(z):
-    return z % 4 * 2 + z // 4
-
-
-def mate(z):
-    return z + 1 - 2 * (z % 2)
-
-
-def to_chip(rows, target):
-    pairs = [(rank(z), rank(target(z) % COLUMN)) for z in range(COLUMN)]
-    return lax.ppermute(rows, ("zlo", "zhi"), pairs)
-
-
-HOPS = (
-    lambda z: z + 2 - 4 * (z % 2),
-    lambda z: z - 1 + 2 * (z % 2),
-    lambda z: z - 3 + 6 * (z % 2),
-)
-ORIGINS = (lambda z: z - 2 + 4 * (z % 2), HOPS[1], HOPS[2])
 
 
 def per_device(
@@ -266,77 +280,77 @@
     down_own = down_weight[0]
     f32, bf16 = jnp.float32, jnp.bfloat16
 
-    own = jnp.concatenate([up_own, down_own])
-    left = along_x(own, 1)
-    right = along_x(own, -1)
-    up_far = along_x(left[:GROUP], 1)
-    down_far = along_x(right[GROUP:], -1)
-
-    z = (lax.axis_index("zhi") * 4 + lax.axis_index("zlo")).astype(jnp.int32)
-    first = [z] + [hop(z) % COLUMN for hop in HOPS]
-    sources = [z] + [origin(z) for origin in ORIGINS]
-    sources += [mate(z)] + [origin(mate(z)) for origin in ORIGINS]
-    slots = jnp.stack([rank(source % COLUMN) for source in sources])
+    up_left, down_left = along_x(up_own, 1), along_x(down_own, 1)
+    up_right, down_right = along_x(up_own, -1), along_x(down_own, -1)
+
     (send,) = call(
         pick_kernel,
-        [shape(SOURCES, 2 * FROM_ONE, WIDTH)],
+        [shape(SOURCES, 4 * FROM_ONE, WIDTH // 2)],
         [tokens, cotangent, chosen, gates],
         [pltpu.VMEM(tokens.shape, bf16)] * 2 + [pltpu.SemaphoreType.DMA((2,))],
+        limit=LARGE,
         outside=(0, 1),
     )
-    blocks = call(
+    (spread,) = call(
         spread_kernel,
-        [shape(2 * CHUNK, WIDTH)] * 4,
-        [jnp.stack(first), within_z(send)],
-        [pltpu.VMEM((SOURCES * 16, WIDTH), bf16), pltpu.VMEM((2, 2 * CHUNK, WIDTH), bf16)],
-    )
-    blocks = [blocks[0]] + [to_chip(block, hop) for block, hop in zip(blocks[1:], HOPS)]
-    blocks += [to_chip(block, mate) for block in blocks]
-
+        [shape(COLUMN, 2 * CHUNK, WIDTH)],
+        [within_z(send)],
+        [pltpu.VMEM((SOURCES * 16, WIDTH), bf16)],
+    )
+    rows = along_z(spread)
+
+    ups = [along_x(up_left, 1), up_left, up_right, up_own]
+    downs = [along_x(down_right, -1), down_left, down_right, down_own]
     weight = shape(GROUP, WIDTH)
-    wide = shape(GROUP, WIDTH, dtype=f32)
-    gradients = [weight, weight, weight, wide, wide, weight, wide, wide]
-    results = [*gradients, shape(COLUMN, CHUNK, WIDTH)]
-    outputs = call(
+    results = [weight] * 8 + [shape(COLUMN, CHUNK, WIDTH)]
+    *gradients, partial = call(
         expert_kernel,
         results,
-        [slots, *blocks, own, left, right, up_far, down_far],
+        [rows, *ups, *downs],
         [pltpu.VMEM(r.shape, r.dtype) for r in results]
         + [pltpu.VMEM((ROWS, WIDTH), bf16)] * 2
         + [pltpu.VMEM((RING, GROUP, WIDTH), bf16)] * 2
         + [pltpu.VMEM((RING, GROUP, ROWS), dtype) for dtype in (bf16, f32)]
-        + [pltpu.SemaphoreType.DMA((24,)), pltpu.SemaphoreType.DMA((9,))],
+        + [pltpu.SemaphoreType.DMA((2 * COLUMN + 2 * RING,))]
+        + [pltpu.SemaphoreType.DMA((2 * RING + 1,))],
         flops=40 * ROWS * GROUP * WIDTH,
         limit=LARGE,
-        outside=range(1, 14),
+        outside=range(9),
         outputs_outside=True,
     )
-    far_up, far_down, left_up, left_down, right_up, right_down, own_up, own_down, partial = outputs
     arrived = along_z(partial)
-
-    up_two = along_x(far_up, 1).astype(f32)
-    down_two = along_x(far_down, -1).astype(f32)
-    up_from_right = along_x(left_up, -1).astype(f32)
-    down_from_left = along_x(right_down, 1).astype(f32)
-    up_from_left = along_x((right_up + up_two).astype(jnp.bfloat16), 1).astype(f32)
-    down_from_right = along_x((left_down + down_two).astype(jnp.bfloat16), -1).astype(f32)
-    total_up = own_up + up_from_right + up_from_left
-    total_down = own_down + down_from_left + down_from_right
-
-    exponent = (LAYERS - 1 - layer_index[0]).astype(f32)
+    far_up, far_down, left_up, left_down, right_up, right_down, own_up, own_down = gradients
+    up_two, down_two = lax.optimization_barrier((along_x(far_up, 1), along_x(far_down, -1)))
+    up_one = along_x(left_up, -1)
+    down_one = along_x(right_down, 1)
+    up_sum = along_x((right_up.astype(f32) + up_two.astype(f32)).astype(bf16), 1)
+    down_sum = along_x((left_down.astype(f32) + down_two.astype(f32)).astype(bf16), -1)
+    exponent = (LAYERS - 1 - layer_index).astype(f32)
     factor = jnp.power(f32(DECAY_RATE), exponent)
-    step_up = adam_step(total_up, first_up[0].T, second_up[0].T, up_own, factor).T[None]
-    step_down = adam_step(total_down, first_down[0], second_down[0], down_own, factor)[None]
+    step_up, step_down = call(
+        step_kernel,
+        [weight, weight],
+        [
+            factor,
+            *(first_up[0].T, second_up[0].T, up_own, own_up, up_one, up_sum),
+            *(first_down[0], second_down[0], down_own, own_down, down_one, down_sum),
+        ],
+        [pltpu.VMEM((2, 6, GROUP, WIDTH), bf16), pltpu.VMEM((2, GROUP, WIDTH), bf16)]
+        + [pltpu.SemaphoreType.DMA((12,)), pltpu.SemaphoreType.DMA((2,))],
+        limit=LARGE,
+        outside=range(1, 13),
+        outputs_outside=True,
+    )
 
     scratch = [pltpu.VMEM((2 * CHUNK, WIDTH), bf16)]
-    (summed,) = call(gather_kernel, [shape(SOURCES, FROM_ONE, WIDTH)], [arrived], scratch)
+    (summed,) = call(gather_kernel, [shape(SOURCES, 5 * FROM_ONE, 256)], [arrived], scratch)
     combined, gate_grad = call(
         combine_kernel,
         [shape(tokens.shape[0], WIDTH), shape(PICKS, 1, EXPERTS, dtype=f32)],
         [within_z(summed), cotangent, chosen, gates],
         [pltpu.VMEM((SOURCES * PADDED, WIDTH), f32)],
     )
-    return (combined, gate_grad.transpose(1, 2, 0), step_up, step_down)
+    return (combined, gate_grad.transpose(1, 2, 0), step_up.T[None], step_down[None])
 
 
 def solution(mesh):

time: 169 us -> 153 us (0.905)
  blocking collectives: 0 us -> 26.9 us
  starting transfers between devices: 82.8 us -> 57.4 us
  waiting for transfers between devices: 53.2 us -> 40.5 us
  other arithmetic: 8.9 us -> 0.27 us
  Pallas kernels: 18 us -> 22.4 us
    ppermute x7 -> x0, starting transfers between devices: 32.3 us -> none  [to_chip(): return lax.ppermute(rows, ('zlo', 'zhi'), pairs)]
    all_to_all x0 -> x1, blocking collectives: none -> 26.9 us  [within_z(): lax.all_to_all(rows, ('y', 'core'), split_axis=0, concat_axis=0, tiled=True)]
    all_to_all x2 -> x1, waiting for transfers between devices: 23.2 us -> 2.79 us  [within_z(): lax.all_to_all(rows, ('y', 'core'), split_axis=0, concat_axis=0, tiled=True)]
    ppermute x7 -> x0, waiting for transfers between devices: 11.7 us -> none  [to_chip(): return lax.ppermute(rows, ('zlo', 'zhi'), pairs)]
    ppermute x10 -> x12, waiting for transfers between devices: 18.4 us -> 28.1 us  [along_x(): lax.ppermute(values, 'x', [(i, (i + step) % RING) for i in range(RING)])]
    all_to_all x1 -> x2, waiting for transfers between devices: 0.01 us -> 9.54 us  [along_z(): lax.all_to_all(rows, ('zlo', 'zhi'), split_axis=0, concat_axis=0, tiled=T...]
    all_to_all x1 -> x2, starting transfers between devices: 4.47 us -> 14 us  [along_z(): lax.all_to_all(rows, ('zlo', 'zhi'), split_axis=0, concat_axis=0, tiled=T...]
    all_to_all x2 -> x1, starting transfers between devices: 13.9 us -> 5.41 us  [within_z(): lax.all_to_all(rows, ('y', 'core'), split_axis=0, concat_axis=0, tiled=True)]
  transfers between devices with their start and end apart: 20 -> 15, of which waited for: 10 -> 9; matrix products, arithmetic and copies ran while one was open for 6% -> 0% of each run, Pallas kernels for 2% -> 4%
where the time goes in v3:
time: 153 us; the launch traced here: 152 us
  starting transfers between devices  57.4 us (38%)
  waiting for transfers between devices  40.5 us (26%)
  blocking collectives  26.9 us (18%)
  Pallas kernels  22.4 us (15%)
  local copies, waits for them, and re-layouts  3.13 us (2%)
  between operations  1.56 us (1%)
    ppermute x12, starting transfers between devices, along_x(): lax.ppermute(values, 'x', [(i, (i + step) % RING) for i in range(RING)])  38 us
    ppermute x12, waiting for transfers between devices, along_x(): lax.ppermute(values, 'x', [(i, (i + step) % RING) for i in range(RING)])  28.1 us
    all_to_all x1, blocking collectives, within_z(): lax.all_to_all(rows, ('y', 'core'), split_axis=0, concat_axis=0, tiled=True)  26.9 us
    pallas_call x6, Pallas kernels, call(): pl.pallas_call(kernel, out_shape=shapes, in_specs=[scalar if a.ndim == 1...  22.4 us
    all_to_all x2, starting transfers between devices, along_z(): lax.all_to_all(rows, ('zlo', 'zhi'), split_axis=0, concat_axis=0, tiled=T...  14 us
    all_to_all x2, waiting for transfers between devices, along_z(): lax.all_to_all(rows, ('zlo', 'zhi'), split_axis=0, concat_axis=0, tiled=T...  9.54 us
    all_to_all x1, starting transfers between devices, within_z(): lax.all_to_all(rows, ('y', 'core'), split_axis=0, concat_axis=0, tiled=True)  5.41 us
    unnamed x30, local copies, waits for them, and re-layouts  3.13 us
  transfers between devices with their start and end apart: 15, of which 9 were waited for; matrix products, arithmetic and copies ran while one was open for 0% of the time, Pallas kernels for 4%

profile of v3, /device:TPU:1, one launch (start us, length us, event | category | flops | bytes accessed | tf_op | source)
XLA Modules:
  0.0 152.1 jit_solution(1650378901401288586)
XLA Ops:
  0.6 2.9 %shard_map.138 = bf16[16,24,640]{2,1,0:T(8,128)(2,1)} custom-call(bf16[48,1280]{1,0:T(8,128)(2,1)} %tokens.1, bf16[48,1280]{1,0:T(8,128)(2,1)} %cotangent.3, s32[3,1,32]{2,1,0:T(1,128)} %bitcast.19, f32[3,1,32]{2,1,0:T(1,128)} %bitcast.21), custom_call_target="tpu_custom_call" | custom-call | bytes 738048 | tf_op jit(solution)/shard_map/pallas_call | solution.py:58
  3.5 26.9 %all_to_all.20.arrived = bf16[16,24,640]{2,1,0:T(8,128)(2,1)S(1)} all-to-all(bf16[16,24,640]{2,1,0:T(8,128)(2,1)} %shard_map.138), channel_id=1, replica_groups=mesh['zlo'=4,'x'=4,'zhi'=2,'y'=8,'core'=2] {'y','core'}, dimensions={0} | all-to-all | bytes 983040 | tf_op jit(solution)/shard_map/all_to_all | solution.py:257
  30.4 1.7 %shard_map.139 = bf16[8,96,1280]{2,1,0:T(8,128)(2,1)} custom-call(bf16[16,24,640]{2,1,0:T(8,128)(2,1)S(1)} %all_to_all.20.arrived), custom_call_target="tpu_custom_call" | custom-call | bytes 2457600 | tf_op jit(solution)/shard_map/pallas_call | solution.py:58
  32.1 0.0 copy-start.6
  32.1 0.0 copy-start.7
  32.1 8.5 %all-to-all-start.1 = ((bf16[8,96,1280]{2,1,0:T(8,128)(2,1)}), bf16[8,96,1280]{2,1,0:T(8,128)(2,1)S(1)}, u32[]{:S(2)}, u32[]{:S(2)}) async-start(bf16[8,96,1280]{2,1,0:T(8,128)(2,1)} %shard_map.139), calls=%async_computation.1 | async-start | bytes 3932160 | tf_op jit(solution)/shard_map/all_to_all | solution.py:261
  40.6 0.0 copy-done.6
  40.7 3.1 %collective-permute-start = (bf16[224,1280]{1,0:T(8,128)(2,1)S(1)}, bf16[224,1280]{1,0:T(8,128)(2,1)S(1)}, u32[]{:S(2)}, u32[]{:S(2)}) collective-permute-start(bf16[224,1280]{1,0:T(8,128)(2,1)S(1)} %bitcast.25), channel_id=1, source_target_pairs={{0,32},{32,64},{64,96},{96,0},{1,33},{33,65},{65,97},{97,1},{2,34}... | collective-permute-start | bytes 1720328 | tf_op jit(solution)/shard_map/ppermute | solution.py:253
  43.8 0.0 copy-done.7
  43.8 3.4 %collective-permute-start.3 = (bf16[224,1280]{1,0:T(8,128)(2,1)S(1)}, bf16[224,1280]{1,0:T(8,128)(2,1)S(1)}, u32[]{:S(2)}, u32[]{:S(2)}) collective-permute-start(bf16[224,1280]{1,0:T(8,128)(2,1)S(1)} %bitcast.29), channel_id=1, source_target_pairs={{0,96},{32,0},{64,32},{96,64},{1,97},{33,1},{65,33},{97,65},{2,98}... | collective-permute-start | bytes 1720328 | tf_op jit(solution)/shard_map/ppermute | solution.py:253
  47.2 3.2 %collective-permute-start.2 = (bf16[224,1280]{1,0:T(8,128)(2,1)S(1)}, bf16[224,1280]{1,0:T(8,128)(2,1)S(1)}, u32[]{:S(2)}, u32[]{:S(2)}) collective-permute-start(bf16[224,1280]{1,0:T(8,128)(2,1)S(1)} %bitcast.26), channel_id=1, source_target_pairs={{0,96},{32,0},{64,32},{96,64},{1,97},{33,1},{65,33},{97,65},{2,98}... | collective-permute-start | bytes 1720328 | tf_op jit(solution)/shard_map/ppermute | solution.py:253
  50.4 2.1 %collective-permute-start.5 = (bf16[224,1280]{1,0:T(8,128)(2,1)S(1)}, bf16[224,1280]{1,0:T(8,128)(2,1)S(1)}, u32[]{:S(2)}, u32[]{:S(2)}) collective-permute-start(bf16[224,1280]{1,0:T(8,128)(2,1)S(1)} %bitcast.30), channel_id=1, source_target_pairs={{0,32},{32,64},{64,96},{96,0},{1,33},{33,65},{65,97},{97,1},{2,34}... | collective-permute-start | bytes 1720328 | tf_op jit(solution)/shard_map/ppermute | solution.py:253
  52.5 6.3 %collective-permute-done.args_1_ = bf16[224,1280]{1,0:T(8,128)(2,1)S(1)} collective-permute-done((bf16[224,1280]{1,0:T(8,128)(2,1)S(1)}, bf16[224,1280]{1,0:T(8,128)(2,1)S(1)}, u32[]{:S(2)}, u32[]{:S(2)}) %collective-permute-start) | collective-permute-done | bytes 573472 | tf_op jit(solution)/shard_map/ppermute | solution.py:253
  58.8 0.0 copy-start.10
  58.8 1.9 %collective-permute-start.1 = (bf16[224,1280]{1,0:T(8,128)(2,1)S(1)}, bf16[224,1280]{1,0:T(8,128)(2,1)S(1)}, u32[]{:S(2)}, u32[]{:S(2)}) collective-permute-start(bf16[224,1280]{1,0:T(8,128)(2,1)S(1)} %collective-permute-done.args_1_), channel_id=1, source_target_pairs={{0,32},{32,64},{64,96},{96,0},{1,33},{33,65},{65,97},{97,1},{2,34}... | collective-permute-start | bytes 1720328 | tf_op jit(solution)/shard_map/ppermute | solution.py:253
  60.7 0.0 collective-permute-done.3.args_6_
  60.7 0.0 copy-start.11
  60.7 4.6 %collective-permute-start.4 = (bf16[224,1280]{1,0:T(8,128)(2,1)S(1)}, bf16[224,1280]{1,0:T(8,128)(2,1)}, u32[]{:S(2)}, u32[]{:S(2)}) collective-permute-start(bf16[224,1280]{1,0:T(8,128)(2,1)S(1)} %collective-permute-done.3.args_6_), channel_id=1, source_target_pairs={{0,96},{32,0},{64,32},{96,64},{1,97},{33,1},{65,33},{97,65},{2,98}... | collective-permute-start | bytes 1720328 | tf_op jit(solution)/shard_map/ppermute | solution.py:253
  65.3 7.8 %collective-permute-done.2.args_2_ = bf16[224,1280]{1,0:T(8,128)(2,1)S(1)} collective-permute-done((bf16[224,1280]{1,0:T(8,128)(2,1)S(1)}, bf16[224,1280]{1,0:T(8,128)(2,1)S(1)}, u32[]{:S(2)}, u32[]{:S(2)}) %collective-permute-start.2) | collective-permute-done | bytes 573472 | tf_op jit(solution)/shard_map/ppermute | solution.py:253
  73.1 0.0 copy-start.12
  73.1 0.0 collective-permute-done.5.args_5_
  73.1 9.9 %collective-permute-done.1.args_0_ = bf16[224,1280]{1,0:T(8,128)(2,1)S(1)} collective-permute-done((bf16[224,1280]{1,0:T(8,128)(2,1)S(1)}, bf16[224,1280]{1,0:T(8,128)(2,1)S(1)}, u32[]{:S(2)}, u32[]{:S(2)}) %collective-permute-start.1) | collective-permute-done | bytes 573472 | tf_op jit(solution)/shard_map/ppermute | solution.py:253
  83.0 0.0 copy-done.10
  83.0 0.0 copy-done.11
  83.0 0.0 copy-done.12
  83.0 0.0 copy-done.13
  83.0 0.0 copy-start.14
  83.0 0.8 copy-done.14
  83.8 1.4 collective-permute-done.4.args_4_
  85.2 1.1 all-to-all-done.1.arrived
  86.4 0.0 copy-start.3
  86.4 1.3 copy-done.3
  87.6 10.2 %shard_map.140 = (bf16[224,1280]{1,0:T(8,128)(2,1)}, bf16[224,1280]{1,0:T(8,128)(2,1)}, bf16[224,1280]{1,0:T(8,128)(2,1)}, bf16[224,1280]{1,0:T(8,128)(2,1)}, bf...) custom-call(bf16[8,96,1280]{2,1,0:T(8,128)(2,1)} %copy-done.3, ...), custom_call_target="tpu_custom_call" | custom-call | flops 4404019200 | bytes 12124160 | tf_op jit(solution)/shard_map/pallas_call | solution.py:58
  97.9 0.0 copy-start.5
  97.9 3.2 %collective-permute-start.7 = (bf16[224,1280]{1,0:T(8,128)(2,1)}, bf16[224,1280]{1,0:T(8,128)(2,1)S(1)}, u32[]{:S(2)}, u32[]{:S(2)}) collective-permute-start(bf16[224,1280]{1,0:T(8,128)(2,1)} %get-tuple-element.25), channel_id=1, source_target_pairs={{0,32},{32,64},{64,96},{96,0},{1,33},{33,65},{65,97},{97,1},{2,34}... | collective-permute-start | bytes 1720328 | tf_op jit(solution)/shard_map/ppermute | solution.py:253
  101.2 3.4 %collective-permute-start.8 = (bf16[224,1280]{1,0:T(8,128)(2,1)}, bf16[224,1280]{1,0:T(8,128)(2,1)S(1)}, u32[]{:S(2)}, u32[]{:S(2)}) collective-permute-start(bf16[224,1280]{1,0:T(8,128)(2,1)} %get-tuple-element.26), channel_id=1, source_target_pairs={{0,96},{32,0},{64,32},{96,64},{1,97},{33,1},{65,33},{97,65},{2,98}... | collective-permute-start | bytes 1720328 | tf_op jit(solution)/shard_map/ppermute | solution.py:253
  104.5 5.4 %all-to-all-start.2 = ((bf16[8,48,1280]{2,1,0:T(8,128)(2,1)}), bf16[8,48,1280]{2,1,0:T(8,128)(2,1)S(1)}, u32[]{:S(2)}, u32[]{:S(2)}) async-start(bf16[8,48,1280]{2,1,0:T(8,128)(2,1)} %get-tuple-element.19), calls=%async_computation.2 | async-start | bytes 1966080 | tf_op jit(solution)/shard_map/all_to_all | solution.py:261
  110.0 0.0 copy-start.4
  110.0 2.1 %collective-permute-start.10 = (bf16[224,1280]{1,0:T(8,128)(2,1)}, bf16[224,1280]{1,0:T(8,128)(2,1)}, u32[]{:S(2)}, u32[]{:S(2)}) collective-permute-start(bf16[224,1280]{1,0:T(8,128)(2,1)} %get-tuple-element.29), channel_id=1, source_target_pairs={{0,32},{32,64},{64,96},{96,0},{1,33},{33,65},{65,97},{97,1},{2,34}... | collective-permute-start | bytes 1720328 | tf_op jit(solution)/shard_map/ppermute | solution.py:253
  112.1 4.6 %collective-permute-start.6 = (bf16[224,1280]{1,0:T(8,128)(2,1)}, bf16[224,1280]{1,0:T(8,128)(2,1)}, u32[]{:S(2)}, u32[]{:S(2)}) collective-permute-start(bf16[224,1280]{1,0:T(8,128)(2,1)} %get-tuple-element.23), channel_id=1, source_target_pairs={{0,96},{32,0},{64,32},{96,64},{1,97},{33,1},{65,33},{97,65},{2,98}... | collective-permute-start | bytes 1720328 | tf_op jit(solution)/shard_map/ppermute | solution.py:253
  116.6 0.0 collective-permute-done.7
  116.6 0.5 collective-permute-done.8
  117.2 0.0 copy-done.5
  117.2 0.1 add_convert_fusion
  117.3 4.6 %collective-permute-start.11 = (bf16[224,1280]{1,0:T(8,128)(2,1)S(1)}, bf16[224,1280]{1,0:T(8,128)(2,1)S(1)}, u32[]{:S(2)}, u32[]{:S(2)}) collective-permute-start(bf16[224,1280]{1,0:T(8,128)(2,1)S(1)} %add_convert_fusion), channel_id=1, source_target_pairs={{0,96},{32,0},{64,32},{96,64},{1,97},{33,1},{65,33},{97,65},{2,98}... | collective-permute-start | bytes 1720328 | tf_op jit(solution)/shard_map/ppermute | solution.py:253
  121.9 0.0 copy-done.4
  121.9 0.1 add_convert_fusion.1
  122.0 1.9 %collective-permute-start.9 = (bf16[224,1280]{1,0:T(8,128)(2,1)S(1)}, bf16[224,1280]{1,0:T(8,128)(2,1)S(1)}, u32[]{:S(2)}, u32[]{:S(2)}) collective-permute-start(bf16[224,1280]{1,0:T(8,128)(2,1)S(1)} %add_convert_fusion.1), channel_id=1, source_target_pairs={{0,32},{32,64},{64,96},{96,0},{1,33},{33,65},{65,97},{97,1},{2,34}... | collective-permute-start | bytes 1720328 | tf_op jit(solution)/shard_map/ppermute | solution.py:253
  124.0 8.4 %all-to-all-done.2.arrived = bf16[8,48,1280]{2,1,0:T(8,128)(2,1)S(1)} async-done(((bf16[8,48,1280]{2,1,0:T(8,128)(2,1)}), bf16[8,48,1280]{2,1,0:T(8,128)(2,1)S(1)}, u32[]{:S(2)}, u32[]{:S(2)}) %all-to-all-start.2) | async-done | bytes 983072 | tf_op jit(solution)/shard_map/all_to_all | solution.py:261
  132.4 1.0 shard_map.141
  133.4 5.4 %all-to-all-start.3 = ((bf16[16,30,256]{2,1,0:T(8,128)(2,1)}), bf16[16,30,256]{2,1,0:T(8,128)(2,1)S(1)}, u32[]{:S(2)}, u32[]{:S(2)}) async-start(bf16[16,30,256]{2,1,0:T(8,128)(2,1)} %shard_map.141), calls=%async_computation.3 | async-start | bytes 524288 | tf_op jit(solution)/shard_map/all_to_all | solution.py:257
  139.5 0.0 collective-permute-done.10.args_10_
  139.5 0.0 collective-permute-done.6.args_4_
  139.6 2.2 %collective-permute-done.11.args_11_ = bf16[224,1280]{1,0:T(8,128)(2,1)S(1)} collective-permute-done((bf16[224,1280]{1,0:T(8,128)(2,1)S(1)}, bf16[224,1280]{1,0:T(8,128)(2,1)S(1)}, u32[]{:S(2)}, u32[]{:S(2)}) %collective-permute-start.11) | collective-permute-done | bytes 573472 | tf_op jit(solution)/shard_map/ppermute | solution.py:253
  141.7 0.0 copy-start.8
  141.7 0.0 collective-permute-done.9.args_5_
  141.7 0.8 copy-done.8
  142.6 0.2 copy-done.9
  142.7 5.2 %shard_map.143 = (bf16[224,1280]{1,0:T(8,128)(2,1)}, bf16[224,1280]{1,0:T(8,128)(2,1)}) custom-call(f32[1]{0:T(128)S(6)} %pow.3.factor, bf16[224,1280]{1,0:T(8,128)(2,1)} %bitcast.31, bf16[224,1280]{1,0:T(8,128)(2,1)} %bitcast.32, bf16[224,1280]{1,0:T(8,128)(2,1)} %bitcast.24, bf16[224,1280]{1,0:T(8,128)(2,1)} %get-tuple-element.22.args_3_, ...), custom_call_target="tpu_custom_call" | custom-call | bytes 8028164 | tf_op jit(solution)/shard_map/pallas_call | solution.py:58
  147.9 2.8 %all-to-all-done.3.returned = bf16[16,30,256]{2,1,0:T(8,128)(2,1)S(1)} async-done(((bf16[16,30,256]{2,1,0:T(8,128)(2,1)}), bf16[16,30,256]{2,1,0:T(8,128)(2,1)S(1)}, u32[]{:S(2)}, u32[]{:S(2)}) %all-to-all-start.3) | async-done | bytes 245792 | tf_op jit(solution)/shard_map/all_to_all | solution.py:257
  150.7 0.0 copy-done
  150.7 0.0 copy-done.1
  150.7 0.0 copy-done.2
  150.7 1.4 shard_map.142
  (5 shorter events, 0.0 us)
Async XLA Ops:
  32.1 8.5 %copy-start.6 = (bf16[1,1280,224]{1,2,0:T(8,128)(2,1)S(1)}, bf16[1,1280,224]{1,2,0:T(8,128)(2,1)}, u32[]{:S(2)}) copy-start(bf16[1,1280,224]{1,2,0:T(8,128)(2,1)} %param.15) | copy-start | bytes 1720324
  32.1 11.7 %copy-start.7 = (bf16[1,224,1280]{2,1,0:T(8,128)(2,1)S(1)}, bf16[1,224,1280]{2,1,0:T(8,128)(2,1)}, u32[]{:S(2)}) copy-start(bf16[1,224,1280]{2,1,0:T(8,128)(2,1)} %param.16) | copy-start | bytes 1720324
  32.1 54.2 %all-to-all-start.1 = ((bf16[8,96,1280]{2,1,0:T(8,128)(2,1)}), bf16[8,96,1280]{2,1,0:T(8,128)(2,1)S(1)}, u32[]{:S(2)}, u32[]{:S(2)}) async-start(bf16[8,96,1280]{2,1,0:T(8,128)(2,1)} %shard_map.139), calls=%async_computation.1 | async-start | bytes 3932160 | tf_op jit(solution)/shard_map/all_to_all | solution.py:261
  40.7 18.1 %collective-permute-start = (bf16[224,1280]{1,0:T(8,128)(2,1)S(1)}, bf16[224,1280]{1,0:T(8,128)(2,1)S(1)}, u32[]{:S(2)}, u32[]{:S(2)}) collective-permute-start(bf16[224,1280]{1,0:T(8,128)(2,1)S(1)} %bitcast.25), channel_id=1, source_target_pairs={{0,32},{32,64},{64,96},{96,0},{1,33},{33,65},{65,97},{97,1},{2,34}... | collective-permute-start | bytes 1720328 | tf_op jit(solution)/shard_map/ppermute | solution.py:253
  43.8 16.9 %collective-permute-start.3 = (bf16[224,1280]{1,0:T(8,128)(2,1)S(1)}, bf16[224,1280]{1,0:T(8,128)(2,1)S(1)}, u32[]{:S(2)}, u32[]{:S(2)}) collective-permute-start(bf16[224,1280]{1,0:T(8,128)(2,1)S(1)} %bitcast.29), channel_id=1, source_target_pairs={{0,96},{32,0},{64,32},{96,64},{1,97},{33,1},{65,33},{97,65},{2,98}... | collective-permute-start | bytes 1720328 | tf_op jit(solution)/shard_map/ppermute | solution.py:253
  47.2 25.9 %collective-permute-start.2 = (bf16[224,1280]{1,0:T(8,128)(2,1)S(1)}, bf16[224,1280]{1,0:T(8,128)(2,1)S(1)}, u32[]{:S(2)}, u32[]{:S(2)}) collective-permute-start(bf16[224,1280]{1,0:T(8,128)(2,1)S(1)} %bitcast.26), channel_id=1, source_target_pairs={{0,96},{32,0},{64,32},{96,64},{1,97},{33,1},{65,33},{97,65},{2,98}... | collective-permute-start | bytes 1720328 | tf_op jit(solution)/shard_map/ppermute | solution.py:253
  50.4 22.7 %collective-permute-start.5 = (bf16[224,1280]{1,0:T(8,128)(2,1)S(1)}, bf16[224,1280]{1,0:T(8,128)(2,1)S(1)}, u32[]{:S(2)}, u32[]{:S(2)}) collective-permute-start(bf16[224,1280]{1,0:T(8,128)(2,1)S(1)} %bitcast.30), channel_id=1, source_target_pairs={{0,32},{32,64},{64,96},{96,0},{1,33},{33,65},{65,97},{97,1},{2,34}... | collective-permute-start | bytes 1720328 | tf_op jit(solution)/shard_map/ppermute | solution.py:253
  58.8 24.2 %copy-start.10 = (bf16[224,1280]{1,0:T(8,128)(2,1)}, bf16[224,1280]{1,0:T(8,128)(2,1)S(1)}, u32[]{:S(2)}) copy-start(bf16[224,1280]{1,0:T(8,128)(2,1)S(1)} %collective-permute-done.args_1_) | copy-start | bytes 1720324
  58.8 24.2 %collective-permute-start.1 = (bf16[224,1280]{1,0:T(8,128)(2,1)S(1)}, bf16[224,1280]{1,0:T(8,128)(2,1)S(1)}, u32[]{:S(2)}, u32[]{:S(2)}) collective-permute-start(bf16[224,1280]{1,0:T(8,128)(2,1)S(1)} %collective-permute-done.args_1_), channel_id=1, source_target_pairs={{0,32},{32,64},{64,96},{96,0},{1,33},{33,65},{65,97},{97,1},{2,34}... | collective-permute-start | bytes 1720328 | tf_op jit(solution)/shard_map/ppermute | solution.py:253
  60.7 22.3 %copy-start.11 = (bf16[224,1280]{1,0:T(8,128)(2,1)}, bf16[224,1280]{1,0:T(8,128)(2,1)S(1)}, u32[]{:S(2)}) copy-start(bf16[224,1280]{1,0:T(8,128)(2,1)S(1)} %collective-permute-done.3.args_6_) | copy-start | bytes 1720324
  60.7 24.5 %collective-permute-start.4 = (bf16[224,1280]{1,0:T(8,128)(2,1)S(1)}, bf16[224,1280]{1,0:T(8,128)(2,1)}, u32[]{:S(2)}, u32[]{:S(2)}) collective-permute-start(bf16[224,1280]{1,0:T(8,128)(2,1)S(1)} %collective-permute-done.3.args_6_), channel_id=1, source_target_pairs={{0,96},{32,0},{64,32},{96,64},{1,97},{33,1},{65,33},{97,65},{2,98}... | collective-permute-start | bytes 1720328 | tf_op jit(solution)/shard_map/ppermute | solution.py:253
  73.1 9.9 %copy-start.12 = (bf16[224,1280]{1,0:T(8,128)(2,1)}, bf16[224,1280]{1,0:T(8,128)(2,1)S(1)}, u32[]{:S(2)}) copy-start(bf16[224,1280]{1,0:T(8,128)(2,1)S(1)} %collective-permute-done.2.args_2_) | copy-start | bytes 1720324
  73.1 9.9 %copy-start.13 = (bf16[224,1280]{1,0:T(8,128)(2,1)}, bf16[224,1280]{1,0:T(8,128)(2,1)S(1)}, u32[]{:S(2)}) copy-start(bf16[224,1280]{1,0:T(8,128)(2,1)S(1)} %collective-permute-done.5.args_5_) | copy-start | bytes 1720324
  83.0 0.8 copy-start.14
  86.4 1.3 copy-start.3
  97.9 19.3 %copy-start.5 = (bf16[224,1280]{1,0:T(8,128)(2,1)S(1)}, bf16[224,1280]{1,0:T(8,128)(2,1)}, u32[]{:S(2)}) copy-start(bf16[224,1280]{1,0:T(8,128)(2,1)} %get-tuple-element.30) | copy-start | bytes 1720324
  97.9 18.7 %collective-permute-start.7 = (bf16[224,1280]{1,0:T(8,128)(2,1)}, bf16[224,1280]{1,0:T(8,128)(2,1)S(1)}, u32[]{:S(2)}, u32[]{:S(2)}) collective-permute-start(bf16[224,1280]{1,0:T(8,128)(2,1)} %get-tuple-element.25), channel_id=1, source_target_pairs={{0,32},{32,64},{64,96},{96,0},{1,33},{33,65},{65,97},{97,1},{2,34}... | collective-permute-start | bytes 1720328 | tf_op jit(solution)/shard_map/ppermute | solution.py:253
  101.2 16.0 %collective-permute-start.8 = (bf16[224,1280]{1,0:T(8,128)(2,1)}, bf16[224,1280]{1,0:T(8,128)(2,1)S(1)}, u32[]{:S(2)}, u32[]{:S(2)}) collective-permute-start(bf16[224,1280]{1,0:T(8,128)(2,1)} %get-tuple-element.26), channel_id=1, source_target_pairs={{0,96},{32,0},{64,32},{96,64},{1,97},{33,1},{65,33},{97,65},{2,98}... | collective-permute-start | bytes 1720328 | tf_op jit(solution)/shard_map/ppermute | solution.py:253
  104.5 27.9 %all-to-all-start.2 = ((bf16[8,48,1280]{2,1,0:T(8,128)(2,1)}), bf16[8,48,1280]{2,1,0:T(8,128)(2,1)S(1)}, u32[]{:S(2)}, u32[]{:S(2)}) async-start(bf16[8,48,1280]{2,1,0:T(8,128)(2,1)} %get-tuple-element.19), calls=%async_computation.2 | async-start | bytes 1966080 | tf_op jit(solution)/shard_map/all_to_all | solution.py:261
  110.0 11.9 %copy-start.4 = (bf16[224,1280]{1,0:T(8,128)(2,1)S(1)}, bf16[224,1280]{1,0:T(8,128)(2,1)}, u32[]{:S(2)}) copy-start(bf16[224,1280]{1,0:T(8,128)(2,1)} %get-tuple-element.24) | copy-start | bytes 1720324
  110.0 29.5 %collective-permute-start.10 = (bf16[224,1280]{1,0:T(8,128)(2,1)}, bf16[224,1280]{1,0:T(8,128)(2,1)}, u32[]{:S(2)}, u32[]{:S(2)}) collective-permute-start(bf16[224,1280]{1,0:T(8,128)(2,1)} %get-tuple-element.29), channel_id=1, source_target_pairs={{0,32},{32,64},{64,96},{96,0},{1,33},{33,65},{65,97},{97,1},{2,34}... | collective-permute-start | bytes 1720328 | tf_op jit(solution)/shard_map/ppermute | solution.py:253
  112.1 27.5 %collective-permute-start.6 = (bf16[224,1280]{1,0:T(8,128)(2,1)}, bf16[224,1280]{1,0:T(8,128)(2,1)}, u32[]{:S(2)}, u32[]{:S(2)}) collective-permute-start(bf16[224,1280]{1,0:T(8,128)(2,1)} %get-tuple-element.23), channel_id=1, source_target_pairs={{0,96},{32,0},{64,32},{96,64},{1,97},{33,1},{65,33},{97,65},{2,98}... | collective-permute-start | bytes 1720328 | tf_op jit(solution)/shard_map/ppermute | solution.py:253
  117.3 24.4 %collective-permute-start.11 = (bf16[224,1280]{1,0:T(8,128)(2,1)S(1)}, bf16[224,1280]{1,0:T(8,128)(2,1)S(1)}, u32[]{:S(2)}, u32[]{:S(2)}) collective-permute-start(bf16[224,1280]{1,0:T(8,128)(2,1)S(1)} %add_convert_fusion), channel_id=1, source_target_pairs={{0,96},{32,0},{64,32},{96,64},{1,97},{33,1},{65,33},{97,65},{2,98}... | collective-permute-start | bytes 1720328 | tf_op jit(solution)/shard_map/ppermute | solution.py:253
  122.0 19.7 %collective-permute-start.9 = (bf16[224,1280]{1,0:T(8,128)(2,1)S(1)}, bf16[224,1280]{1,0:T(8,128)(2,1)S(1)}, u32[]{:S(2)}, u32[]{:S(2)}) collective-permute-start(bf16[224,1280]{1,0:T(8,128)(2,1)S(1)} %add_convert_fusion.1), channel_id=1, source_target_pairs={{0,32},{32,64},{64,96},{96,0},{1,33},{33,65},{65,97},{97,1},{2,34}... | collective-permute-start | bytes 1720328 | tf_op jit(solution)/shard_map/ppermute | solution.py:253
  133.4 17.3 %all-to-all-start.3 = ((bf16[16,30,256]{2,1,0:T(8,128)(2,1)}), bf16[16,30,256]{2,1,0:T(8,128)(2,1)S(1)}, u32[]{:S(2)}, u32[]{:S(2)}) async-start(bf16[16,30,256]{2,1,0:T(8,128)(2,1)} %shard_map.141), calls=%async_computation.3 | async-start | bytes 524288 | tf_op jit(solution)/shard_map/all_to_all | solution.py:257
  141.7 0.8 copy-start.8
  141.7 1.0 copy-start.9
  142.7 8.0 %copy-start = (bf16[48,1280]{1,0:T(8,128)(2,1)S(1)}, bf16[48,1280]{1,0:T(8,128)(2,1)}, u32[]{:S(2)}) copy-start(bf16[48,1280]{1,0:T(8,128)(2,1)} %cotangent.3) | copy-start | bytes 368644
  142.7 8.0 %copy-start.1 = (s32[1,32,3]{1,0,2:T(1,128)S(1)}, s32[1,32,3]{1,0,2:T(1,128)}, u32[]{:S(2)}) copy-start(s32[1,32,3]{1,0,2:T(1,128)} %param.13) | copy-start | bytes 1156
  142.7 8.0 %copy-start.2 = (f32[1,32,3]{1,0,2:T(1,128)S(1)}, f32[1,32,3]{1,0,2:T(1,128)}, u32[]{:S(2)}) copy-start(f32[1,32,3]{1,0,2:T(1,128)} %param.14) | copy-start | bytes 1156

commit v4 on v3

--- a/solution.py
+++ b/solution.py
@@ -25,26 +25,25 @@
 WIDTH = 1280
 GROUP = 224
 ROWS = COLUMN * CHUNK
-SMALL, LARGE = 12 * 1024 * 1024, 60 * 1024 * 1024
+SMALL, MIDDLE, LARGE = 12 * 1024 * 1024, 52 * 1024 * 1024, 60 * 1024 * 1024
 
 
 def adam_step(gradient, first_moment, second_moment, weight, factor):
-    running_mean = BETA_ONE * first_moment.astype(jnp.float32) + (1.0 - BETA_ONE) * gradient
-    running_square = (
-        BETA_TWO * second_moment.astype(jnp.float32) + (1.0 - BETA_TWO) * gradient * gradient
-    )
-    mean_hat = running_mean * (1.0 / (1.0 - BETA_ONE**STEP_COUNT))
-    square_hat = running_square * (1.0 / (1.0 - BETA_TWO**STEP_COUNT))
-    update = mean_hat / (jnp.sqrt(square_hat) + EPSILON) + WEIGHT_DECAY * weight.astype(jnp.float32)
-    return (factor * update).astype(jnp.bfloat16)
-
-
-def contract(left, right, left_dim, right_dim, precision=None):
+    mean_scale = factor * (1.0 / (1.0 - BETA_ONE**STEP_COUNT))
+    square_scale = 1.0 / (1.0 - BETA_TWO**STEP_COUNT)
+    mean = (mean_scale * BETA_ONE) * first_moment.astype(jnp.float32)
+    mean = mean + (mean_scale * (1.0 - BETA_ONE)) * gradient
+    square = (square_scale * BETA_TWO) * second_moment.astype(jnp.float32)
+    square = square + (square_scale * (1.0 - BETA_TWO)) * (gradient * gradient)
+    decay = (factor * WEIGHT_DECAY) * weight.astype(jnp.float32)
+    return (mean / (jnp.sqrt(square) + EPSILON) + decay).astype(jnp.bfloat16)
+
+
+def contract(left, right, left_dim, right_dim):
     return lax.dot_general(
         left,
         right,
         (((left_dim,), (right_dim,)), ((), ())),
-        precision=precision,
         preferred_element_type=jnp.float32,
     )
 
@@ -232,15 +231,21 @@
     rows[...] = jnp.zeros_like(rows)
     for i in range(SOURCES):
         for n in range(5):
-            part = returned[i, n * FROM_ONE : (n + 1) * FROM_ONE].astype(jnp.float32)
+            part = returned[i, n * FROM_ONE : (n + 1) * FROM_ONE]
             rows[i * PADDED : i * PADDED + FROM_ONE, n * 256 : (n + 1) * 256] = part
     masks = slot_masks()
     choice = row_choice(masks, chosen, tokens)
     gate = row_values(masks, gates)
     weighted = jnp.where(choice, gate, 0.0)
-    combined[...] = contract(weighted, rows[...], 0, 0, lax.Precision.HIGHEST).astype(jnp.bfloat16)
+    total = None
+    for _ in range(3):
+        piece = weighted.astype(jnp.bfloat16)
+        weighted = weighted - piece.astype(jnp.float32)
+        term = contract(piece, rows[...], 0, 0)
+        total = term if total is None else total + term
+    combined[...] = total.astype(jnp.bfloat16)
     back = contract(choice.astype(jnp.bfloat16), cotangent[...], 1, 0)
-    inner = jnp.sum(back * rows[...], axis=1, keepdims=True)
+    inner = jnp.sum(back * rows[...].astype(jnp.float32), axis=1, keepdims=True)
     for k in range(PICKS):
         gate_grad[k] = jnp.sum(jnp.where(masks[k], inner, 0.0), axis=0, keepdims=True)
 
@@ -314,7 +319,7 @@
         + [pltpu.SemaphoreType.DMA((2 * COLUMN + 2 * RING,))]
         + [pltpu.SemaphoreType.DMA((2 * RING + 1,))],
         flops=40 * ROWS * GROUP * WIDTH,
-        limit=LARGE,
+        limit=MIDDLE,
         outside=range(9),
         outputs_outside=True,
     )
@@ -348,7 +353,7 @@
         combine_kernel,
         [shape(tokens.shape[0], WIDTH), shape(PICKS, 1, EXPERTS, dtype=f32)],
         [within_z(summed), cotangent, chosen, gates],
-        [pltpu.VMEM((SOURCES * PADDED, WIDTH), f32)],
+        [pltpu.VMEM((SOURCES * PADDED, WIDTH), bf16)],
     )
     return (combined, gate_grad.transpose(1, 2, 0), step_up.T[None], step_down[None])
 

time: 153 us -> 152 us (level)
  other arithmetic: 0.27 us -> 2.38 us
  waiting for transfers between devices: 40.5 us -> 38.9 us
    all_to_all x2, waiting for transfers between devices: 9.54 us -> 7.27 us  [along_z(): lax.all_to_all(rows, ('zlo', 'zhi'), split_axis=0, concat_axis=0, tiled=T...]
    unnamed x30 -> x26, local copies, waits for them, and re-layouts: 3.13 us -> 1.66 us
  transfers between devices with their start and end apart: 15 -> 15, of which waited for: 9 -> 9; matrix products, arithmetic and copies ran while one was open for 0% -> 2% of each run, Pallas kernels for 4% -> 4%
where the time goes in v4:
time: 152 us; the launch traced here: 151 us
  starting transfers between devices  57.4 us (38%)
  waiting for transfers between devices  38.9 us (26%)
  blocking collectives  26.9 us (18%)
  Pallas kernels  22.7 us (15%)
  other arithmetic  2.38 us (2%)
  local copies, waits for them, and re-layouts  1.66 us (1%)
  between operations  1.54 us (1%)
    ppermute x12, starting transfers between devices, along_x(): lax.ppermute(values, 'x', [(i, (i + step) % RING) for i in range(RING)])  38 us
    ppermute x12, waiting for transfers between devices, along_x(): lax.ppermute(values, 'x', [(i, (i + step) % RING) for i in range(RING)])  28.5 us
    all_to_all x1, blocking collectives, within_z(): lax.all_to_all(rows, ('y', 'core'), split_axis=0, concat_axis=0, tiled=True)  26.9 us
    pallas_call x6, Pallas kernels, call(): pl.pallas_call(kernel, out_shape=shapes, in_specs=[scalar if a.ndim == 1...  22.7 us
    all_to_all x2, starting transfers between devices, along_z(): lax.all_to_all(rows, ('zlo', 'zhi'), split_axis=0, concat_axis=0, tiled=T...  13.9 us
    all_to_all x2, waiting for transfers between devices, along_z(): lax.all_to_all(rows, ('zlo', 'zhi'), split_axis=0, concat_axis=0, tiled=T...  7.27 us
    all_to_all x1, starting transfers between devices, within_z(): lax.all_to_all(rows, ('y', 'core'), split_axis=0, concat_axis=0, tiled=True)  5.47 us
    all_to_all x1, waiting for transfers between devices, within_z(): lax.all_to_all(rows, ('y', 'core'), split_axis=0, concat_axis=0, tiled=True)  3.05 us
  transfers between devices with their start and end apart: 15, of which 9 were waited for; matrix products, arithmetic and copies ran while one was open for 2% of the time, Pallas kernels for 4%

profile of v4, /device:TPU:1, one launch (start us, length us, event | category | flops | bytes accessed | tf_op | source)
XLA Modules:
  0.0 151.4 jit_solution(3143172500082426309)
XLA Ops:
  0.6 2.9 %shard_map.138 = bf16[16,24,640]{2,1,0:T(8,128)(2,1)} custom-call(bf16[48,1280]{1,0:T(8,128)(2,1)} %tokens.1, bf16[48,1280]{1,0:T(8,128)(2,1)} %cotangent.3, s32[3,1,32]{2,1,0:T(1,128)} %bitcast.19, f32[3,1,32]{2,1,0:T(1,128)} %bitcast.21), custom_call_target="tpu_custom_call" | custom-call | bytes 738048 | tf_op jit(solution)/shard_map/pallas_call | solution.py:57
  3.5 26.9 %all_to_all.20.arrived = bf16[16,24,640]{2,1,0:T(8,128)(2,1)S(1)} all-to-all(bf16[16,24,640]{2,1,0:T(8,128)(2,1)} %shard_map.138), channel_id=1, replica_groups=mesh['zlo'=4,'x'=4,'zhi'=2,'y'=8,'core'=2] {'y','core'}, dimensions={0} | all-to-all | bytes 983040 | tf_op jit(solution)/shard_map/all_to_all | solution.py:262
  30.4 1.7 %shard_map.139 = bf16[8,96,1280]{2,1,0:T(8,128)(2,1)} custom-call(bf16[16,24,640]{2,1,0:T(8,128)(2,1)S(1)} %all_to_all.20.arrived), custom_call_target="tpu_custom_call" | custom-call | bytes 2457600 | tf_op jit(solution)/shard_map/pallas_call | solution.py:57
  32.1 0.0 copy-start.5
  32.1 0.0 copy-start.6
  32.1 8.5 %all-to-all-start.1 = ((bf16[8,96,1280]{2,1,0:T(8,128)(2,1)}), bf16[8,96,1280]{2,1,0:T(8,128)(2,1)}, u32[]{:S(2)}, u32[]{:S(2)}) async-start(bf16[8,96,1280]{2,1,0:T(8,128)(2,1)} %shard_map.139), calls=%async_computation.1 | async-start | bytes 3932160 | tf_op jit(solution)/shard_map/all_to_all | solution.py:266
  40.6 0.0 copy-done.5
  40.6 3.1 %collective-permute-start = (bf16[224,1280]{1,0:T(8,128)(2,1)S(1)}, bf16[224,1280]{1,0:T(8,128)(2,1)S(1)}, u32[]{:S(2)}, u32[]{:S(2)}) collective-permute-start(bf16[224,1280]{1,0:T(8,128)(2,1)S(1)} %bitcast.25), channel_id=1, source_target_pairs={{0,32},{32,64},{64,96},{96,0},{1,33},{33,65},{65,97},{97,1},{2,34}... | collective-permute-start | bytes 1720328 | tf_op jit(solution)/shard_map/ppermute | solution.py:258
  43.8 0.0 copy-done.6
  43.8 3.4 %collective-permute-start.3 = (bf16[224,1280]{1,0:T(8,128)(2,1)S(1)}, bf16[224,1280]{1,0:T(8,128)(2,1)S(1)}, u32[]{:S(2)}, u32[]{:S(2)}) collective-permute-start(bf16[224,1280]{1,0:T(8,128)(2,1)S(1)} %bitcast.29), channel_id=1, source_target_pairs={{0,96},{32,0},{64,32},{96,64},{1,97},{33,1},{65,33},{97,65},{2,98}... | collective-permute-start | bytes 1720328 | tf_op jit(solution)/shard_map/ppermute | solution.py:258
  47.2 3.2 %collective-permute-start.2 = (bf16[224,1280]{1,0:T(8,128)(2,1)S(1)}, bf16[224,1280]{1,0:T(8,128)(2,1)S(1)}, u32[]{:S(2)}, u32[]{:S(2)}) collective-permute-start(bf16[224,1280]{1,0:T(8,128)(2,1)S(1)} %bitcast.26), channel_id=1, source_target_pairs={{0,96},{32,0},{64,32},{96,64},{1,97},{33,1},{65,33},{97,65},{2,98}... | collective-permute-start | bytes 1720328 | tf_op jit(solution)/shard_map/ppermute | solution.py:258
  50.4 2.1 %collective-permute-start.5 = (bf16[224,1280]{1,0:T(8,128)(2,1)S(1)}, bf16[224,1280]{1,0:T(8,128)(2,1)S(1)}, u32[]{:S(2)}, u32[]{:S(2)}) collective-permute-start(bf16[224,1280]{1,0:T(8,128)(2,1)S(1)} %bitcast.30), channel_id=1, source_target_pairs={{0,32},{32,64},{64,96},{96,0},{1,33},{33,65},{65,97},{97,1},{2,34}... | collective-permute-start | bytes 1720328 | tf_op jit(solution)/shard_map/ppermute | solution.py:258
  52.5 6.4 %collective-permute-done.args_1_ = bf16[224,1280]{1,0:T(8,128)(2,1)S(1)} collective-permute-done((bf16[224,1280]{1,0:T(8,128)(2,1)S(1)}, bf16[224,1280]{1,0:T(8,128)(2,1)S(1)}, u32[]{:S(2)}, u32[]{:S(2)}) %collective-permute-start) | collective-permute-done | bytes 573472 | tf_op jit(solution)/shard_map/ppermute | solution.py:258
  58.9 0.0 copy-start.8
  58.9 1.9 %collective-permute-start.1 = (bf16[224,1280]{1,0:T(8,128)(2,1)S(1)}, bf16[224,1280]{1,0:T(8,128)(2,1)S(1)}, u32[]{:S(2)}, u32[]{:S(2)}) collective-permute-start(bf16[224,1280]{1,0:T(8,128)(2,1)S(1)} %collective-permute-done.args_1_), channel_id=1, source_target_pairs={{0,32},{32,64},{64,96},{96,0},{1,33},{33,65},{65,97},{97,1},{2,34}... | collective-permute-start | bytes 1720328 | tf_op jit(solution)/shard_map/ppermute | solution.py:258
  60.8 0.0 collective-permute-done.3.args_6_
  60.8 0.0 copy-start.9
  60.8 4.6 %collective-permute-start.4 = (bf16[224,1280]{1,0:T(8,128)(2,1)S(1)}, bf16[224,1280]{1,0:T(8,128)(2,1)}, u32[]{:S(2)}, u32[]{:S(2)}) collective-permute-start(bf16[224,1280]{1,0:T(8,128)(2,1)S(1)} %collective-permute-done.3.args_6_), channel_id=1, source_target_pairs={{0,96},{32,0},{64,32},{96,64},{1,97},{33,1},{65,33},{97,65},{2,98}... | collective-permute-start | bytes 1720328 | tf_op jit(solution)/shard_map/ppermute | solution.py:258
  65.4 7.7 %collective-permute-done.2.args_2_ = bf16[224,1280]{1,0:T(8,128)(2,1)S(1)} collective-permute-done((bf16[224,1280]{1,0:T(8,128)(2,1)S(1)}, bf16[224,1280]{1,0:T(8,128)(2,1)S(1)}, u32[]{:S(2)}, u32[]{:S(2)}) %collective-permute-start.2) | collective-permute-done | bytes 573472 | tf_op jit(solution)/shard_map/ppermute | solution.py:258
  73.1 0.0 copy-start.10
  73.1 0.0 collective-permute-done.5.args_5_
  73.1 0.0 copy-start.11
  73.1 10.0 %collective-permute-done.1.args_0_ = bf16[224,1280]{1,0:T(8,128)(2,1)S(1)} collective-permute-done((bf16[224,1280]{1,0:T(8,128)(2,1)S(1)}, bf16[224,1280]{1,0:T(8,128)(2,1)S(1)}, u32[]{:S(2)}, u32[]{:S(2)}) %collective-permute-start.1) | collective-permute-done | bytes 573472 | tf_op jit(solution)/shard_map/ppermute | solution.py:258
  83.1 0.0 copy-done.11
  83.1 0.0 copy-start.12
  83.1 0.8 copy-done.12
  83.9 1.4 collective-permute-done.4.args_4_
  85.3 0.0 copy-done.10
  85.3 1.2 all-to-all-done.1.arrived
  86.5 0.0 copy-done.8
  86.5 0.0 copy-done.9
  86.5 10.9 %shard_map.140 = (bf16[224,1280]{1,0:T(8,128)(2,1)S(1)}, bf16[224,1280]{1,0:T(8,128)(2,1)S(1)}, bf16[224,1280]{1,0:T(8,128)(2,1)S(1)}, bf16[224,1280]{1,0:T(8,12...) custom-call(bf16[8,96,1280]{2,1,0:T(8,128)(2,1)} %all-to-all-done.1., ...), custom_call_target="tpu_custom_call" | custom-call | flops 4404019200 | bytes 12124160 | tf_op jit(solution)/shard_map/pallas_call | solution.py:57
  97.4 0.0 copy-start.4
  97.4 3.2 %collective-permute-start.7 = (bf16[224,1280]{1,0:T(8,128)(2,1)S(1)}, bf16[224,1280]{1,0:T(8,128)(2,1)}, u32[]{:S(2)}, u32[]{:S(2)}) collective-permute-start(bf16[224,1280]{1,0:T(8,128)(2,1)S(1)} %get-tuple-element.25), channel_id=1, source_target_pairs={{0,32},{32,64},{64,96},{96,0},{1,33},{33,65},{65,97},{97,1},{2,34}... | collective-permute-start | bytes 1720328 | tf_op jit(solution)/shard_map/ppermute | solution.py:258
  100.6 3.4 %collective-permute-start.8 = (bf16[224,1280]{1,0:T(8,128)(2,1)S(1)}, bf16[224,1280]{1,0:T(8,128)(2,1)}, u32[]{:S(2)}, u32[]{:S(2)}) collective-permute-start(bf16[224,1280]{1,0:T(8,128)(2,1)S(1)} %get-tuple-element.26), channel_id=1, source_target_pairs={{0,96},{32,0},{64,32},{96,64},{1,97},{33,1},{65,33},{97,65},{2,98}... | collective-permute-start | bytes 1720328 | tf_op jit(solution)/shard_map/ppermute | solution.py:258
  104.0 5.4 %all-to-all-start.2 = ((bf16[8,48,1280]{2,1,0:T(8,128)(2,1)}), bf16[8,48,1280]{2,1,0:T(8,128)(2,1)S(1)}, u32[]{:S(2)}, u32[]{:S(2)}) async-start(bf16[8,48,1280]{2,1,0:T(8,128)(2,1)} %get-tuple-element.19), calls=%async_computation.2 | async-start | bytes 1966080 | tf_op jit(solution)/shard_map/all_to_all | solution.py:266
  109.4 0.0 copy-start.3
  109.4 2.1 %collective-permute-start.10 = (bf16[224,1280]{1,0:T(8,128)(2,1)}, bf16[224,1280]{1,0:T(8,128)(2,1)}, u32[]{:S(2)}, u32[]{:S(2)}) collective-permute-start(bf16[224,1280]{1,0:T(8,128)(2,1)} %get-tuple-element.29), channel_id=1, source_target_pairs={{0,32},{32,64},{64,96},{96,0},{1,33},{33,65},{65,97},{97,1},{2,34}... | collective-permute-start | bytes 1720328 | tf_op jit(solution)/shard_map/ppermute | solution.py:258
  111.4 4.6 %collective-permute-start.6 = (bf16[224,1280]{1,0:T(8,128)(2,1)S(1)}, bf16[224,1280]{1,0:T(8,128)(2,1)}, u32[]{:S(2)}, u32[]{:S(2)}) collective-permute-start(bf16[224,1280]{1,0:T(8,128)(2,1)S(1)} %get-tuple-element.23), channel_id=1, source_target_pairs={{0,96},{32,0},{64,32},{96,64},{1,97},{33,1},{65,33},{97,65},{2,98}... | collective-permute-start | bytes 1720328 | tf_op jit(solution)/shard_map/ppermute | solution.py:258
  116.0 0.0 collective-permute-done.7
  116.0 0.7 collective-permute-done.8
  116.7 0.0 copy-done.4
  116.8 1.2 add_convert_fusion
  117.9 4.6 %collective-permute-start.11 = (bf16[224,1280]{1,0:T(8,128)(2,1)S(1)}, bf16[224,1280]{1,0:T(8,128)(2,1)S(1)}, u32[]{:S(2)}, u32[]{:S(2)}) collective-permute-start(bf16[224,1280]{1,0:T(8,128)(2,1)S(1)} %add_convert_fusion), channel_id=1, source_target_pairs={{0,96},{32,0},{64,32},{96,64},{1,97},{33,1},{65,33},{97,65},{2,98}... | collective-permute-start | bytes 1720328 | tf_op jit(solution)/shard_map/ppermute | solution.py:258
  122.5 0.0 copy-done.3
  122.5 1.2 add_convert_fusion.1
  123.7 1.9 %collective-permute-start.9 = (bf16[224,1280]{1,0:T(8,128)(2,1)S(1)}, bf16[224,1280]{1,0:T(8,128)(2,1)}, u32[]{:S(2)}, u32[]{:S(2)}) collective-permute-start(bf16[224,1280]{1,0:T(8,128)(2,1)S(1)} %add_convert_fusion.1), channel_id=1, source_target_pairs={{0,32},{32,64},{64,96},{96,0},{1,33},{33,65},{65,97},{97,1},{2,34}... | collective-permute-start | bytes 1720328 | tf_op jit(solution)/shard_map/ppermute | solution.py:258
  125.7 6.1 %all-to-all-done.2.arrived = bf16[8,48,1280]{2,1,0:T(8,128)(2,1)S(1)} async-done(((bf16[8,48,1280]{2,1,0:T(8,128)(2,1)}), bf16[8,48,1280]{2,1,0:T(8,128)(2,1)S(1)}, u32[]{:S(2)}, u32[]{:S(2)}) %all-to-all-start.2) | async-done | bytes 983072 | tf_op jit(solution)/shard_map/all_to_all | solution.py:266
  131.8 1.0 shard_map.141
  132.8 5.5 %all-to-all-start.3 = ((bf16[16,30,256]{2,1,0:T(8,128)(2,1)}), bf16[16,30,256]{2,1,0:T(8,128)(2,1)S(1)}, u32[]{:S(2)}, u32[]{:S(2)}) async-start(bf16[16,30,256]{2,1,0:T(8,128)(2,1)} %shard_map.141), calls=%async_computation.3 | async-start | bytes 524288 | tf_op jit(solution)/shard_map/all_to_all | solution.py:262
  139.0 0.0 collective-permute-done.10.args_10_
  139.0 0.0 collective-permute-done.6.args_4_
  139.0 2.3 %collective-permute-done.11.args_11_ = bf16[224,1280]{1,0:T(8,128)(2,1)S(1)} collective-permute-done((bf16[224,1280]{1,0:T(8,128)(2,1)S(1)}, bf16[224,1280]{1,0:T(8,128)(2,1)S(1)}, u32[]{:S(2)}, u32[]{:S(2)}) %collective-permute-start.11) | collective-permute-done | bytes 573472 | tf_op jit(solution)/shard_map/ppermute | solution.py:258
  141.3 0.0 copy-start.7
  141.3 0.0 collective-permute-done.9.args_5_
  141.3 0.8 copy-done.7
  142.1 0.0 copy-start
  142.1 0.0 copy-start.1
  142.1 4.9 %shard_map.143 = (bf16[224,1280]{1,0:T(8,128)(2,1)}, bf16[224,1280]{1,0:T(8,128)(2,1)}) custom-call(f32[1]{0:T(128)S(6)} %pow.3.factor, bf16[224,1280]{1,0:T(8,128)(2,1)} %bitcast.31, bf16[224,1280]{1,0:T(8,128)(2,1)} %bitcast.32, bf16[224,1280]{1,0:T(8,128)(2,1)} %bitcast.24, bf16[224,1280]{1,0:T(8,128)(2,1)} %get-tuple-element.22.args_3_, ...), custom_call_target="tpu_custom_call" | custom-call | bytes 8028164 | tf_op jit(solution)/shard_map/pallas_call | solution.py:57
  147.1 3.0 %all-to-all-done.3.returned = bf16[16,30,256]{2,1,0:T(8,128)(2,1)S(1)} async-done(((bf16[16,30,256]{2,1,0:T(8,128)(2,1)}), bf16[16,30,256]{2,1,0:T(8,128)(2,1)S(1)}, u32[]{:S(2)}, u32[]{:S(2)}) %all-to-all-start.3) | async-done | bytes 245792 | tf_op jit(solution)/shard_map/all_to_all | solution.py:262
  150.1 0.0 copy-done
  150.1 0.0 copy-done.1
  150.2 0.0 copy-done.2
  150.2 1.2 shard_map.142
  (1 shorter events, 0.0 us)
Async XLA Ops:
  32.1 8.5 %copy-start.5 = (bf16[1,1280,224]{1,2,0:T(8,128)(2,1)S(1)}, bf16[1,1280,224]{1,2,0:T(8,128)(2,1)}, u32[]{:S(2)}) copy-start(bf16[1,1280,224]{1,2,0:T(8,128)(2,1)} %param.15) | copy-start | bytes 1720324
  32.1 11.7 %copy-start.6 = (bf16[1,224,1280]{2,1,0:T(8,128)(2,1)S(1)}, bf16[1,224,1280]{2,1,0:T(8,128)(2,1)}, u32[]{:S(2)}) copy-start(bf16[1,224,1280]{2,1,0:T(8,128)(2,1)} %param.16) | copy-start | bytes 1720324
  32.1 54.3 %all-to-all-start.1 = ((bf16[8,96,1280]{2,1,0:T(8,128)(2,1)}), bf16[8,96,1280]{2,1,0:T(8,128)(2,1)}, u32[]{:S(2)}, u32[]{:S(2)}) async-start(bf16[8,96,1280]{2,1,0:T(8,128)(2,1)} %shard_map.139), calls=%async_computation.1 | async-start | bytes 3932160 | tf_op jit(solution)/shard_map/all_to_all | solution.py:266
  40.6 18.2 %collective-permute-start = (bf16[224,1280]{1,0:T(8,128)(2,1)S(1)}, bf16[224,1280]{1,0:T(8,128)(2,1)S(1)}, u32[]{:S(2)}, u32[]{:S(2)}) collective-permute-start(bf16[224,1280]{1,0:T(8,128)(2,1)S(1)} %bitcast.25), channel_id=1, source_target_pairs={{0,32},{32,64},{64,96},{96,0},{1,33},{33,65},{65,97},{97,1},{2,34}... | collective-permute-start | bytes 1720328 | tf_op jit(solution)/shard_map/ppermute | solution.py:258
  43.8 17.0 %collective-permute-start.3 = (bf16[224,1280]{1,0:T(8,128)(2,1)S(1)}, bf16[224,1280]{1,0:T(8,128)(2,1)S(1)}, u32[]{:S(2)}, u32[]{:S(2)}) collective-permute-start(bf16[224,1280]{1,0:T(8,128)(2,1)S(1)} %bitcast.29), channel_id=1, source_target_pairs={{0,96},{32,0},{64,32},{96,64},{1,97},{33,1},{65,33},{97,65},{2,98}... | collective-permute-start | bytes 1720328 | tf_op jit(solution)/shard_map/ppermute | solution.py:258
  47.2 25.9 %collective-permute-start.2 = (bf16[224,1280]{1,0:T(8,128)(2,1)S(1)}, bf16[224,1280]{1,0:T(8,128)(2,1)S(1)}, u32[]{:S(2)}, u32[]{:S(2)}) collective-permute-start(bf16[224,1280]{1,0:T(8,128)(2,1)S(1)} %bitcast.26), channel_id=1, source_target_pairs={{0,96},{32,0},{64,32},{96,64},{1,97},{33,1},{65,33},{97,65},{2,98}... | collective-permute-start | bytes 1720328 | tf_op jit(solution)/shard_map/ppermute | solution.py:258
  50.4 22.7 %collective-permute-start.5 = (bf16[224,1280]{1,0:T(8,128)(2,1)S(1)}, bf16[224,1280]{1,0:T(8,128)(2,1)S(1)}, u32[]{:S(2)}, u32[]{:S(2)}) collective-permute-start(bf16[224,1280]{1,0:T(8,128)(2,1)S(1)} %bitcast.30), channel_id=1, source_target_pairs={{0,32},{32,64},{64,96},{96,0},{1,33},{33,65},{65,97},{97,1},{2,34}... | collective-permute-start | bytes 1720328 | tf_op jit(solution)/shard_map/ppermute | solution.py:258
  58.9 27.6 %copy-start.8 = (bf16[224,1280]{1,0:T(8,128)(2,1)}, bf16[224,1280]{1,0:T(8,128)(2,1)S(1)}, u32[]{:S(2)}) copy-start(bf16[224,1280]{1,0:T(8,128)(2,1)S(1)} %collective-permute-done.args_1_) | copy-start | bytes 1720324
  58.9 24.2 %collective-permute-start.1 = (bf16[224,1280]{1,0:T(8,128)(2,1)S(1)}, bf16[224,1280]{1,0:T(8,128)(2,1)S(1)}, u32[]{:S(2)}, u32[]{:S(2)}) collective-permute-start(bf16[224,1280]{1,0:T(8,128)(2,1)S(1)} %collective-permute-done.args_1_), channel_id=1, source_target_pairs={{0,32},{32,64},{64,96},{96,0},{1,33},{33,65},{65,97},{97,1},{2,34}... | collective-permute-start | bytes 1720328 | tf_op jit(solution)/shard_map/ppermute | solution.py:258
  60.8 25.7 %copy-start.9 = (bf16[224,1280]{1,0:T(8,128)(2,1)}, bf16[224,1280]{1,0:T(8,128)(2,1)S(1)}, u32[]{:S(2)}) copy-start(bf16[224,1280]{1,0:T(8,128)(2,1)S(1)} %collective-permute-done.3.args_6_) | copy-start | bytes 1720324
  60.8 24.5 %collective-permute-start.4 = (bf16[224,1280]{1,0:T(8,128)(2,1)S(1)}, bf16[224,1280]{1,0:T(8,128)(2,1)}, u32[]{:S(2)}, u32[]{:S(2)}) collective-permute-start(bf16[224,1280]{1,0:T(8,128)(2,1)S(1)} %collective-permute-done.3.args_6_), channel_id=1, source_target_pairs={{0,96},{32,0},{64,32},{96,64},{1,97},{33,1},{65,33},{97,65},{2,98}... | collective-permute-start | bytes 1720328 | tf_op jit(solution)/shard_map/ppermute | solution.py:258
  73.1 12.2 %copy-start.10 = (bf16[224,1280]{1,0:T(8,128)(2,1)}, bf16[224,1280]{1,0:T(8,128)(2,1)S(1)}, u32[]{:S(2)}) copy-start(bf16[224,1280]{1,0:T(8,128)(2,1)S(1)} %collective-permute-done.2.args_2_) | copy-start | bytes 1720324
  73.1 10.0 %copy-start.11 = (bf16[224,1280]{1,0:T(8,128)(2,1)}, bf16[224,1280]{1,0:T(8,128)(2,1)S(1)}, u32[]{:S(2)}) copy-start(bf16[224,1280]{1,0:T(8,128)(2,1)S(1)} %collective-permute-done.5.args_5_) | copy-start | bytes 1720324
  83.1 0.8 copy-start.12
  97.4 19.4 %copy-start.4 = (bf16[224,1280]{1,0:T(8,128)(2,1)S(1)}, bf16[224,1280]{1,0:T(8,128)(2,1)}, u32[]{:S(2)}) copy-start(bf16[224,1280]{1,0:T(8,128)(2,1)} %get-tuple-element.30) | copy-start | bytes 1720324
  97.4 18.7 %collective-permute-start.7 = (bf16[224,1280]{1,0:T(8,128)(2,1)S(1)}, bf16[224,1280]{1,0:T(8,128)(2,1)}, u32[]{:S(2)}, u32[]{:S(2)}) collective-permute-start(bf16[224,1280]{1,0:T(8,128)(2,1)S(1)} %get-tuple-element.25), channel_id=1, source_target_pairs={{0,32},{32,64},{64,96},{96,0},{1,33},{33,65},{65,97},{97,1},{2,34}... | collective-permute-start | bytes 1720328 | tf_op jit(solution)/shard_map/ppermute | solution.py:258
  100.6 16.1 %collective-permute-start.8 = (bf16[224,1280]{1,0:T(8,128)(2,1)S(1)}, bf16[224,1280]{1,0:T(8,128)(2,1)}, u32[]{:S(2)}, u32[]{:S(2)}) collective-permute-start(bf16[224,1280]{1,0:T(8,128)(2,1)S(1)} %get-tuple-element.26), channel_id=1, source_target_pairs={{0,96},{32,0},{64,32},{96,64},{1,97},{33,1},{65,33},{97,65},{2,98}... | collective-permute-start | bytes 1720328 | tf_op jit(solution)/shard_map/ppermute | solution.py:258
  104.0 27.8 %all-to-all-start.2 = ((bf16[8,48,1280]{2,1,0:T(8,128)(2,1)}), bf16[8,48,1280]{2,1,0:T(8,128)(2,1)S(1)}, u32[]{:S(2)}, u32[]{:S(2)}) async-start(bf16[8,48,1280]{2,1,0:T(8,128)(2,1)} %get-tuple-element.19), calls=%async_computation.2 | async-start | bytes 1966080 | tf_op jit(solution)/shard_map/all_to_all | solution.py:266
  109.4 13.2 %copy-start.3 = (bf16[224,1280]{1,0:T(8,128)(2,1)S(1)}, bf16[224,1280]{1,0:T(8,128)(2,1)}, u32[]{:S(2)}) copy-start(bf16[224,1280]{1,0:T(8,128)(2,1)} %get-tuple-element.24) | copy-start | bytes 1720324
  109.4 29.6 %collective-permute-start.10 = (bf16[224,1280]{1,0:T(8,128)(2,1)}, bf16[224,1280]{1,0:T(8,128)(2,1)}, u32[]{:S(2)}, u32[]{:S(2)}) collective-permute-start(bf16[224,1280]{1,0:T(8,128)(2,1)} %get-tuple-element.29), channel_id=1, source_target_pairs={{0,32},{32,64},{64,96},{96,0},{1,33},{33,65},{65,97},{97,1},{2,34}... | collective-permute-start | bytes 1720328 | tf_op jit(solution)/shard_map/ppermute | solution.py:258
  111.4 27.5 %collective-permute-start.6 = (bf16[224,1280]{1,0:T(8,128)(2,1)S(1)}, bf16[224,1280]{1,0:T(8,128)(2,1)}, u32[]{:S(2)}, u32[]{:S(2)}) collective-permute-start(bf16[224,1280]{1,0:T(8,128)(2,1)S(1)} %get-tuple-element.23), channel_id=1, source_target_pairs={{0,96},{32,0},{64,32},{96,64},{1,97},{33,1},{65,33},{97,65},{2,98}... | collective-permute-start | bytes 1720328 | tf_op jit(solution)/shard_map/ppermute | solution.py:258
  117.9 23.4 %collective-permute-start.11 = (bf16[224,1280]{1,0:T(8,128)(2,1)S(1)}, bf16[224,1280]{1,0:T(8,128)(2,1)S(1)}, u32[]{:S(2)}, u32[]{:S(2)}) collective-permute-start(bf16[224,1280]{1,0:T(8,128)(2,1)S(1)} %add_convert_fusion), channel_id=1, source_target_pairs={{0,96},{32,0},{64,32},{96,64},{1,97},{33,1},{65,33},{97,65},{2,98}... | collective-permute-start | bytes 1720328 | tf_op jit(solution)/shard_map/ppermute | solution.py:258
  123.7 17.6 %collective-permute-start.9 = (bf16[224,1280]{1,0:T(8,128)(2,1)S(1)}, bf16[224,1280]{1,0:T(8,128)(2,1)}, u32[]{:S(2)}, u32[]{:S(2)}) collective-permute-start(bf16[224,1280]{1,0:T(8,128)(2,1)S(1)} %add_convert_fusion.1), channel_id=1, source_target_pairs={{0,32},{32,64},{64,96},{96,0},{1,33},{33,65},{65,97},{97,1},{2,34}... | collective-permute-start | bytes 1720328 | tf_op jit(solution)/shard_map/ppermute | solution.py:258
  132.8 17.3 %all-to-all-start.3 = ((bf16[16,30,256]{2,1,0:T(8,128)(2,1)}), bf16[16,30,256]{2,1,0:T(8,128)(2,1)S(1)}, u32[]{:S(2)}, u32[]{:S(2)}) async-start(bf16[16,30,256]{2,1,0:T(8,128)(2,1)} %shard_map.141), calls=%async_computation.3 | async-start | bytes 524288 | tf_op jit(solution)/shard_map/all_to_all | solution.py:262
  141.3 0.8 copy-start.7
  142.1 8.0 %copy-start = (bf16[48,1280]{1,0:T(8,128)(2,1)S(1)}, bf16[48,1280]{1,0:T(8,128)(2,1)}, u32[]{:S(2)}) copy-start(bf16[48,1280]{1,0:T(8,128)(2,1)} %cotangent.3) | copy-start | bytes 368644
  142.1 8.0 %copy-start.1 = (s32[1,32,3]{1,0,2:T(1,128)S(1)}, s32[1,32,3]{1,0,2:T(1,128)}, u32[]{:S(2)}) copy-start(s32[1,32,3]{1,0,2:T(1,128)} %param.13) | copy-start | bytes 1156
  142.1 8.0 %copy-start.2 = (f32[1,32,3]{1,0,2:T(1,128)S(1)}, f32[1,32,3]{1,0,2:T(1,128)}, u32[]{:S(2)}) copy-start(f32[1,32,3]{1,0,2:T(1,128)} %param.14) | copy-start | bytes 1156

commit v5 on v4

--- a/solution.py
+++ b/solution.py
@@ -176,10 +176,17 @@
 CUTS = [pl.ds(n, 256) for n in range(0, WIDTH, 256)]
 
 
+def gradients(back_hidden, slope, units, rows, grads, up_out, down_out):
+    back = (slope * back_hidden).astype(jnp.bfloat16)
+    for cut in CUTS:
+        for out, a, b in zip((up_out, down_out), (back, units), (rows, grads)):
+            out[:, cut] = contract(a, b[:, cut], 1, 0).astype(jnp.bfloat16)
+
+
 def expert_kernel(arrived, *args):
-    ups, downs, outs, staged = args[:4], args[4:8], args[8:17], args[17:26]
-    rows, grads, up, down, units, slopes, sems, out_sems = args[26:]
-    partial = 8
+    ups, downs, outs, staged = args[:4], args[4:8], args[8:13], args[13:18]
+    rows, grads, up, down, sems, out_sems = args[18:]
+    up_far, down_far, units, slopes, partial = staged
     pairs = row_copies(arrived, 0, rows)
     pairs += [(ups[i], up.at[i]) for i in range(RING)] + row_copies(arrived, 1, grads)
     pairs += [(downs[i], down.at[i]) for i in range(RING)]
@@ -191,38 +198,58 @@
         share = 0.5 * (1.0 + lax.erf(pre * 0.7071067811865476))
         units[i] = (pre * share).astype(jnp.bfloat16)
         slopes[i] = share + pre * (0.3989422804014327 * jnp.exp(-0.5 * pre * pre))
+    writes = start_all([(units, outs[2]), (slopes, outs[3])], out_sems)
     wait_all(copies[COLUMN + RING :])
-    writes = []
-    for i in range(RING):
-        back = (slopes[i] * contract(down[i], grads[...], 1, 1)).astype(jnp.bfloat16)
-        here = slice(2 * i, 2 * i + 2)
-        for cut in CUTS:
-            for out, a, b in zip(staged[here], (back, units[i]), (rows, grads)):
-                out[:, cut] = contract(a, b[:, cut], 1, 0).astype(jnp.bfloat16)
-        writes += start_all(list(zip(staged[here], outs[here])), out_sems, len(writes))
+    back_hidden = contract(down[0], grads[...], 1, 1)
+    gradients(back_hidden, slopes[0], units[0], rows, grads, up_far, down_far)
+    writes += start_all([(up_far, outs[0]), (down_far, outs[1])], out_sems, len(writes))
     for cut in CUTS:
         total = contract(units[0], down[0, :, cut], 0, 0)
         for i in range(1, RING):
             total = total + contract(units[i], down[i, :, cut], 0, 0)
         for j in range(COLUMN):
-            staged[partial][j, :, cut] = total[j * CHUNK : j * CHUNK + CHUNK].astype(jnp.bfloat16)
-    wait_all(writes + start_all([(staged[partial], outs[partial])], out_sems, len(writes)))
+            partial[j, :, cut] = total[j * CHUNK : j * CHUNK + CHUNK].astype(jnp.bfloat16)
+    wait_all(writes + start_all([(partial, outs[4])], out_sems, len(writes)))
+
+
+def backward_kernel(arrived, *args):
+    downs, (hidden, slope), outs, staged = args[:3], args[3:5], args[5:11], args[11:17]
+    rows, grads, down, units, slopes, sems, out_sems = args[17:]
+    copies = start_all(row_copies(arrived, 1, grads), sems)
+    first = [(downs[0], down.at[0]), (slope.at[1], slopes.at[0]), (hidden.at[1], units.at[0])]
+    pairs = first + row_copies(arrived, 0, rows)
+    for i in (1, 2):
+        pairs.append((downs[i], down.at[i]))
+        pairs += [(slope.at[i + 1], slopes.at[i]), (hidden.at[i + 1], units.at[i])]
+    copies += start_all(pairs, sems, len(copies))
+    wait_all(copies[: COLUMN + 3])
+    writes = []
+    for i in range(3):
+        if i:
+            late = 2 * COLUMN + 3 * i
+            wait_all(copies[late : late + 3])
+        back_hidden = contract(down[i], grads[...], 1, 1)
+        if not i:
+            wait_all(copies[COLUMN + 3 : 2 * COLUMN + 3])
+        here = slice(2 * i, 2 * i + 2)
+        gradients(back_hidden, slopes[i], units[i], rows, grads, *staged[here])
+        writes += start_all(list(zip(staged[here], outs[here])), out_sems, len(writes))
+    wait_all(writes)
 
 
 def step_kernel(factor, *args):
-    sources, outs, (held, staged, sems, out_sems) = args[:12], args[12:14], args[14:]
-    parts = [sources[:6], sources[6:]]
-    pairs = [(source, held.at[n, m]) for n in range(2) for m, source in enumerate(parts[n])]
-    copies = start_all(pairs, sems)
-    writes = []
+    sources, out, (held, staged, sems, out_sems) = args[:6], args[6], args[7:]
+    copies = start_all([(source, held.at[n]) for n, source in enumerate(sources)], sems)
+    wait_all(copies)
+    half, writes = GROUP // 2, []
     for n in range(2):
-        wait_all(copies[6 * n : 6 * n + 6])
-        for start in range(0, GROUP, 32):
-            here = pl.ds(start, 32)
-            first_moment, second_moment, weight, own, one, two = [held[n, m, here] for m in range(6)]
+        for start in range(n * half, (n + 1) * half, 16):
+            here = pl.ds(start, 16)
+            first_moment, second_moment, weight, own, one, two = [held[m, here] for m in range(6)]
             gradient = own.astype(jnp.float32) + one.astype(jnp.float32) + two.astype(jnp.float32)
-            staged[n, here] = adam_step(gradient, first_moment, second_moment, weight, factor[0])
-        writes += start_all([(staged.at[n], outs[n])], out_sems, len(writes))
+            staged[here] = adam_step(gradient, first_moment, second_moment, weight, factor[0])
+        part = pl.ds(n * half, half)
+        writes += start_all([(staged.at[part], out.at[part])], out_sems, n)
     wait_all(writes)
 
 
@@ -307,46 +334,43 @@
     ups = [along_x(up_left, 1), up_left, up_right, up_own]
     downs = [along_x(down_right, -1), down_left, down_right, down_own]
     weight = shape(GROUP, WIDTH)
-    results = [weight] * 8 + [shape(COLUMN, CHUNK, WIDTH)]
-    *gradients, partial = call(
+    products = ROWS * GROUP * WIDTH
+    held = [shape(RING, GROUP, ROWS), shape(RING, GROUP, ROWS, dtype=f32)]
+    results = [weight, weight, *held, shape(COLUMN, CHUNK, WIDTH)]
+    far_up, far_down, hidden, slope, partial = call(
         expert_kernel,
         results,
         [rows, *ups, *downs],
         [pltpu.VMEM(r.shape, r.dtype) for r in results]
         + [pltpu.VMEM((ROWS, WIDTH), bf16)] * 2
         + [pltpu.VMEM((RING, GROUP, WIDTH), bf16)] * 2
-        + [pltpu.VMEM((RING, GROUP, ROWS), dtype) for dtype in (bf16, f32)]
-        + [pltpu.SemaphoreType.DMA((2 * COLUMN + 2 * RING,))]
-        + [pltpu.SemaphoreType.DMA((2 * RING + 1,))],
-        flops=40 * ROWS * GROUP * WIDTH,
+        + [pltpu.SemaphoreType.DMA((2 * COLUMN + 2 * RING,)), pltpu.SemaphoreType.DMA((5,))],
+        flops=22 * products,
         limit=MIDDLE,
         outside=range(9),
         outputs_outside=True,
     )
     arrived = along_z(partial)
-    far_up, far_down, left_up, left_down, right_up, right_down, own_up, own_down = gradients
+    results = [weight] * 6
+    left_up, left_down, right_up, right_down, own_up, own_down = call(
+        backward_kernel,
+        results,
+        [rows, *downs[1:], hidden, slope],
+        [pltpu.VMEM(r.shape, r.dtype) for r in results]
+        + [pltpu.VMEM((ROWS, WIDTH), bf16)] * 2
+        + [pltpu.VMEM((3, GROUP, WIDTH), bf16)]
+        + [pltpu.VMEM((3, GROUP, ROWS), dtype) for dtype in (bf16, f32)]
+        + [pltpu.SemaphoreType.DMA((2 * COLUMN + 9,)), pltpu.SemaphoreType.DMA((6,))],
+        flops=18 * products,
+        limit=LARGE,
+        outside=range(6),
+        outputs_outside=True,
+    )
     up_two, down_two = lax.optimization_barrier((along_x(far_up, 1), along_x(far_down, -1)))
     up_one = along_x(left_up, -1)
     down_one = along_x(right_down, 1)
     up_sum = along_x((right_up.astype(f32) + up_two.astype(f32)).astype(bf16), 1)
     down_sum = along_x((left_down.astype(f32) + down_two.astype(f32)).astype(bf16), -1)
-    exponent = (LAYERS - 1 - layer_index).astype(f32)
-    factor = jnp.power(f32(DECAY_RATE), exponent)
-    step_up, step_down = call(
-        step_kernel,
-        [weight, weight],
-        [
-            factor,
-            *(first_up[0].T, second_up[0].T, up_own, own_up, up_one, up_sum),
-            *(first_down[0], second_down[0], down_own, own_down, down_one, down_sum),
-        ],
-        [pltpu.VMEM((2, 6, GROUP, WIDTH), bf16), pltpu.VMEM((2, GROUP, WIDTH), bf16)]
-        + [pltpu.SemaphoreType.DMA((12,)), pltpu.SemaphoreType.DMA((2,))],
-        limit=LARGE,
-        outside=range(1, 13),
-        outputs_outside=True,
-    )
-
     scratch = [pltpu.VMEM((2 * CHUNK, WIDTH), bf16)]
     (summed,) = call(gather_kernel, [shape(SOURCES, 5 * FROM_ONE, 256)], [arrived], scratch)
     combined, gate_grad = call(
@@ -355,6 +379,27 @@
         [within_z(summed), cotangent, chosen, gates],
         [pltpu.VMEM((SOURCES * PADDED, WIDTH), bf16)],
     )
+    up_one, combined = lax.optimization_barrier((up_one, combined))
+
+    exponent = (LAYERS - 1 - layer_index).astype(f32)
+    factor = jnp.power(f32(DECAY_RATE), exponent)
+    steps = []
+    for parts in (
+        (first_up[0].T, second_up[0].T, up_own, own_up, up_one, up_sum),
+        (first_down[0], second_down[0], down_own, own_down, down_one, down_sum),
+    ):
+        steps += call(
+            step_kernel,
+            [weight],
+            [factor, *parts],
+            [pltpu.VMEM((6, GROUP, WIDTH), bf16), pltpu.VMEM((GROUP, WIDTH), bf16)]
+            + [pltpu.SemaphoreType.DMA((6,)), pltpu.SemaphoreType.DMA((2,))],
+            limit=LARGE,
+            outside=range(1, 7),
+            outputs_outside=True,
+        )
+    step_up, step_down = steps
+
     return (combined, gate_grad.transpose(1, 2, 0), step_up.T[None], step_down[None])
 
 

time: 152 us -> 158 us (1.039); the launches traced: 151 us -> 155 us
  Pallas kernels: 22.7 us -> 28.3 us
  waiting for transfers between devices: 38.9 us -> 35.3 us
    pallas_call x6 -> x8, Pallas kernels: 22.7 us -> 28.3 us  [call(): pl.pallas_call(kernel, out_shape=shapes, in_specs=[scalar if a.ndim == 1...]
    all_to_all x2, waiting for transfers between devices: 7.27 us -> 2.63 us  [along_z(): lax.all_to_all(rows, ('zlo', 'zhi'), split_axis=0, concat_axis=0, tiled=T...]
    ppermute x12, waiting for transfers between devices: 28.5 us -> 32.7 us  [along_x(): lax.ppermute(values, 'x', [(i, (i + step) % RING) for i in range(RING)])]
    all_to_all x1, waiting for transfers between devices: 3.05 us -> 0.01 us  [within_z(): lax.all_to_all(rows, ('y', 'core'), split_axis=0, concat_axis=0, tiled=True)]
  transfers between devices with their start and end apart: 15 -> 15, of which waited for: 9 -> 6; matrix products, arithmetic and copies ran while one was open for 2% -> 1% of each run, Pallas kernels for 4% -> 8%
where the time goes in v5:
time: 158 us; the launch traced here: 155 us
  starting transfers between devices  58.9 us (37%)
  waiting for transfers between devices  35.3 us (22%)
  Pallas kernels  28.3 us (18%)
  blocking collectives  26.9 us (17%)
  local copies, waits for them, and re-layouts  2.5 us (2%)
  between operations  1.73 us (1%)
    ppermute x12, starting transfers between devices, along_x(): lax.ppermute(values, 'x', [(i, (i + step) % RING) for i in range(RING)])  38.5 us
    ppermute x12, waiting for transfers between devices, along_x(): lax.ppermute(values, 'x', [(i, (i + step) % RING) for i in range(RING)])  32.7 us
    pallas_call x8, Pallas kernels, call(): pl.pallas_call(kernel, out_shape=shapes, in_specs=[scalar if a.ndim == 1...  28.3 us
    all_to_all x1, blocking collectives, within_z(): lax.all_to_all(rows, ('y', 'core'), split_axis=0, concat_axis=0, tiled=True)  26.9 us
    all_to_all x2, starting transfers between devices, along_z(): lax.all_to_all(rows, ('zlo', 'zhi'), split_axis=0, concat_axis=0, tiled=T...  15.1 us
    all_to_all x1, starting transfers between devices, within_z(): lax.all_to_all(rows, ('y', 'core'), split_axis=0, concat_axis=0, tiled=True)  5.26 us
  transfers between devices with their start and end apart: 15, of which 6 were waited for; matrix products, arithmetic and copies ran while one was open for 1% of the time, Pallas kernels for 8%

profile of v5, /device:TPU:1, one launch (start us, length us, event | category | flops | bytes accessed | tf_op | source)
XLA Modules:
  0.0 154.9 jit_solution(2712681297555009269)
XLA Ops:
  0.6 2.9 %shard_map.138 = bf16[16,24,640]{2,1,0:T(8,128)(2,1)} custom-call(bf16[48,1280]{1,0:T(8,128)(2,1)} %tokens.1, bf16[48,1280]{1,0:T(8,128)(2,1)} %cotangent.3, s32[3,1,32]{2,1,0:T(1,128)} %bitcast.19, f32[3,1,32]{2,1,0:T(1,128)} %bitcast.21), custom_call_target="tpu_custom_call" | custom-call | bytes 738048 | tf_op jit(solution)/shard_map/pallas_call | solution.py:57
  3.5 26.9 %all_to_all.20.arrived = bf16[16,24,640]{2,1,0:T(8,128)(2,1)S(1)} all-to-all(bf16[16,24,640]{2,1,0:T(8,128)(2,1)} %shard_map.138), channel_id=1, replica_groups=mesh['zlo'=4,'x'=4,'zhi'=2,'y'=8,'core'=2] {'y','core'}, dimensions={0} | all-to-all | bytes 983040 | tf_op jit(solution)/shard_map/all_to_all | solution.py:289
  30.4 1.7 %shard_map.139 = bf16[8,96,1280]{2,1,0:T(8,128)(2,1)} custom-call(bf16[16,24,640]{2,1,0:T(8,128)(2,1)S(1)} %all_to_all.20.arrived), custom_call_target="tpu_custom_call" | custom-call | bytes 2457600 | tf_op jit(solution)/shard_map/pallas_call | solution.py:57
  32.1 0.0 copy-start.4
  32.1 0.0 copy-start.5
  32.1 8.5 %all-to-all-start.1 = ((bf16[8,96,1280]{2,1,0:T(8,128)(2,1)}), bf16[8,96,1280]{2,1,0:T(8,128)(2,1)}, u32[]{:S(2)}, u32[]{:S(2)}) async-start(bf16[8,96,1280]{2,1,0:T(8,128)(2,1)} %shard_map.139), calls=%async_computation.1 | async-start | bytes 3932160 | tf_op jit(solution)/shard_map/all_to_all | solution.py:293
  40.6 0.0 copy-done.4
  40.6 4.4 %collective-permute-start.1 = (bf16[224,1280]{1,0:T(8,128)(2,1)S(1)}, bf16[224,1280]{1,0:T(8,128)(2,1)S(1)}, u32[]{:S(2)}, u32[]{:S(2)}) collective-permute-start(bf16[224,1280]{1,0:T(8,128)(2,1)S(1)} %bitcast.26), channel_id=1, source_target_pairs={{0,96},{32,0},{64,32},{96,64},{1,97},{33,1},{65,33},{97,65},{2,98}... | collective-permute-start | bytes 1720328 | tf_op jit(solution)/shard_map/ppermute | solution.py:285
  45.0 0.0 copy-done.5
  45.1 1.9 %collective-permute-start.2 = (bf16[224,1280]{1,0:T(8,128)(2,1)S(1)}, bf16[224,1280]{1,0:T(8,128)(2,1)S(1)}, u32[]{:S(2)}, u32[]{:S(2)}) collective-permute-start(bf16[224,1280]{1,0:T(8,128)(2,1)S(1)} %bitcast.32), channel_id=1, source_target_pairs={{0,32},{32,64},{64,96},{96,0},{1,33},{33,65},{65,97},{97,1},{2,34}... | collective-permute-start | bytes 1720328 | tf_op jit(solution)/shard_map/ppermute | solution.py:285
  47.0 2.1 %collective-permute-start = (bf16[224,1280]{1,0:T(8,128)(2,1)S(1)}, bf16[224,1280]{1,0:T(8,128)(2,1)S(1)}, u32[]{:S(2)}, u32[]{:S(2)}) collective-permute-start(bf16[224,1280]{1,0:T(8,128)(2,1)S(1)} %bitcast.27), channel_id=1, source_target_pairs={{0,32},{32,64},{64,96},{96,0},{1,33},{33,65},{65,97},{97,1},{2,34}... | collective-permute-start | bytes 1720328 | tf_op jit(solution)/shard_map/ppermute | solution.py:285
  49.1 4.4 %collective-permute-start.4 = (bf16[224,1280]{1,0:T(8,128)(2,1)S(1)}, bf16[224,1280]{1,0:T(8,128)(2,1)S(1)}, u32[]{:S(2)}, u32[]{:S(2)}) collective-permute-start(bf16[224,1280]{1,0:T(8,128)(2,1)S(1)} %bitcast.33), channel_id=1, source_target_pairs={{0,96},{32,0},{64,32},{96,64},{1,97},{33,1},{65,33},{97,65},{2,98}... | collective-permute-start | bytes 1720328 | tf_op jit(solution)/shard_map/ppermute | solution.py:285
  53.5 4.3 %collective-permute-done.1.args_6_.args_1_ = bf16[224,1280]{1,0:T(8,128)(2,1)S(1)} collective-permute-done((bf16[224,1280]{1,0:T(8,128)(2,1)S(1)}, bf16[224,1280]{1,0:T(8,128)(2,1)S(1)}, u32[]{:S(2)}, u32[]{:S(2)}) %collective-permute-start.1) | collective-permute-done | bytes 573472 | tf_op jit(solution)/shard_map/ppermute | solution.py:285
  57.8 0.0 copy-start.8
  57.8 5.4 %collective-permute-start.5 = (bf16[224,1280]{1,0:T(8,128)(2,1)S(1)}, bf16[224,1280]{1,0:T(8,128)(2,1)S(1)}, u32[]{:S(2)}, u32[]{:S(2)}) collective-permute-start(bf16[224,1280]{1,0:T(8,128)(2,1)S(1)} %collective-permute-done.1.args_6_.args_1_), channel_id=1, source_target_pairs={{0,96},{32,0},{64,32},{96,64},{1,97},{33,1},{65,33},{97,65},{2,98}... | collective-permute-start | bytes 1720328 | tf_op jit(solution)/shard_map/ppermute | solution.py:285
  63.2 0.0 collective-permute-done.2.args_1_
  63.3 0.0 copy-start.10
  63.3 1.9 %collective-permute-start.3 = (bf16[224,1280]{1,0:T(8,128)(2,1)S(1)}, bf16[224,1280]{1,0:T(8,128)(2,1)S(1)}, u32[]{:S(2)}, u32[]{:S(2)}) collective-permute-start(bf16[224,1280]{1,0:T(8,128)(2,1)S(1)} %collective-permute-done.2.args_1_), channel_id=1, source_target_pairs={{0,32},{32,64},{64,96},{96,0},{1,33},{33,65},{65,97},{97,1},{2,34}... | collective-permute-start | bytes 1720328 | tf_op jit(solution)/shard_map/ppermute | solution.py:285
  65.2 10.3 %collective-permute-done.args_5_.args_0_ = bf16[224,1280]{1,0:T(8,128)(2,1)S(1)} collective-permute-done((bf16[224,1280]{1,0:T(8,128)(2,1)S(1)}, bf16[224,1280]{1,0:T(8,128)(2,1)S(1)}, u32[]{:S(2)}, u32[]{:S(2)}) %collective-permute-start) | collective-permute-done | bytes 573472 | tf_op jit(solution)/shard_map/ppermute | solution.py:285
  75.4 0.0 copy-start.9
  75.4 0.0 collective-permute-done.4.args_2_
  75.4 0.0 copy-start.11
  75.4 6.6 %collective-permute-done.5.args_4_ = bf16[224,1280]{1,0:T(8,128)(2,1)S(1)} collective-permute-done((bf16[224,1280]{1,0:T(8,128)(2,1)S(1)}, bf16[224,1280]{1,0:T(8,128)(2,1)S(1)}, u32[]{:S(2)}, u32[]{:S(2)}) %collective-permute-start.5) | collective-permute-done | bytes 573472 | tf_op jit(solution)/shard_map/ppermute | solution.py:285
  82.0 0.0 copy-done.10
  82.1 0.0 copy-done.11
  82.1 0.0 copy-start.12
  82.1 0.8 copy-done.12
  82.9 4.7 %collective-permute-done.3.args_0_ = bf16[224,1280]{1,0:T(8,128)(2,1)S(1)} collective-permute-done((bf16[224,1280]{1,0:T(8,128)(2,1)S(1)}, bf16[224,1280]{1,0:T(8,128)(2,1)S(1)}, u32[]{:S(2)}, u32[]{:S(2)}) %collective-permute-start.3) | collective-permute-done | bytes 573472 | tf_op jit(solution)/shard_map/ppermute | solution.py:285
  87.6 0.0 copy-done.8
  87.6 0.0 copy-done.9
  87.6 0.0 all-to-all-done.1.arrived
  87.6 7.4 %shard_map.140 = (bf16[224,1280]{1,0:T(8,128)(2,1)S(1)}, bf16[224,1280]{1,0:T(8,128)(2,1)S(1)}, bf16[4,224,384]{2,1,0:T(8,128)(2,1)}, f32[4,224,384]{2,1,0:T(8,128)}, bf16[8,48,1280]{2,1,0:T(8,128)(2,1)}) custom-call(bf16[8,96,1280]{2,1,0:T(8,128)(2,1)} %all-to-all-done.1.arrived, bf16[224,1280]{1,0:T(8,128)(2,1)S(1)} %collective-permute-done.3.args_0_, ...), custom_call_target="tpu_custom_call" | custom-call | flops 2422210560 | bytes 10747904 | tf_op jit(solution)/shard_map/pallas_call | solution.py:57
  95.0 1.9 %collective-permute-start.7 = (bf16[224,1280]{1,0:T(8,128)(2,1)S(1)}, bf16[224,1280]{1,0:T(8,128)(2,1)S(1)}, u32[]{:S(2)}, u32[]{:S(2)}) collective-permute-start(bf16[224,1280]{1,0:T(8,128)(2,1)S(1)} %get-tuple-element.31), channel_id=1, source_target_pairs={{0,32},{32,64},{64,96},{96,0},{1,33},{33,65},{65,97},{97,1},{2,34}... | collective-permute-start | bytes 1720328 | tf_op jit(solution)/shard_map/ppermute | solution.py:285
  97.0 4.5 %collective-permute-start.8 = (bf16[224,1280]{1,0:T(8,128)(2,1)S(1)}, bf16[224,1280]{1,0:T(8,128)(2,1)S(1)}, u32[]{:S(2)}, u32[]{:S(2)}) collective-permute-start(bf16[224,1280]{1,0:T(8,128)(2,1)S(1)} %get-tuple-element.32), channel_id=1, source_target_pairs={{0,96},{32,0},{64,32},{96,64},{1,97},{33,1},{65,33},{97,65},{2,98}... | collective-permute-start | bytes 1720328 | tf_op jit(solution)/shard_map/ppermute | solution.py:285
  101.6 6.6 %all-to-all-start.2 = ((bf16[8,48,1280]{2,1,0:T(8,128)(2,1)}), bf16[8,48,1280]{2,1,0:T(8,128)(2,1)S(1)}, u32[]{:S(2)}, u32[]{:S(2)}) async-start(bf16[8,48,1280]{2,1,0:T(8,128)(2,1)} %get-tuple-element.24), calls=%async_computation.2 | async-start | bytes 1966080 | tf_op jit(solution)/shard_map/all_to_all | solution.py:293
  108.1 6.6 %shard_map.141 = (bf16[224,1280]{1,0:T(8,128)(2,1)}, bf16[224,1280]{1,0:T(8,128)(2,1)}, bf16[224,1280]{1,0:T(8,128)(2,1)}, bf16[224,1280]{1,0:T(8,128)(2,1)}, bf...) custom-call(bf16[8,96,1280]{2,1,0:T(8,128)(2,1)} %all-to-all-done.1.arrived, bf16[224,1280]{1,0:T(8,128)(2,1)} %copy-done.9, ...), custom_call_target="tpu_custom_call" | custom-call | flops 1981808640 | bytes 9191424 | tf_op jit(solution)/shard_map/pallas_call | solution.py:57
  114.7 0.0 copy-start.3
  114.7 2.1 %collective-permute-start.10 = (bf16[224,1280]{1,0:T(8,128)(2,1)}, bf16[224,1280]{1,0:T(8,128)(2,1)}, u32[]{:S(2)}, u32[]{:S(2)}) collective-permute-start(bf16[224,1280]{1,0:T(8,128)(2,1)} %get-tuple-element.35), channel_id=1, source_target_pairs={{0,32},{32,64},{64,96},{96,0},{1,33},{33,65},{65,97},{97,1},{2,34}... | collective-permute-start | bytes 1720328 | tf_op jit(solution)/shard_map/ppermute | solution.py:285
  116.8 4.6 %collective-permute-start.6 = (bf16[224,1280]{1,0:T(8,128)(2,1)}, bf16[224,1280]{1,0:T(8,128)(2,1)}, u32[]{:S(2)}, u32[]{:S(2)}) collective-permute-start(bf16[224,1280]{1,0:T(8,128)(2,1)} %get-tuple-element.23), channel_id=1, source_target_pairs={{0,96},{32,0},{64,32},{96,64},{1,97},{33,1},{65,33},{97,65},{2,98}... | collective-permute-start | bytes 1720328 | tf_op jit(solution)/shard_map/ppermute | solution.py:285
  121.3 0.0 collective-permute-done.7
  121.3 0.0 collective-permute-done.8
  121.4 1.2 add_convert_fusion
  122.6 1.9 %collective-permute-start.11 = (bf16[224,1280]{1,0:T(8,128)(2,1)S(1)}, bf16[224,1280]{1,0:T(8,128)(2,1)S(1)}, u32[]{:S(2)}, u32[]{:S(2)}) collective-permute-start(bf16[224,1280]{1,0:T(8,128)(2,1)S(1)} %add_convert_fusion), channel_id=1, source_target_pairs={{0,96},{32,0},{64,32},{96,64},{1,97},{33,1},{65,33},{97,65},{2,98}... | collective-permute-start | bytes 1720328 | tf_op jit(solution)/shard_map/ppermute | solution.py:285
  124.5 0.0 copy-done.3
  124.5 0.1 add_convert_fusion.1
  124.6 3.4 %collective-permute-start.9 = (bf16[224,1280]{1,0:T(8,128)(2,1)S(1)}, bf16[224,1280]{1,0:T(8,128)(2,1)S(1)}, u32[]{:S(2)}, u32[]{:S(2)}) collective-permute-start(bf16[224,1280]{1,0:T(8,128)(2,1)S(1)} %add_convert_fusion.1), channel_id=1, source_target_pairs={{0,32},{32,64},{64,96},{96,0},{1,33},{33,65},{65,97},{97,1},{2,34}... | collective-permute-start | bytes 1720328 | tf_op jit(solution)/shard_map/ppermute | solution.py:285
  128.0 2.6 %all-to-all-done.2.arrived = bf16[8,48,1280]{2,1,0:T(8,128)(2,1)S(1)} async-done(((bf16[8,48,1280]{2,1,0:T(8,128)(2,1)}), bf16[8,48,1280]{2,1,0:T(8,128)(2,1)S(1)}, u32[]{:S(2)}, u32[]{:S(2)}) %all-to-all-start.2) | async-done | bytes 983072 | tf_op jit(solution)/shard_map/all_to_all | solution.py:293
  130.6 1.0 shard_map.142
  131.6 5.3 %all-to-all-start.3 = ((bf16[16,30,256]{2,1,0:T(8,128)(2,1)}), bf16[16,30,256]{2,1,0:T(8,128)(2,1)S(1)}, u32[]{:S(2)}, u32[]{:S(2)}) async-start(bf16[16,30,256]{2,1,0:T(8,128)(2,1)} %shard_map.142), calls=%async_computation.3 | async-start | bytes 524288 | tf_op jit(solution)/shard_map/all_to_all | solution.py:289
  137.6 0.0 collective-permute-done.10.args_4_
  137.6 6.7 %collective-permute-done.11.args_5_ = bf16[224,1280]{1,0:T(8,128)(2,1)S(1)} collective-permute-done((bf16[224,1280]{1,0:T(8,128)(2,1)S(1)}, bf16[224,1280]{1,0:T(8,128)(2,1)S(1)}, u32[]{:S(2)}, u32[]{:S(2)}) %collective-permute-start.11) | collective-permute-done | bytes 573472 | tf_op jit(solution)/shard_map/ppermute | solution.py:285
  144.4 0.0 copy-start.7
  144.4 0.8 copy-done.7
  145.2 0.0 copy-start
  145.2 3.8 %shard_map.145 = bf16[224,1280]{1,0:T(8,128)(2,1)} custom-call(f32[1]{0:T(128)S(6)} %pow.3.factor, bf16[224,1280]{1,0:T(8,128)(2,1)} %bitcast.28, bf16[224,1280]{1,0:T(8,128)(2,1)} %bitcast.29, bf16[224,1280]{1,0:T(8,128)(2,1)} %bitcast.25, bf16[224,1280]{1,0:T(8,128)(2,1)} %get-tuple-element.34.args_3_, bf16[224,1280]{1,0:T(8,128)(2,1)} %collective-permute-done.10.args_4_, ...), custom_call_target="tpu_custom_call" | custom-call | bytes 4014084 | tf_op jit(solution)/shard_map/pallas_call | solution.py:57
  148.9 0.0 all-to-all-done.3.returned
  148.9 0.0 copy-done
  149.0 0.0 copy-done.1
  149.0 0.0 copy-done.2
  149.0 1.2 shard_map.143
  150.2 0.0 collective-permute-done.6.args_4_
  150.2 0.0 collective-permute-done.9.args_5_
  150.2 0.8 copy-done.6
  151.0 3.7 %shard_map.144 = bf16[224,1280]{1,0:T(8,128)(2,1)} custom-call(f32[1]{0:T(128)S(6)} %pow.3.factor, bf16[224,1280]{1,0:T(8,128)(2,1)} %bitcast.34, bf16[224,1280]{1,0:T(8,128)(2,1)} %bitcast.35, bf16[224,1280]{1,0:T(8,128)(2,1)} %bitcast.31, bf16[224,1280]{1,0:T(8,128)(2,1)} %get-tuple-element.28.args_3_, bf16[224,1280]{1,0:T(8,128)(2,1)} %collective-permute-done.6.args_4_, ...), custom_call_target="tpu_custom_call" | custom-call | bytes 4014084 | tf_op jit(solution)/shard_map/pallas_call | solution.py:57
  (3 shorter events, 0.0 us)
Async XLA Ops:
  32.1 8.5 %copy-start.4 = (bf16[1,224,1280]{2,1,0:T(8,128)(2,1)S(1)}, bf16[1,224,1280]{2,1,0:T(8,128)(2,1)}, u32[]{:S(2)}) copy-start(bf16[1,224,1280]{2,1,0:T(8,128)(2,1)} %param.16) | copy-start | bytes 1720324
  32.1 12.9 %copy-start.5 = (bf16[1,1280,224]{1,2,0:T(8,128)(2,1)S(1)}, bf16[1,1280,224]{1,2,0:T(8,128)(2,1)}, u32[]{:S(2)}) copy-start(bf16[1,1280,224]{1,2,0:T(8,128)(2,1)} %param.15) | copy-start | bytes 1720324
  32.1 55.5 %all-to-all-start.1 = ((bf16[8,96,1280]{2,1,0:T(8,128)(2,1)}), bf16[8,96,1280]{2,1,0:T(8,128)(2,1)}, u32[]{:S(2)}, u32[]{:S(2)}) async-start(bf16[8,96,1280]{2,1,0:T(8,128)(2,1)} %shard_map.139), calls=%async_computation.1 | async-start | bytes 3932160 | tf_op jit(solution)/shard_map/all_to_all | solution.py:293
  40.6 17.2 %collective-permute-start.1 = (bf16[224,1280]{1,0:T(8,128)(2,1)S(1)}, bf16[224,1280]{1,0:T(8,128)(2,1)S(1)}, u32[]{:S(2)}, u32[]{:S(2)}) collective-permute-start(bf16[224,1280]{1,0:T(8,128)(2,1)S(1)} %bitcast.26), channel_id=1, source_target_pairs={{0,96},{32,0},{64,32},{96,64},{1,97},{33,1},{65,33},{97,65},{2,98}... | collective-permute-start | bytes 1720328 | tf_op jit(solution)/shard_map/ppermute | solution.py:285
  45.1 18.2 %collective-permute-start.2 = (bf16[224,1280]{1,0:T(8,128)(2,1)S(1)}, bf16[224,1280]{1,0:T(8,128)(2,1)S(1)}, u32[]{:S(2)}, u32[]{:S(2)}) collective-permute-start(bf16[224,1280]{1,0:T(8,128)(2,1)S(1)} %bitcast.32), channel_id=1, source_target_pairs={{0,32},{32,64},{64,96},{96,0},{1,33},{33,65},{65,97},{97,1},{2,34}... | collective-permute-start | bytes 1720328 | tf_op jit(solution)/shard_map/ppermute | solution.py:285
  47.0 28.5 %collective-permute-start = (bf16[224,1280]{1,0:T(8,128)(2,1)S(1)}, bf16[224,1280]{1,0:T(8,128)(2,1)S(1)}, u32[]{:S(2)}, u32[]{:S(2)}) collective-permute-start(bf16[224,1280]{1,0:T(8,128)(2,1)S(1)} %bitcast.27), channel_id=1, source_target_pairs={{0,32},{32,64},{64,96},{96,0},{1,33},{33,65},{65,97},{97,1},{2,34}... | collective-permute-start | bytes 1720328 | tf_op jit(solution)/shard_map/ppermute | solution.py:285
  49.1 26.4 %collective-permute-start.4 = (bf16[224,1280]{1,0:T(8,128)(2,1)S(1)}, bf16[224,1280]{1,0:T(8,128)(2,1)S(1)}, u32[]{:S(2)}, u32[]{:S(2)}) collective-permute-start(bf16[224,1280]{1,0:T(8,128)(2,1)S(1)} %bitcast.33), channel_id=1, source_target_pairs={{0,96},{32,0},{64,32},{96,64},{1,97},{33,1},{65,33},{97,65},{2,98}... | collective-permute-start | bytes 1720328 | tf_op jit(solution)/shard_map/ppermute | solution.py:285
  57.8 29.8 %copy-start.8 = (bf16[224,1280]{1,0:T(8,128)(2,1)}, bf16[224,1280]{1,0:T(8,128)(2,1)S(1)}, u32[]{:S(2)}) copy-start(bf16[224,1280]{1,0:T(8,128)(2,1)S(1)} %collective-permute-done.1.args_6_.args_1_) | copy-start | bytes 1720324
  57.8 24.2 %collective-permute-start.5 = (bf16[224,1280]{1,0:T(8,128)(2,1)S(1)}, bf16[224,1280]{1,0:T(8,128)(2,1)S(1)}, u32[]{:S(2)}, u32[]{:S(2)}) collective-permute-start(bf16[224,1280]{1,0:T(8,128)(2,1)S(1)} %collective-permute-done.1.args_6_.args_1_), channel_id=1, source_target_pairs={{0,96},{32,0},{64,32},{96,64},{1,97},{33,1},{65,33},{97,65},{2,98}... | collective-permute-start | bytes 1720328 | tf_op jit(solution)/shard_map/ppermute | solution.py:285
  63.3 18.8 %copy-start.10 = (bf16[224,1280]{1,0:T(8,128)(2,1)}, bf16[224,1280]{1,0:T(8,128)(2,1)S(1)}, u32[]{:S(2)}) copy-start(bf16[224,1280]{1,0:T(8,128)(2,1)S(1)} %collective-permute-done.2.args_1_) | copy-start | bytes 1720324
  63.3 24.3 %collective-permute-start.3 = (bf16[224,1280]{1,0:T(8,128)(2,1)S(1)}, bf16[224,1280]{1,0:T(8,128)(2,1)S(1)}, u32[]{:S(2)}, u32[]{:S(2)}) collective-permute-start(bf16[224,1280]{1,0:T(8,128)(2,1)S(1)} %collective-permute-done.2.args_1_), channel_id=1, source_target_pairs={{0,32},{32,64},{64,96},{96,0},{1,33},{33,65},{65,97},{97,1},{2,34}... | collective-permute-start | bytes 1720328 | tf_op jit(solution)/shard_map/ppermute | solution.py:285
  75.4 12.2 %copy-start.9 = (bf16[224,1280]{1,0:T(8,128)(2,1)}, bf16[224,1280]{1,0:T(8,128)(2,1)S(1)}, u32[]{:S(2)}) copy-start(bf16[224,1280]{1,0:T(8,128)(2,1)S(1)} %collective-permute-done.args_5_.args_0_) | copy-start | bytes 1720324
  75.4 6.6 %copy-start.11 = (bf16[224,1280]{1,0:T(8,128)(2,1)}, bf16[224,1280]{1,0:T(8,128)(2,1)S(1)}, u32[]{:S(2)}) copy-start(bf16[224,1280]{1,0:T(8,128)(2,1)S(1)} %collective-permute-done.4.args_2_) | copy-start | bytes 1720324
  82.1 0.8 copy-start.12
  95.0 26.3 %collective-permute-start.7 = (bf16[224,1280]{1,0:T(8,128)(2,1)S(1)}, bf16[224,1280]{1,0:T(8,128)(2,1)S(1)}, u32[]{:S(2)}, u32[]{:S(2)}) collective-permute-start(bf16[224,1280]{1,0:T(8,128)(2,1)S(1)} %get-tuple-element.31), channel_id=1, source_target_pairs={{0,32},{32,64},{64,96},{96,0},{1,33},{33,65},{65,97},{97,1},{2,34}... | collective-permute-start | bytes 1720328 | tf_op jit(solution)/shard_map/ppermute | solution.py:285
  97.0 24.3 %collective-permute-start.8 = (bf16[224,1280]{1,0:T(8,128)(2,1)S(1)}, bf16[224,1280]{1,0:T(8,128)(2,1)S(1)}, u32[]{:S(2)}, u32[]{:S(2)}) collective-permute-start(bf16[224,1280]{1,0:T(8,128)(2,1)S(1)} %get-tuple-element.32), channel_id=1, source_target_pairs={{0,96},{32,0},{64,32},{96,64},{1,97},{33,1},{65,33},{97,65},{2,98}... | collective-permute-start | bytes 1720328 | tf_op jit(solution)/shard_map/ppermute | solution.py:285
  101.6 29.1 %all-to-all-start.2 = ((bf16[8,48,1280]{2,1,0:T(8,128)(2,1)}), bf16[8,48,1280]{2,1,0:T(8,128)(2,1)S(1)}, u32[]{:S(2)}, u32[]{:S(2)}) async-start(bf16[8,48,1280]{2,1,0:T(8,128)(2,1)} %get-tuple-element.24), calls=%async_computation.2 | async-start | bytes 1966080 | tf_op jit(solution)/shard_map/all_to_all | solution.py:293
  114.7 9.8 %copy-start.3 = (bf16[224,1280]{1,0:T(8,128)(2,1)S(1)}, bf16[224,1280]{1,0:T(8,128)(2,1)}, u32[]{:S(2)}) copy-start(bf16[224,1280]{1,0:T(8,128)(2,1)} %get-tuple-element.30) | copy-start | bytes 1720324
  114.7 22.9 %collective-permute-start.10 = (bf16[224,1280]{1,0:T(8,128)(2,1)}, bf16[224,1280]{1,0:T(8,128)(2,1)}, u32[]{:S(2)}, u32[]{:S(2)}) collective-permute-start(bf16[224,1280]{1,0:T(8,128)(2,1)} %get-tuple-element.35), channel_id=1, source_target_pairs={{0,32},{32,64},{64,96},{96,0},{1,33},{33,65},{65,97},{97,1},{2,34}... | collective-permute-start | bytes 1720328 | tf_op jit(solution)/shard_map/ppermute | solution.py:285
  116.8 33.5 %collective-permute-start.6 = (bf16[224,1280]{1,0:T(8,128)(2,1)}, bf16[224,1280]{1,0:T(8,128)(2,1)}, u32[]{:S(2)}, u32[]{:S(2)}) collective-permute-start(bf16[224,1280]{1,0:T(8,128)(2,1)} %get-tuple-element.23), channel_id=1, source_target_pairs={{0,96},{32,0},{64,32},{96,64},{1,97},{33,1},{65,33},{97,65},{2,98}... | collective-permute-start | bytes 1720328 | tf_op jit(solution)/shard_map/ppermute | solution.py:285
  122.6 21.8 %collective-permute-start.11 = (bf16[224,1280]{1,0:T(8,128)(2,1)S(1)}, bf16[224,1280]{1,0:T(8,128)(2,1)S(1)}, u32[]{:S(2)}, u32[]{:S(2)}) collective-permute-start(bf16[224,1280]{1,0:T(8,128)(2,1)S(1)} %add_convert_fusion), channel_id=1, source_target_pairs={{0,96},{32,0},{64,32},{96,64},{1,97},{33,1},{65,33},{97,65},{2,98}... | collective-permute-start | bytes 1720328 | tf_op jit(solution)/shard_map/ppermute | solution.py:285
  124.6 25.6 %collective-permute-start.9 = (bf16[224,1280]{1,0:T(8,128)(2,1)S(1)}, bf16[224,1280]{1,0:T(8,128)(2,1)S(1)}, u32[]{:S(2)}, u32[]{:S(2)}) collective-permute-start(bf16[224,1280]{1,0:T(8,128)(2,1)S(1)} %add_convert_fusion.1), channel_id=1, source_target_pairs={{0,32},{32,64},{64,96},{96,0},{1,33},{33,65},{65,97},{97,1},{2,34}... | collective-permute-start | bytes 1720328 | tf_op jit(solution)/shard_map/ppermute | solution.py:285
  131.6 17.3 %all-to-all-start.3 = ((bf16[16,30,256]{2,1,0:T(8,128)(2,1)}), bf16[16,30,256]{2,1,0:T(8,128)(2,1)S(1)}, u32[]{:S(2)}, u32[]{:S(2)}) async-start(bf16[16,30,256]{2,1,0:T(8,128)(2,1)} %shard_map.142), calls=%async_computation.3 | async-start | bytes 524288 | tf_op jit(solution)/shard_map/all_to_all | solution.py:289
  144.4 0.8 copy-start.7
  145.2 3.8 %copy-start = (bf16[48,1280]{1,0:T(8,128)(2,1)S(1)}, bf16[48,1280]{1,0:T(8,128)(2,1)}, u32[]{:S(2)}) copy-start(bf16[48,1280]{1,0:T(8,128)(2,1)} %cotangent.3) | copy-start | bytes 368644
  145.2 3.8 %copy-start.1 = (s32[1,32,3]{1,0,2:T(1,128)S(1)}, s32[1,32,3]{1,0,2:T(1,128)}, u32[]{:S(2)}) copy-start(s32[1,32,3]{1,0,2:T(1,128)} %param.13) | copy-start | bytes 1156
  145.2 3.8 %copy-start.2 = (f32[1,32,3]{1,0,2:T(1,128)S(1)}, f32[1,32,3]{1,0,2:T(1,128)}, u32[]{:S(2)}) copy-start(f32[1,32,3]{1,0,2:T(1,128)} %param.14) | copy-start | bytes 1156
  150.2 0.8 copy-start.6

commit v6 on v5

--- a/solution.py
+++ b/solution.py
@@ -39,11 +39,12 @@
     return (mean / (jnp.sqrt(square) + EPSILON) + decay).astype(jnp.bfloat16)
 
 
-def contract(left, right, left_dim, right_dim):
+def contract(left, right, left_dim, right_dim, precision=None):
     return lax.dot_general(
         left,
         right,
         (((left_dim,), (right_dim,)), ((), ())),
+        precision=precision,
         preferred_element_type=jnp.float32,
     )
 
@@ -371,16 +372,6 @@
     down_one = along_x(right_down, 1)
     up_sum = along_x((right_up.astype(f32) + up_two.astype(f32)).astype(bf16), 1)
     down_sum = along_x((left_down.astype(f32) + down_two.astype(f32)).astype(bf16), -1)
-    scratch = [pltpu.VMEM((2 * CHUNK, WIDTH), bf16)]
-    (summed,) = call(gather_kernel, [shape(SOURCES, 5 * FROM_ONE, 256)], [arrived], scratch)
-    combined, gate_grad = call(
-        combine_kernel,
-        [shape(tokens.shape[0], WIDTH), shape(PICKS, 1, EXPERTS, dtype=f32)],
-        [within_z(summed), cotangent, chosen, gates],
-        [pltpu.VMEM((SOURCES * PADDED, WIDTH), bf16)],
-    )
-    up_one, combined = lax.optimization_barrier((up_one, combined))
-
     exponent = (LAYERS - 1 - layer_index).astype(f32)
     factor = jnp.power(f32(DECAY_RATE), exponent)
     steps = []
@@ -400,6 +391,14 @@
         )
     step_up, step_down = steps
 
+    scratch = [pltpu.VMEM((2 * CHUNK, WIDTH), bf16)]
+    (summed,) = call(gather_kernel, [shape(SOURCES, 5 * FROM_ONE, 256)], [arrived], scratch)
+    combined, gate_grad = call(
+        combine_kernel,
+        [shape(tokens.shape[0], WIDTH), shape(PICKS, 1, EXPERTS, dtype=f32)],
+        [within_z(summed), cotangent, chosen, gates],
+        [pltpu.VMEM((SOURCES * PADDED, WIDTH), bf16)],
+    )
     return (combined, gate_grad.transpose(1, 2, 0), step_up.T[None], step_down[None])
 
 

time: 158 us -> 152 us (0.962)
  starting transfers between devices: 58.9 us -> 55.8 us
    ppermute x12, starting transfers between devices: 38.5 us -> 36.7 us  [along_x(): lax.ppermute(values, 'x', [(i, (i + step) % RING) for i in range(RING)])]
    ppermute x12, waiting for transfers between devices: 32.7 us -> 30.9 us  [along_x(): lax.ppermute(values, 'x', [(i, (i + step) % RING) for i in range(RING)])]
  transfers between devices with their start and end apart: 15 -> 15, of which waited for: 6 -> 7; matrix products, arithmetic and copies ran while one was open for 1% -> 1% of each run, Pallas kernels for 8% -> 10%
where the time goes in v6:
time: 152 us; the launch traced here: 150 us
  starting transfers between devices  55.8 us (37%)
  waiting for transfers between devices  34.7 us (23%)
  Pallas kernels  28.3 us (19%)
  blocking collectives  26.9 us (18%)
  local copies, waits for them, and re-layouts  1.67 us (1%)
  between operations  1.6 us (1%)
    ppermute x12, starting transfers between devices, along_x(): lax.ppermute(values, 'x', [(i, (i + step) % RING) for i in range(RING)])  36.7 us
    ppermute x12, waiting for transfers between devices, along_x(): lax.ppermute(values, 'x', [(i, (i + step) % RING) for i in range(RING)])  30.9 us
    pallas_call x8, Pallas kernels, call(): pl.pallas_call(kernel, out_shape=shapes, in_specs=[scalar if a.ndim == 1...  28.3 us
    all_to_all x1, blocking collectives, within_z(): lax.all_to_all(rows, ('y', 'core'), split_axis=0, concat_axis=0, tiled=True)  26.9 us
    all_to_all x2, starting transfers between devices, along_z(): lax.all_to_all(rows, ('zlo', 'zhi'), split_axis=0, concat_axis=0, tiled=T...  13.9 us
    all_to_all x1, starting transfers between devices, within_z(): lax.all_to_all(rows, ('y', 'core'), split_axis=0, concat_axis=0, tiled=True)  5.31 us
    all_to_all x2, waiting for transfers between devices, along_z(): lax.all_to_all(rows, ('zlo', 'zhi'), split_axis=0, concat_axis=0, tiled=T...  3.79 us
  transfers between devices with their start and end apart: 15, of which 7 were waited for; matrix products, arithmetic and copies ran while one was open for 1% of the time, Pallas kernels for 10%

profile of v6, /device:TPU:1, one launch (start us, length us, event | category | flops | bytes accessed | tf_op | source)
XLA Modules:
  0.0 150.3 jit_solution(14354960317899778946)
XLA Ops:
  0.6 2.9 %shard_map.138 = bf16[16,24,640]{2,1,0:T(8,128)(2,1)} custom-call(bf16[48,1280]{1,0:T(8,128)(2,1)} %tokens.1, bf16[48,1280]{1,0:T(8,128)(2,1)} %cotangent.3, s32[3,1,32]{2,1,0:T(1,128)} %bitcast.19, f32[3,1,32]{2,1,0:T(1,128)} %bitcast.21), custom_call_target="tpu_custom_call" | custom-call | bytes 738048 | tf_op jit(solution)/shard_map/pallas_call | solution.py:58
  3.5 26.9 %all_to_all.20.arrived = bf16[16,24,640]{2,1,0:T(8,128)(2,1)S(1)} all-to-all(bf16[16,24,640]{2,1,0:T(8,128)(2,1)} %shard_map.138), channel_id=1, replica_groups=mesh['zlo'=4,'x'=4,'zhi'=2,'y'=8,'core'=2] {'y','core'}, dimensions={0} | all-to-all | bytes 983040 | tf_op jit(solution)/shard_map/all_to_all | solution.py:290
  30.4 1.7 %shard_map.139 = bf16[8,96,1280]{2,1,0:T(8,128)(2,1)} custom-call(bf16[16,24,640]{2,1,0:T(8,128)(2,1)S(1)} %all_to_all.20.arrived), custom_call_target="tpu_custom_call" | custom-call | bytes 2457600 | tf_op jit(solution)/shard_map/pallas_call | solution.py:58
  32.1 0.0 copy-start.5
  32.1 0.0 copy-start.4
  32.1 8.5 %all-to-all-start.1 = ((bf16[8,96,1280]{2,1,0:T(8,128)(2,1)}), bf16[8,96,1280]{2,1,0:T(8,128)(2,1)}, u32[]{:S(2)}, u32[]{:S(2)}) async-start(bf16[8,96,1280]{2,1,0:T(8,128)(2,1)} %shard_map.139), calls=%async_computation.1 | async-start | bytes 3932160 | tf_op jit(solution)/shard_map/all_to_all | solution.py:294
  40.6 0.0 copy-done.5
  40.7 3.1 %collective-permute-start = (bf16[224,1280]{1,0:T(8,128)(2,1)S(1)}, bf16[224,1280]{1,0:T(8,128)(2,1)S(1)}, u32[]{:S(2)}, u32[]{:S(2)}) collective-permute-start(bf16[224,1280]{1,0:T(8,128)(2,1)S(1)} %bitcast.32), channel_id=1, source_target_pairs={{0,32},{32,64},{64,96},{96,0},{1,33},{33,65},{65,97},{97,1},{2,34}... | collective-permute-start | bytes 1720328 | tf_op jit(solution)/shard_map/ppermute | solution.py:286
  43.8 0.0 copy-done.4
  43.8 3.4 %collective-permute-start.3 = (bf16[224,1280]{1,0:T(8,128)(2,1)S(1)}, bf16[224,1280]{1,0:T(8,128)(2,1)S(1)}, u32[]{:S(2)}, u32[]{:S(2)}) collective-permute-start(bf16[224,1280]{1,0:T(8,128)(2,1)S(1)} %bitcast.26), channel_id=1, source_target_pairs={{0,96},{32,0},{64,32},{96,64},{1,97},{33,1},{65,33},{97,65},{2,98}... | collective-permute-start | bytes 1720328 | tf_op jit(solution)/shard_map/ppermute | solution.py:286
  47.2 3.2 %collective-permute-start.2 = (bf16[224,1280]{1,0:T(8,128)(2,1)S(1)}, bf16[224,1280]{1,0:T(8,128)(2,1)S(1)}, u32[]{:S(2)}, u32[]{:S(2)}) collective-permute-start(bf16[224,1280]{1,0:T(8,128)(2,1)S(1)} %bitcast.33), channel_id=1, source_target_pairs={{0,96},{32,0},{64,32},{96,64},{1,97},{33,1},{65,33},{97,65},{2,98}... | collective-permute-start | bytes 1720328 | tf_op jit(solution)/shard_map/ppermute | solution.py:286
  50.4 2.1 %collective-permute-start.5 = (bf16[224,1280]{1,0:T(8,128)(2,1)S(1)}, bf16[224,1280]{1,0:T(8,128)(2,1)S(1)}, u32[]{:S(2)}, u32[]{:S(2)}) collective-permute-start(bf16[224,1280]{1,0:T(8,128)(2,1)S(1)} %bitcast.27), channel_id=1, source_target_pairs={{0,32},{32,64},{64,96},{96,0},{1,33},{33,65},{65,97},{97,1},{2,34}... | collective-permute-start | bytes 1720328 | tf_op jit(solution)/shard_map/ppermute | solution.py:286
  52.5 6.4 %collective-permute-done.args_1_ = bf16[224,1280]{1,0:T(8,128)(2,1)S(1)} collective-permute-done((bf16[224,1280]{1,0:T(8,128)(2,1)S(1)}, bf16[224,1280]{1,0:T(8,128)(2,1)S(1)}, u32[]{:S(2)}, u32[]{:S(2)}) %collective-permute-start) | collective-permute-done | bytes 573472 | tf_op jit(solution)/shard_map/ppermute | solution.py:286
  58.9 0.0 copy-start.10
  58.9 1.9 %collective-permute-start.1 = (bf16[224,1280]{1,0:T(8,128)(2,1)S(1)}, bf16[224,1280]{1,0:T(8,128)(2,1)S(1)}, u32[]{:S(2)}, u32[]{:S(2)}) collective-permute-start(bf16[224,1280]{1,0:T(8,128)(2,1)S(1)} %collective-permute-done.args_1_), channel_id=1, source_target_pairs={{0,32},{32,64},{64,96},{96,0},{1,33},{33,65},{65,97},{97,1},{2,34}... | collective-permute-start | bytes 1720328 | tf_op jit(solution)/shard_map/ppermute | solution.py:286
  60.8 0.0 collective-permute-done.3.args_6_.args_1_
  60.8 0.0 copy-start.8
  60.8 4.6 %collective-permute-start.4 = (bf16[224,1280]{1,0:T(8,128)(2,1)S(1)}, bf16[224,1280]{1,0:T(8,128)(2,1)}, u32[]{:S(2)}, u32[]{:S(2)}) collective-permute-start(bf16[224,1280]{1,0:T(8,128)(2,1)S(1)} %collective-permute-done.3.args_6_.args_1_), channel_id=1, source_target_pairs={{0,96},{32,0},{64,32},{96,64},{1,97},{33,1},{65,33},{97,65},{2,98}... | collective-permute-start | bytes 1720328 | tf_op jit(solution)/shard_map/ppermute | solution.py:286
  65.4 7.7 %collective-permute-done.2.args_2_ = bf16[224,1280]{1,0:T(8,128)(2,1)S(1)} collective-permute-done((bf16[224,1280]{1,0:T(8,128)(2,1)S(1)}, bf16[224,1280]{1,0:T(8,128)(2,1)S(1)}, u32[]{:S(2)}, u32[]{:S(2)}) %collective-permute-start.2) | collective-permute-done | bytes 573472 | tf_op jit(solution)/shard_map/ppermute | solution.py:286
  73.1 0.0 copy-start.11
  73.1 0.0 collective-permute-done.5.args_5_.args_0_
  73.1 10.0 %collective-permute-done.1.args_0_ = bf16[224,1280]{1,0:T(8,128)(2,1)S(1)} collective-permute-done((bf16[224,1280]{1,0:T(8,128)(2,1)S(1)}, bf16[224,1280]{1,0:T(8,128)(2,1)S(1)}, u32[]{:S(2)}, u32[]{:S(2)}) %collective-permute-start.1) | collective-permute-done | bytes 573472 | tf_op jit(solution)/shard_map/ppermute | solution.py:286
  83.1 0.0 copy-done.10
  83.1 0.0 copy-done.11
  83.1 2.2 %collective-permute-done.4.args_4_ = bf16[224,1280]{1,0:T(8,128)(2,1)} collective-permute-done((bf16[224,1280]{1,0:T(8,128)(2,1)S(1)}, bf16[224,1280]{1,0:T(8,128)(2,1)}, u32[]{:S(2)}, u32[]{:S(2)}) %collective-permute-start.4) | collective-permute-done | bytes 573472 | tf_op jit(solution)/shard_map/ppermute | solution.py:286
  85.3 0.0 copy-done.8
  85.3 0.0 copy-done.9
  85.3 1.2 all-to-all-done.1.arrived
  86.5 7.4 %shard_map.140 = (bf16[224,1280]{1,0:T(8,128)(2,1)S(1)}, bf16[224,1280]{1,0:T(8,128)(2,1)S(1)}, bf16[4,224,384]{2,1,0:T(8,128)(2,1)}, f32[4,224,384]{2,1,0:T(8,128)}, bf16[8,48,1280]{2,1,0:T(8,128)(2,1)}) custom-call(bf16[8,96,1280]{2,1,0:T(8,128)(2,1)} %all-to-all-done.1.arrived, bf16[224,1280]{1,0:T(8,128)(2,1)S(1)} %collective-permute-done.1.args_0_, ...), custom_call_target="tpu_custom_call" | custom-call | flops 2422210560 | bytes 10747904 | tf_op jit(solution)/shard_map/pallas_call | solution.py:58
  93.9 3.1 %collective-permute-start.7 = (bf16[224,1280]{1,0:T(8,128)(2,1)S(1)}, bf16[224,1280]{1,0:T(8,128)(2,1)S(1)}, u32[]{:S(2)}, u32[]{:S(2)}) collective-permute-start(bf16[224,1280]{1,0:T(8,128)(2,1)S(1)} %get-tuple-element.27), channel_id=1, source_target_pairs={{0,32},{32,64},{64,96},{96,0},{1,33},{33,65},{65,97},{97,1},{2,34}... | collective-permute-start | bytes 1720328 | tf_op jit(solution)/shard_map/ppermute | solution.py:286
  97.0 3.4 %collective-permute-start.8 = (bf16[224,1280]{1,0:T(8,128)(2,1)S(1)}, bf16[224,1280]{1,0:T(8,128)(2,1)S(1)}, u32[]{:S(2)}, u32[]{:S(2)}) collective-permute-start(bf16[224,1280]{1,0:T(8,128)(2,1)S(1)} %get-tuple-element.28), channel_id=1, source_target_pairs={{0,96},{32,0},{64,32},{96,64},{1,97},{33,1},{65,33},{97,65},{2,98}... | collective-permute-start | bytes 1720328 | tf_op jit(solution)/shard_map/ppermute | solution.py:286
  100.4 5.4 %all-to-all-start.2 = ((bf16[8,48,1280]{2,1,0:T(8,128)(2,1)}), bf16[8,48,1280]{2,1,0:T(8,128)(2,1)S(1)}, u32[]{:S(2)}, u32[]{:S(2)}) async-start(bf16[8,48,1280]{2,1,0:T(8,128)(2,1)} %get-tuple-element.19), calls=%async_computation.2 | async-start | bytes 1966080 | tf_op jit(solution)/shard_map/all_to_all | solution.py:294
  105.8 6.6 %shard_map.143 = (bf16[224,1280]{1,0:T(8,128)(2,1)}, bf16[224,1280]{1,0:T(8,128)(2,1)}, bf16[224,1280]{1,0:T(8,128)(2,1)}, bf16[224,1280]{1,0:T(8,128)(2,1)}, bf...) custom-call(bf16[8,96,1280]{2,1,0:T(8,128)(2,1)} %all-to-all-done.1.arrived, bf16[224,1280]{1,0:T(8,128)(2,1)} %copy-done.9, ...), custom_call_target="tpu_custom_call" | custom-call | flops 1981808640 | bytes 9191424 | tf_op jit(solution)/shard_map/pallas_call | solution.py:58
  112.3 0.0 copy-start.3
  112.3 3.5 %collective-permute-start.6 = (bf16[224,1280]{1,0:T(8,128)(2,1)}, bf16[224,1280]{1,0:T(8,128)(2,1)}, u32[]{:S(2)}, u32[]{:S(2)}) collective-permute-start(bf16[224,1280]{1,0:T(8,128)(2,1)} %get-tuple-element.25), channel_id=1, source_target_pairs={{0,96},{32,0},{64,32},{96,64},{1,97},{33,1},{65,33},{97,65},{2,98}... | collective-permute-start | bytes 1720328 | tf_op jit(solution)/shard_map/ppermute | solution.py:286
  115.8 1.9 %collective-permute-start.10 = (bf16[224,1280]{1,0:T(8,128)(2,1)}, bf16[224,1280]{1,0:T(8,128)(2,1)}, u32[]{:S(2)}, u32[]{:S(2)}) collective-permute-start(bf16[224,1280]{1,0:T(8,128)(2,1)} %get-tuple-element.31), channel_id=1, source_target_pairs={{0,32},{32,64},{64,96},{96,0},{1,33},{33,65},{65,97},{97,1},{2,34}... | collective-permute-start | bytes 1720328 | tf_op jit(solution)/shard_map/ppermute | solution.py:286
  117.8 0.0 collective-permute-done.7
  117.8 0.0 collective-permute-done.8
  117.8 1.2 add_convert_fusion
  119.0 4.6 %collective-permute-start.11 = (bf16[224,1280]{1,0:T(8,128)(2,1)S(1)}, bf16[224,1280]{1,0:T(8,128)(2,1)S(1)}, u32[]{:S(2)}, u32[]{:S(2)}) collective-permute-start(bf16[224,1280]{1,0:T(8,128)(2,1)S(1)} %add_convert_fusion), channel_id=1, source_target_pairs={{0,96},{32,0},{64,32},{96,64},{1,97},{33,1},{65,33},{97,65},{2,98}... | collective-permute-start | bytes 1720328 | tf_op jit(solution)/shard_map/ppermute | solution.py:286
  123.6 0.0 copy-done.3
  123.6 0.1 add_convert_fusion.1
  123.7 1.9 %collective-permute-start.9 = (bf16[224,1280]{1,0:T(8,128)(2,1)S(1)}, bf16[224,1280]{1,0:T(8,128)(2,1)S(1)}, u32[]{:S(2)}, u32[]{:S(2)}) collective-permute-start(bf16[224,1280]{1,0:T(8,128)(2,1)S(1)} %add_convert_fusion.1), channel_id=1, source_target_pairs={{0,32},{32,64},{64,96},{96,0},{1,33},{33,65},{65,97},{97,1},{2,34}... | collective-permute-start | bytes 1720328 | tf_op jit(solution)/shard_map/ppermute | solution.py:286
  125.6 2.6 %all-to-all-done.2.arrived = bf16[8,48,1280]{2,1,0:T(8,128)(2,1)S(1)} async-done(((bf16[8,48,1280]{2,1,0:T(8,128)(2,1)}), bf16[8,48,1280]{2,1,0:T(8,128)(2,1)S(1)}, u32[]{:S(2)}, u32[]{:S(2)}) %all-to-all-start.2) | async-done | bytes 983072 | tf_op jit(solution)/shard_map/all_to_all | solution.py:294
  128.3 1.0 shard_map.141
  129.3 5.3 %all-to-all-start.3 = ((bf16[16,30,256]{2,1,0:T(8,128)(2,1)}), bf16[16,30,256]{2,1,0:T(8,128)(2,1)S(1)}, u32[]{:S(2)}, u32[]{:S(2)}) async-start(bf16[16,30,256]{2,1,0:T(8,128)(2,1)} %shard_map.141), calls=%async_computation.3 | async-start | bytes 524288 | tf_op jit(solution)/shard_map/all_to_all | solution.py:290
  135.3 0.0 collective-permute-done.10.args_4_
  135.3 4.6 %collective-permute-done.11.args_5_ = bf16[224,1280]{1,0:T(8,128)(2,1)S(1)} collective-permute-done((bf16[224,1280]{1,0:T(8,128)(2,1)S(1)}, bf16[224,1280]{1,0:T(8,128)(2,1)S(1)}, u32[]{:S(2)}, u32[]{:S(2)}) %collective-permute-start.11) | collective-permute-done | bytes 573472 | tf_op jit(solution)/shard_map/ppermute | solution.py:286
  139.9 0.0 copy-start.7
  139.9 0.8 copy-done.7
  140.7 3.7 %shard_map.145 = bf16[224,1280]{1,0:T(8,128)(2,1)} custom-call(f32[1]{0:T(128)S(6)} %pow.3.factor, bf16[224,1280]{1,0:T(8,128)(2,1)} %bitcast.28, bf16[224,1280]{1,0:T(8,128)(2,1)} %bitcast.29, bf16[224,1280]{1,0:T(8,128)(2,1)} %bitcast.25, bf16[224,1280]{1,0:T(8,128)(2,1)} %get-tuple-element.30.args_3_, bf16[224,1280]{1,0:T(8,128)(2,1)} %collective-permute-done.10.args_4_, ...), custom_call_target="tpu_custom_call" | custom-call | bytes 4014084 | tf_op jit(solution)/shard_map/pallas_call | solution.py:58
  144.4 0.0 collective-permute-done.6.args_4_
  144.4 0.0 collective-permute-done.9.args_5_
  144.4 0.0 copy-start.6
  144.4 0.8 copy-done.6
  145.3 0.0 copy-start
  145.3 0.0 copy-start.1
  145.3 0.0 copy-start.2
  145.3 3.8 %shard_map.144 = bf16[224,1280]{1,0:T(8,128)(2,1)} custom-call(f32[1]{0:T(128)S(6)} %pow.3.factor, bf16[224,1280]{1,0:T(8,128)(2,1)} %bitcast.34, bf16[224,1280]{1,0:T(8,128)(2,1)} %bitcast.35, bf16[224,1280]{1,0:T(8,128)(2,1)} %bitcast.31, bf16[224,1280]{1,0:T(8,128)(2,1)} %get-tuple-element.24.args_3_, bf16[224,1280]{1,0:T(8,128)(2,1)} %collective-permute-done.6.args_4_, ...), custom_call_target="tpu_custom_call" | custom-call | bytes 4014084 | tf_op jit(solution)/shard_map/pallas_call | solution.py:58
  149.0 0.0 all-to-all-done.3.returned
  149.0 0.0 copy-done
  149.1 0.0 copy-done.1
  149.1 0.0 copy-done.2
  149.1 1.2 shard_map.142
  (1 shorter events, 0.0 us)
Async XLA Ops:
  32.1 8.5 %copy-start.5 = (bf16[1,1280,224]{1,2,0:T(8,128)(2,1)S(1)}, bf16[1,1280,224]{1,2,0:T(8,128)(2,1)}, u32[]{:S(2)}) copy-start(bf16[1,1280,224]{1,2,0:T(8,128)(2,1)} %param.15) | copy-start | bytes 1720324
  32.1 11.7 %copy-start.4 = (bf16[1,224,1280]{2,1,0:T(8,128)(2,1)S(1)}, bf16[1,224,1280]{2,1,0:T(8,128)(2,1)}, u32[]{:S(2)}) copy-start(bf16[1,224,1280]{2,1,0:T(8,128)(2,1)} %param.16) | copy-start | bytes 1720324
  32.1 54.3 %all-to-all-start.1 = ((bf16[8,96,1280]{2,1,0:T(8,128)(2,1)}), bf16[8,96,1280]{2,1,0:T(8,128)(2,1)}, u32[]{:S(2)}, u32[]{:S(2)}) async-start(bf16[8,96,1280]{2,1,0:T(8,128)(2,1)} %shard_map.139), calls=%async_computation.1 | async-start | bytes 3932160 | tf_op jit(solution)/shard_map/all_to_all | solution.py:294
  40.7 18.2 %collective-permute-start = (bf16[224,1280]{1,0:T(8,128)(2,1)S(1)}, bf16[224,1280]{1,0:T(8,128)(2,1)S(1)}, u32[]{:S(2)}, u32[]{:S(2)}) collective-permute-start(bf16[224,1280]{1,0:T(8,128)(2,1)S(1)} %bitcast.32), channel_id=1, source_target_pairs={{0,32},{32,64},{64,96},{96,0},{1,33},{33,65},{65,97},{97,1},{2,34}... | collective-permute-start | bytes 1720328 | tf_op jit(solution)/shard_map/ppermute | solution.py:286
  43.8 17.0 %collective-permute-start.3 = (bf16[224,1280]{1,0:T(8,128)(2,1)S(1)}, bf16[224,1280]{1,0:T(8,128)(2,1)S(1)}, u32[]{:S(2)}, u32[]{:S(2)}) collective-permute-start(bf16[224,1280]{1,0:T(8,128)(2,1)S(1)} %bitcast.26), channel_id=1, source_target_pairs={{0,96},{32,0},{64,32},{96,64},{1,97},{33,1},{65,33},{97,65},{2,98}... | collective-permute-start | bytes 1720328 | tf_op jit(solution)/shard_map/ppermute | solution.py:286
  47.2 25.9 %collective-permute-start.2 = (bf16[224,1280]{1,0:T(8,128)(2,1)S(1)}, bf16[224,1280]{1,0:T(8,128)(2,1)S(1)}, u32[]{:S(2)}, u32[]{:S(2)}) collective-permute-start(bf16[224,1280]{1,0:T(8,128)(2,1)S(1)} %bitcast.33), channel_id=1, source_target_pairs={{0,96},{32,0},{64,32},{96,64},{1,97},{33,1},{65,33},{97,65},{2,98}... | collective-permute-start | bytes 1720328 | tf_op jit(solution)/shard_map/ppermute | solution.py:286
  50.4 22.7 %collective-permute-start.5 = (bf16[224,1280]{1,0:T(8,128)(2,1)S(1)}, bf16[224,1280]{1,0:T(8,128)(2,1)S(1)}, u32[]{:S(2)}, u32[]{:S(2)}) collective-permute-start(bf16[224,1280]{1,0:T(8,128)(2,1)S(1)} %bitcast.27), channel_id=1, source_target_pairs={{0,32},{32,64},{64,96},{96,0},{1,33},{33,65},{65,97},{97,1},{2,34}... | collective-permute-start | bytes 1720328 | tf_op jit(solution)/shard_map/ppermute | solution.py:286
  58.9 24.2 %copy-start.10 = (bf16[224,1280]{1,0:T(8,128)(2,1)}, bf16[224,1280]{1,0:T(8,128)(2,1)S(1)}, u32[]{:S(2)}) copy-start(bf16[224,1280]{1,0:T(8,128)(2,1)S(1)} %collective-permute-done.args_1_) | copy-start | bytes 1720324
  58.9 24.2 %collective-permute-start.1 = (bf16[224,1280]{1,0:T(8,128)(2,1)S(1)}, bf16[224,1280]{1,0:T(8,128)(2,1)S(1)}, u32[]{:S(2)}, u32[]{:S(2)}) collective-permute-start(bf16[224,1280]{1,0:T(8,128)(2,1)S(1)} %collective-permute-done.args_1_), channel_id=1, source_target_pairs={{0,32},{32,64},{64,96},{96,0},{1,33},{33,65},{65,97},{97,1},{2,34}... | collective-permute-start | bytes 1720328 | tf_op jit(solution)/shard_map/ppermute | solution.py:286
  60.8 24.5 %copy-start.8 = (bf16[224,1280]{1,0:T(8,128)(2,1)}, bf16[224,1280]{1,0:T(8,128)(2,1)S(1)}, u32[]{:S(2)}) copy-start(bf16[224,1280]{1,0:T(8,128)(2,1)S(1)} %collective-permute-done.3.args_6_.args_1_) | copy-start | bytes 1720324
  60.8 24.5 %collective-permute-start.4 = (bf16[224,1280]{1,0:T(8,128)(2,1)S(1)}, bf16[224,1280]{1,0:T(8,128)(2,1)}, u32[]{:S(2)}, u32[]{:S(2)}) collective-permute-start(bf16[224,1280]{1,0:T(8,128)(2,1)S(1)} %collective-permute-done.3.args_6_.args_1_), channel_id=1, source_target_pairs={{0,96},{32,0},{64,32},{96,64},{1,97},{33,1},{65,33},{97,65},{2,98}... | collective-permute-start | bytes 1720328 | tf_op jit(solution)/shard_map/ppermute | solution.py:286
  73.1 10.0 %copy-start.11 = (bf16[224,1280]{1,0:T(8,128)(2,1)}, bf16[224,1280]{1,0:T(8,128)(2,1)S(1)}, u32[]{:S(2)}) copy-start(bf16[224,1280]{1,0:T(8,128)(2,1)S(1)} %collective-permute-done.2.args_2_) | copy-start | bytes 1720324
  73.1 12.2 %copy-start.9 = (bf16[224,1280]{1,0:T(8,128)(2,1)}, bf16[224,1280]{1,0:T(8,128)(2,1)S(1)}, u32[]{:S(2)}) copy-start(bf16[224,1280]{1,0:T(8,128)(2,1)S(1)} %collective-permute-done.5.args_5_.args_0_) | copy-start | bytes 1720324
  93.9 23.9 %collective-permute-start.7 = (bf16[224,1280]{1,0:T(8,128)(2,1)S(1)}, bf16[224,1280]{1,0:T(8,128)(2,1)S(1)}, u32[]{:S(2)}, u32[]{:S(2)}) collective-permute-start(bf16[224,1280]{1,0:T(8,128)(2,1)S(1)} %get-tuple-element.27), channel_id=1, source_target_pairs={{0,32},{32,64},{64,96},{96,0},{1,33},{33,65},{65,97},{97,1},{2,34}... | collective-permute-start | bytes 1720328 | tf_op jit(solution)/shard_map/ppermute | solution.py:286
  97.0 20.8 %collective-permute-start.8 = (bf16[224,1280]{1,0:T(8,128)(2,1)S(1)}, bf16[224,1280]{1,0:T(8,128)(2,1)S(1)}, u32[]{:S(2)}, u32[]{:S(2)}) collective-permute-start(bf16[224,1280]{1,0:T(8,128)(2,1)S(1)} %get-tuple-element.28), channel_id=1, source_target_pairs={{0,96},{32,0},{64,32},{96,64},{1,97},{33,1},{65,33},{97,65},{2,98}... | collective-permute-start | bytes 1720328 | tf_op jit(solution)/shard_map/ppermute | solution.py:286
  100.4 27.9 %all-to-all-start.2 = ((bf16[8,48,1280]{2,1,0:T(8,128)(2,1)}), bf16[8,48,1280]{2,1,0:T(8,128)(2,1)S(1)}, u32[]{:S(2)}, u32[]{:S(2)}) async-start(bf16[8,48,1280]{2,1,0:T(8,128)(2,1)} %get-tuple-element.19), calls=%async_computation.2 | async-start | bytes 1966080 | tf_op jit(solution)/shard_map/all_to_all | solution.py:294
  112.3 11.2 %copy-start.3 = (bf16[224,1280]{1,0:T(8,128)(2,1)S(1)}, bf16[224,1280]{1,0:T(8,128)(2,1)}, u32[]{:S(2)}) copy-start(bf16[224,1280]{1,0:T(8,128)(2,1)} %get-tuple-element.26) | copy-start | bytes 1720324
  112.3 32.1 %collective-permute-start.6 = (bf16[224,1280]{1,0:T(8,128)(2,1)}, bf16[224,1280]{1,0:T(8,128)(2,1)}, u32[]{:S(2)}, u32[]{:S(2)}) collective-permute-start(bf16[224,1280]{1,0:T(8,128)(2,1)} %get-tuple-element.25), channel_id=1, source_target_pairs={{0,96},{32,0},{64,32},{96,64},{1,97},{33,1},{65,33},{97,65},{2,98}... | collective-permute-start | bytes 1720328 | tf_op jit(solution)/shard_map/ppermute | solution.py:286
  115.8 19.4 %collective-permute-start.10 = (bf16[224,1280]{1,0:T(8,128)(2,1)}, bf16[224,1280]{1,0:T(8,128)(2,1)}, u32[]{:S(2)}, u32[]{:S(2)}) collective-permute-start(bf16[224,1280]{1,0:T(8,128)(2,1)} %get-tuple-element.31), channel_id=1, source_target_pairs={{0,32},{32,64},{64,96},{96,0},{1,33},{33,65},{65,97},{97,1},{2,34}... | collective-permute-start | bytes 1720328 | tf_op jit(solution)/shard_map/ppermute | solution.py:286
  119.0 20.9 %collective-permute-start.11 = (bf16[224,1280]{1,0:T(8,128)(2,1)S(1)}, bf16[224,1280]{1,0:T(8,128)(2,1)S(1)}, u32[]{:S(2)}, u32[]{:S(2)}) collective-permute-start(bf16[224,1280]{1,0:T(8,128)(2,1)S(1)} %add_convert_fusion), channel_id=1, source_target_pairs={{0,96},{32,0},{64,32},{96,64},{1,97},{33,1},{65,33},{97,65},{2,98}... | collective-permute-start | bytes 1720328 | tf_op jit(solution)/shard_map/ppermute | solution.py:286
  123.7 20.7 %collective-permute-start.9 = (bf16[224,1280]{1,0:T(8,128)(2,1)S(1)}, bf16[224,1280]{1,0:T(8,128)(2,1)S(1)}, u32[]{:S(2)}, u32[]{:S(2)}) collective-permute-start(bf16[224,1280]{1,0:T(8,128)(2,1)S(1)} %add_convert_fusion.1), channel_id=1, source_target_pairs={{0,32},{32,64},{64,96},{96,0},{1,33},{33,65},{65,97},{97,1},{2,34}... | collective-permute-start | bytes 1720328 | tf_op jit(solution)/shard_map/ppermute | solution.py:286
  129.3 19.8 %all-to-all-start.3 = ((bf16[16,30,256]{2,1,0:T(8,128)(2,1)}), bf16[16,30,256]{2,1,0:T(8,128)(2,1)S(1)}, u32[]{:S(2)}, u32[]{:S(2)}) async-start(bf16[16,30,256]{2,1,0:T(8,128)(2,1)} %shard_map.141), calls=%async_computation.3 | async-start | bytes 524288 | tf_op jit(solution)/shard_map/all_to_all | solution.py:290
  139.9 0.8 copy-start.7
  144.4 0.8 copy-start.6
  145.3 3.8 %copy-start = (bf16[48,1280]{1,0:T(8,128)(2,1)S(1)}, bf16[48,1280]{1,0:T(8,128)(2,1)}, u32[]{:S(2)}) copy-start(bf16[48,1280]{1,0:T(8,128)(2,1)} %cotangent.3) | copy-start | bytes 368644
  145.3 3.8 %copy-start.1 = (s32[1,32,3]{1,0,2:T(1,128)S(1)}, s32[1,32,3]{1,0,2:T(1,128)}, u32[]{:S(2)}) copy-start(s32[1,32,3]{1,0,2:T(1,128)} %param.13) | copy-start | bytes 1156
  145.3 3.8 %copy-start.2 = (f32[1,32,3]{1,0,2:T(1,128)S(1)}, f32[1,32,3]{1,0,2:T(1,128)}, u32[]{:S(2)}) copy-start(f32[1,32,3]{1,0,2:T(1,128)} %param.14) | copy-start | bytes 1156
